TPU v7x, 128 devices: a whole 4x4x4 slice. The times are simulated.
128 devices in a mesh: compute: 8 (over z_lo, x), memory: 8 (over y, core), pair: 2 (over z_hi).
Axes of the slice: x: 4, y: 4, z: 4 (z_hi: 2, z_lo: 2; z = z_hi * 2 + z_lo), core: 2. Of those that a mesh axis runs over, the one named last changes fastest.
Arguments:
- hidden: bfloat16 [2048, 8192], P('memory', 'pair'), may hold values from -80 to 80
- norm_gain: bfloat16 [8192], P('pair'), may hold values from 0.25 to 1.75
- w_query: bfloat16 [8192, 8192], P('pair', 'compute'), may hold values from -0.0625 to 0.0625
- w_key: bfloat16 [8192, 1024], P('pair', 'compute'), may hold values from -0.0625 to 0.0625
- w_value: bfloat16 [8192, 1024], P('pair', 'compute'), may hold values from -0.0625 to 0.0625
- query_bias: bfloat16 [8192], P('compute'), may hold values from -4 to 4
- key_bias: bfloat16 [1024], P('compute'), may hold values from -4 to 4
- value_bias: bfloat16 [1024], P('compute'), may hold values from -4 to 4
- prefix_keys: bfloat16 [8, 8192, 1024], P('memory', 'pair', 'compute'), may hold values from -240 to 240
- prefix_values: bfloat16 [8, 8192, 1024], P('memory', 'pair', 'compute'), may hold values from -12 to 12
- reply_keys: bfloat16 [8, 384, 128, 1024], P('memory', 'pair', None, 'compute'), may hold values from -9 to 9
- reply_values: bfloat16 [8, 384, 128, 1024], P('memory', 'pair', None, 'compute'), may hold values from -12 to 12
- reply_length: int32 [2048], P(('memory', 'pair')), may hold values from 1 to 128
- prefix_ids: int32 [2048], P(('memory', 'pair')), may hold values from 0 to 7, as said below
- prompt_home: int32 [8], replicated, may hold values from 0 to 7, as said below
Outputs:
- attention: bfloat16 [2048, 8192], P(('memory', 'pair'), 'compute')
- stored_rows: bfloat16 [2, 8, 384, 1024], P(None, 'memory', None, 'compute')
Inputs may be any that keep to these rules, and one draw needn't show every extreme that they name: `prefix_ids`: among the 128 rollouts of each aligned block (the rollouts of one device, blocks in the order of memory then pair), at most 24 have a prompt whose prompt_home // 1 is the same memory index; in every draw one memory index gets exactly 24 from every block. `prompt_home`: A permutation of the prompts.
All inputs are finite; a program needn't handle non-finite values.
Results may differ from a plain program's by a relative error of at most 0.012.
The roundings to bfloat16 on the way count: a program that leaves them out, or rounds other values in their place, can miss the bound.
Values may be sent and summed in bfloat16 or wider, within the bound.
No kernel may reach another device: no remote copies, remote signals or barrier semaphores. Data moves between devices by JAX's collectives and lax.ppermute only.
A program may use at most 192 MiB of HBM per device.

v0:
```python
from functools import partial

import jax
import jax.numpy as jnp
from jax import lax
from jax.sharding import PartitionSpec as P

D = 8192
HD = 128
PREFIX = 8192


EPSILON = 1e-06
ROPE_BASE = 1000000.0
MASKED = -1e30


def rotate(vectors, position):
    half_dim = vectors.shape[-1] // 2
    ladder = jnp.arange(half_dim, dtype=jnp.float32) * (2.0 / vectors.shape[-1])
    frequency = jnp.power(ROPE_BASE, -ladder)
    angles = position.astype(jnp.float32)[:, None, None] * frequency
    cosine = jnp.cos(angles)
    sine_part = jnp.sin(angles)
    first_half = vectors[..., :half_dim]
    second_half = vectors[..., half_dim:]
    return jnp.concatenate(
        [
            first_half * cosine - second_half * sine_part,
            second_half * cosine + first_half * sine_part,
        ],
        axis=-1,
    )


def shared_product(prompt_values, weights):
    return jnp.einsum("skgt,tkd->skgd", weights, prompt_values, preferred_element_type=jnp.float32)


def own_product(value_rows, weights):
    return jnp.einsum("skgt,stkd->skgd", weights, value_rows, preferred_element_type=jnp.float32)


def absorb(carried, scores, visible, product):
    running_max, weight_sum, combined = carried
    scores = jnp.where(visible, scores, MASKED)
    new_max = jnp.maximum(running_max, jnp.max(scores, axis=-1))
    weights = jnp.where(visible, jnp.exp(scores - new_max[..., None]), 0.0)
    shrink = jnp.exp(running_max - new_max)
    weight_sum = weight_sum * shrink + jnp.sum(weights, axis=-1)
    combined = combined * shrink[..., None] + product(weights.astype(jnp.bfloat16))
    return (new_max, weight_sum, combined)


def combine(partials, log_sums):
    highest = jnp.max(log_sums, axis=1, keepdims=True)
    scales = jnp.exp(log_sums - highest)
    return jnp.sum(partials * scales[..., None], axis=1) / jnp.sum(scales, axis=1)[..., None]


def duplicate(packed, holders, pair_count, capacity):
    grouped = packed.reshape((holders, 1, capacity) + packed.shape[1:])
    spread = jnp.broadcast_to(grouped, (holders, pair_count, capacity) + packed.shape[1:])
    return spread.reshape((holders * pair_count, capacity) + packed.shape[1:])


def body(
    hidden,
    norm_gain,
    w_query,
    w_key,
    w_value,
    query_bias,
    key_bias,
    value_bias,
    prefix_keys,
    prefix_values,
    reply_keys,
    reply_values,
    reply_length,
    prefix_ids,
    prompt_home,
):
    holders = lax.axis_size("memory")
    pair_count = lax.axis_size("pair")
    span_index = lax.axis_index("pair")
    own_rows = hidden.shape[0] // pair_count
    capacity = 3 * own_rows // (2 * holders)
    slot_count = holders * pair_count * capacity
    query_width = w_query.shape[1]
    kv_width = w_key.shape[1]
    kv_heads = kv_width // HD
    head_count = query_width // HD
    group_size = head_count // kv_heads
    widened = hidden.astype(jnp.float32)
    row_totals = lax.psum(jnp.sum(widened * widened, axis=1), "pair")
    inverse_rms = lax.rsqrt(row_totals / D + EPSILON)
    normed = (widened * inverse_rms[:, None] * norm_gain.astype(jnp.float32)[None, :]).astype(
        jnp.bfloat16
    )
    projected = lax.psum_scatter(
        jnp.concatenate(
            [
                jnp.dot(normed, w_query, preferred_element_type=jnp.float32),
                jnp.dot(normed, w_key, preferred_element_type=jnp.float32),
                jnp.dot(normed, w_value, preferred_element_type=jnp.float32),
            ],
            axis=1,
        ),
        "pair",
        scatter_dimension=0,
        tiled=True,
    )
    position = PREFIX + reply_length
    query_part = projected[:, :query_width] + query_bias.astype(jnp.float32)
    key_part = projected[:, query_width : query_width + kv_width] + key_bias.astype(jnp.float32)
    value_part = projected[:, query_width + kv_width :] + value_bias.astype(jnp.float32)
    queries = (
        rotate(query_part.reshape(own_rows, head_count, HD), position)
        .reshape(own_rows, query_width)
        .astype(jnp.bfloat16)
    )
    fresh_keys = (
        rotate(key_part.reshape(own_rows, kv_heads, HD), position)
        .reshape(own_rows, kv_width)
        .astype(jnp.bfloat16)
    )
    fresh = jnp.concatenate([fresh_keys, value_part.astype(jnp.bfloat16)], axis=1)
    prompt_total = prompt_home.shape[0]
    prompt_hold = prompt_total // holders
    matches = prefix_ids[:, None] == jnp.arange(prompt_total, dtype=jnp.int32)[None, :]
    places = jnp.sum(jnp.where(matches, prompt_home[None, :], 0), axis=1)
    owners = places // prompt_hold
    local_prompt = places % prompt_hold
    owner_table = (owners[:, None] == jnp.arange(holders, dtype=jnp.int32)[None, :]).astype(
        jnp.int32
    )
    earlier = jnp.cumsum(owner_table, axis=0) - owner_table
    target = owners * capacity + jnp.sum(earlier * owner_table, axis=1)

    def place_rows(values_in):
        empty_rows = jnp.zeros((holders * capacity,) + values_in.shape[1:], values_in.dtype)
        return empty_rows.at[target].set(values_in)

    send_query = place_rows(queries)
    send_fresh = place_rows(fresh)
    send_length = place_rows(reply_length)
    send_prompt = place_rows(local_prompt)
    arrived = (
        lax.all_to_all(
            duplicate(send_query, holders, pair_count, capacity),
            ("memory", "pair"),
            split_axis=0,
            concat_axis=0,
            tiled=True,
        ),
        lax.all_to_all(
            duplicate(send_fresh, holders, pair_count, capacity),
            ("memory", "pair"),
            split_axis=0,
            concat_axis=0,
            tiled=True,
        ),
        lax.all_to_all(
            duplicate(send_length, holders, pair_count, capacity),
            ("memory", "pair"),
            split_axis=0,
            concat_axis=0,
            tiled=True,
        ),
        lax.all_to_all(
            duplicate(send_prompt, holders, pair_count, capacity),
            ("memory", "pair"),
            split_axis=0,
            concat_axis=0,
            tiled=True,
        ),
    )
    arrived_query = arrived[0].reshape(slot_count, kv_heads, group_size, HD)
    arrived_fresh = arrived[1].reshape(slot_count, 2 * kv_width)
    arrived_length = arrived[2].reshape(slot_count)
    arrived_prompt = arrived[3].reshape(slot_count)
    scale = HD ** (-0.5)
    carried = (
        jnp.full((slot_count, kv_heads, group_size), MASKED, jnp.float32),
        jnp.zeros((slot_count, kv_heads, group_size), jnp.float32),
        jnp.zeros((slot_count, kv_heads, group_size, HD), jnp.float32),
    )
    prompt_keys = prefix_keys[0].reshape(-1, kv_heads, HD)
    prompt_values = prefix_values[0].reshape(-1, kv_heads, HD)
    scores = (
        jnp.einsum("skgd,tkd->skgt", arrived_query, prompt_keys, preferred_element_type=jnp.float32)
        * scale
    )
    visible = (arrived_prompt == 0)[:, None, None, None]
    carried = absorb(carried, scores, visible, partial(shared_product, prompt_values))
    local_slots = slot_count // pair_count
    slot_start = span_index * local_slots
    reply_key_rows = reply_keys.reshape(local_slots, -1, kv_heads, HD)
    reply_value_rows = reply_values.reshape(local_slots, -1, kv_heads, HD)
    reply_span = reply_key_rows.shape[1]
    local_query = lax.dynamic_slice_in_dim(arrived_query, slot_start, local_slots, 0)
    local_length = lax.dynamic_slice_in_dim(arrived_length, slot_start, local_slots, 0)
    local_carry = tuple(
        (lax.dynamic_slice_in_dim(member, slot_start, local_slots, 0) for member in carried)
    )
    scores = (
        jnp.einsum(
            "skgd,stkd->skgt", local_query, reply_key_rows, preferred_element_type=jnp.float32
        )
        * scale
    )
    positions = jnp.arange(reply_span, dtype=jnp.int32)
    visible = (positions[None, :] < local_length[:, None])[:, None, None, :]
    local_carry = absorb(local_carry, scores, visible, partial(own_product, reply_value_rows))
    carried = tuple(
        (
            lax.dynamic_update_slice_in_dim(member, piece, slot_start, 0)
            for member, piece in zip(carried, local_carry)
        )
    )
    new_key_rows = arrived_fresh[:, :kv_width].reshape(slot_count, 1, kv_heads, HD)
    new_value_rows = arrived_fresh[:, kv_width:].reshape(slot_count, 1, kv_heads, HD)
    scores = (
        jnp.einsum(
            "skgd,stkd->skgt", arrived_query, new_key_rows, preferred_element_type=jnp.float32
        )
        * scale
    )
    visible = jnp.broadcast_to(span_index == pair_count - 1, scores.shape)
    carried = absorb(carried, scores, visible, partial(own_product, new_value_rows))
    running_max, weight_sum, combined = carried
    partial_out = (combined / weight_sum[..., None]).reshape(slot_count, query_width)
    log_sums = (running_max + jnp.log(weight_sum)).reshape(slot_count, head_count)
    returned = (
        lax.all_to_all(
            partial_out.reshape(holders * pair_count, capacity, query_width),
            ("memory", "pair"),
            split_axis=0,
            concat_axis=0,
            tiled=True,
        ),
        lax.all_to_all(
            log_sums.reshape(holders * pair_count, capacity, head_count),
            ("memory", "pair"),
            split_axis=0,
            concat_axis=0,
            tiled=True,
        ),
    )
    merged = combine(
        returned[0].reshape(holders, pair_count, capacity, head_count, HD),
        returned[1].reshape(holders, pair_count, capacity, head_count),
    )
    merged = merged.astype(jnp.bfloat16).reshape(holders * capacity, query_width)
    attention = jnp.take(merged, target, axis=0)
    stored_rows = jnp.stack([arrived_fresh[:, :kv_width], arrived_fresh[:, kv_width:]])[:, None]
    return (attention, stored_rows)


def solution(mesh):
    in_specs = (
        P("memory", "pair"),
        P("pair"),
        P("pair", "compute"),
        P("pair", "compute"),
        P("pair", "compute"),
        P("compute"),
        P("compute"),
        P("compute"),
        P("memory", "pair", "compute"),
        P("memory", "pair", "compute"),
        P("memory", "pair", None, "compute"),
        P("memory", "pair", None, "compute"),
        P(("memory", "pair")),
        P(("memory", "pair")),
        P(),
    )
    out_specs = (P(("memory", "pair"), "compute"), P(None, "memory", None, "compute"))
    return jax.shard_map(body, mesh=mesh, in_specs=in_specs, out_specs=out_specs, check_vma=False)
```

profile of v0, /device:TPU:1, one launch (start us, length us, event | category | flops | bytes accessed | tf_op | source)
XLA Modules:
  0.0 231.6 jit_solution(6401653423568961642)
XLA Ops:
  7.2 2.2 fusion.13
  9.5 6.7 %psum.7 = f32[256]{0:T(256)S(1)} all-reduce(f32[256]{0:T(256)S(1)} %fusion.13), channel_id=1, replica_groups=mesh['compute'=8,'memory'=8,'pair'=2] {'pair'}, use_global_device_ids=true, to_apply=%region_5.6 | all-reduce | flops 256 | bytes 2048 | tf_op jit(solution)/shard_map/psum | solution.py:96
  16.9 3.0 %fusion.76 = f32[256,128]{0,1:T(8,128)S(1)} fusion(bf16[4096,128]{1,0:T(8,128)(2,1)} %param.18, bf16[256,4096]{1,0:T(8,128)(2,1)} %param.15, f32[4096]{0:T(1024)S(1)} %convert_element_type.56, f32[256]{0:T(256)S(1)} %add_rsqrt_fusion), kind=kOutput, calls=%fused_computation.131 | convolution fusion | flops 272629760 | bytes 3294208 | tf_op jit(solution)/shard_map/dot_general | solution.py:105
  19.9 2.5 %fusion.74 = f32[256,128]{0,1:T(8,128)S(1)} fusion(bf16[4096,128]{1,0:T(8,128)(2,1)} %param.19, bf16[256,4096]{1,0:T(8,128)(2,1)S(1)} %copy-done.2, f32[4096]{0:T(1024)S(1)} %convert_element_type.56, f32[256]{0:T(256)S(1)} %add_rsqrt_fusion), kind=kOutput, calls=%fused_computation.130 | convolution fusion | flops 272629760 | bytes 3294208 | tf_op jit(solution)/shard_map/dot_general | solution.py:106
  22.5 3.6 %fusion.78 = f32[256,1024]{0,1:T(8,128)S(1)} fusion(bf16[4096,1024]{1,0:T(8,128)(2,1)S(1)} %copy-done.4, bf16[256,4096]{1,0:T(8,128)(2,1)S(1)} %copy-done.2, f32[4096]{0:T(1024)S(1)} %convert_element_type.56, f32[256]{0:T(256)S(1)} %add_rsqrt_fusion), kind=kOutput, calls=%fused_computation.132 | convolution fusion | flops 2151677952 | bytes 11551744 | tf_op jit(solution)/shard_map/dot_general | solution.py:104
  29.7 9.0 %all-to-all-start.2 = ((s32[16,1,24]{2,1,0:T(1,128)}), s32[16,1,24]{2,1,0:T(1,128)S(1)}, u32[]{:S(2)}, u32[]{:S(2)}) async-start(s32[16,1,24]{2,1,0:T(1,128)} %bitcast.19), calls=%async_computation.3 | async-start | bytes 16384 | tf_op jit(solution)/shard_map/all_to_all | solution.py:164
  40.1 17.9 %reduce-scatter.2.cloned.1.call-done = f32[128,1280]{0,1:T(8,128)} async-done(((f32[256,1280]{0,1:T(8,128)}), f32[128,1280]{0,1:T(8,128)}) %reduce-scatter.2.cloned.1.call-update) | async-done | bytes 655376 | tf_op jit(solution)/shard_map/reduce_scatter | solution.py:101
  61.0 5.0 %all-to-all-start = ((s32[16,1,24]{2,1,0:T(1,128)}), s32[16,1,24]{2,1,0:T(1,128)S(1)}, u32[]{:S(2)}, u32[]{:S(2)}) async-start(s32[16,1,24]{2,1,0:T(1,128)} %bitcast.2), calls=%async_computation | async-start | bytes 16384 | tf_op jit(solution)/shard_map/all_to_all | solution.py:171
  67.1 5.7 %all-to-all-done = s32[16,1,24]{2,1,0:T(1,128)S(1)} async-done(((s32[16,1,24]{2,1,0:T(1,128)}), s32[16,1,24]{2,1,0:T(1,128)S(1)}, u32[]{:S(2)}, u32[]{:S(2)}) %all-to-all-start) | async-done | bytes 1568 | tf_op jit(solution)/shard_map/all_to_all | solution.py:171
  73.5 4.0 %all-to-all-start.3 = ((bf16[16,24,256]{2,1,0:T(8,128)(2,1)}), bf16[16,24,256]{2,1,0:T(8,128)(2,1)S(1)}, u32[]{:S(2)}, u32[]{:S(2)}) async-start(bf16[16,24,256]{2,1,0:T(8,128)(2,1)} %bitcast.32), calls=%async_computation.4 | async-start | bytes 393216 | tf_op jit(solution)/shard_map/all_to_all | solution.py:157
  77.8 1.3 scatter_custom_fusion.1
  79.1 7.2 %all-to-all-done.3 = bf16[16,24,256]{2,1,0:T(8,128)(2,1)S(1)} async-done(((bf16[16,24,256]{2,1,0:T(8,128)(2,1)}), bf16[16,24,256]{2,1,0:T(8,128)(2,1)S(1)}, u32[]{:S(2)}, u32[]{:S(2)}) %all-to-all-start.3) | async-done | bytes 196640 | tf_op jit(solution)/shard_map/all_to_all | solution.py:157
  87.3 3.8 %all-to-all-start.1 = ((bf16[16,24,1024]{2,1,0:T(8,128)(2,1)}), bf16[16,24,1024]{2,1,0:T(8,128)(2,1)S(1)}, u32[]{:S(2)}, u32[]{:S(2)}) async-start(bf16[16,24,1024]{2,1,0:T(8,128)(2,1)} %bitcast.6), calls=%async_computation.2 | async-start | bytes 1572864 | tf_op jit(solution)/shard_map/all_to_all | solution.py:150
  92.7 14.5 %all-to-all-done.1 = bf16[16,24,1024]{2,1,0:T(8,128)(2,1)S(1)} async-done(((bf16[16,24,1024]{2,1,0:T(8,128)(2,1)}), bf16[16,24,1024]{2,1,0:T(8,128)(2,1)S(1)}, u32[]{:S(2)}, u32[]{:S(2)}) %all-to-all-start.1) | async-done | bytes 786464 | tf_op jit(solution)/shard_map/all_to_all | solution.py:150
  108.1 5.5 %fusion.82 = (f32[192,8]{1,0:T(8,128)S(1)}, f32[192,8,128]{2,1,0:T(8,128)S(1)}) fusion(bf16[1,192,128,128]{3,2,1,0:T(8,128)(2,1)} %param.25, bf16[384,1,8,128]{3,2,0,1:T(8,128)(2,1)S(1)} %bitcast.244, s32[]{:T(128)S(6)} %select_n.84, pred[192,128]{1,0:T(8,128)(4,1)S(1)} %iota_compare_fusion), kind=kOutput, calls=%fused_computation.134 | convolution fusion | flops 50919936 | bytes 7501828 | tf_op jit(solution)/shard_map/skgd,stkd->skgt/dot_general | solution.py:208
  113.7 18.8 %fusion.1 = (f32[384,8]{0,1:T(8,128)S(1)}, f32[384,8,4096]{2,0,1:T(8,128)}) fusion(pred[384]{0:T(512)(128)(4,1)S(1)} %eq.52, bf16[1,4096,128]{2,1,0:T(8,128)(2,1)S(1)} %copy-done, bf16[384,8,128]{2,1,0:T(8,128)(2,1)S(1)} %bitcast.245), kind=kOutput, calls=%fused_computation.8 | convolution fusion | flops 3258971136 | bytes 52179328 | tf_op jit(solution)/shard_map/skgd,tkd->skgt/dot_general | solution.py:192
  132.6 22.0 %fusion.2 = f32[384,8]{0,1:T(8,128)S(1)} fusion(f32[384,8,4096]{2,0,1:T(8,128)} %get-tuple-element.25, f32[384,8]{0,1:T(8,128)S(1)} %get-tuple-element.21, pred[384]{0:T(512)(128)(4,1)S(1)} %eq.52), kind=kLoop, calls=%fused_computation.9 | loop fusion | flops 62911488 | bytes 50356608 | tf_op jit(solution)/shard_map/reduce_sum | solution.py:50
  155.6 3.9 %fusion.9 = f32[192,8,128]{2,1,0:T(8,128)S(1)} fusion(bf16[1,192,128,128]{3,2,1,0:T(8,128)(2,1)} %param.26, f32[192,8,128]{2,1,0:T(8,128)S(1)} %get-tuple-element.27, f32[192,8]{1,0:T(8,128)S(1)} %copy.88, pred[192,128]{1,0:T(8,128)(4,1)S(1)} %iota_compare_fusion), kind=kOutput, calls=%fused_computation.15 | convolution fusion | flops 50921472 | bytes 7895040 | tf_op jit(solution)/shard_map/skgt,stkd->skgd/dot_general | solution.py:41
  160.8 3.6 %all-to-all-start.5 = ((f32[16,1,192]{2,1,0:T(1,128)}), f32[16,1,192]{2,1,0:T(1,128)S(1)}, u32[]{:S(2)}, u32[]{:S(2)}) async-start(f32[16,1,192]{2,1,0:T(1,128)} %reshape.453), calls=%async_computation.6 | async-start | bytes 32768 | tf_op jit(solution)/shard_map/all_to_all | solution.py:243
  164.4 19.3 %bitcast_add_fusion = f32[1,128,384,8]{1,2,3,0:T(8,128)S(1)} fusion(f32[384,8,4096]{2,0,1:T(8,128)} %get-tuple-element.25, f32[384,8]{0,1:T(8,128)S(1)} %get-tuple-element.21, pred[384]{0:T(512)(128)(4,1)S(1)} %eq.52, bf16[1,4096,128]{2,1,0:T(8,128)(2,1)} %param.24, f32[384,8]{0,1:T(8,128)S(1)} %get-tuple-element.20), kind=kOutput, calls=%fused_computation.24 | convolution fusion | flops 3284533248 | bytes 52978048 | tf_op jit(solution)/shard_map/skgt,tkd->skgd/dot_general | solution.py:37
  184.1 1.5 fusion.16
  186.6 1.4 reshape_reshape.6
  187.9 7.1 %all-to-all-start.4 = ((f32[16,24,1024]{2,1,0:T(8,128)}), f32[16,24,1024]{2,1,0:T(8,128)S(1)}, u32[]{:S(2)}, u32[]{:S(2)}) async-start(f32[16,24,1024]{2,1,0:T(8,128)} %reshape_reshape.6), calls=%async_computation.5 | async-start | bytes 3145728 | tf_op jit(solution)/shard_map/all_to_all | solution.py:236
  197.3 24.6 %all-to-all-done.4 = f32[16,24,1024]{2,1,0:T(8,128)S(1)} async-done(((f32[16,24,1024]{2,1,0:T(8,128)}), f32[16,24,1024]{2,1,0:T(8,128)S(1)}, u32[]{:S(2)}, u32[]{:S(2)}) %all-to-all-start.4) | async-done | bytes 1572896 | tf_op jit(solution)/shard_map/all_to_all | solution.py:236
  (102 shorter events, 22.7 us)
Async XLA Ops:
  7.2 106.5 %copy-start = (bf16[1,4096,128]{2,1,0:T(8,128)(2,1)S(1)}, bf16[1,4096,128]{2,1,0:T(8,128)(2,1)}, u32[]{:S(2)}) copy-start(bf16[1,4096,128]{2,1,0:T(8,128)(2,1)} %param.23) | copy-start | bytes 3145732
  7.2 12.7 %copy-start.2 = (bf16[256,4096]{1,0:T(8,128)(2,1)S(1)}, bf16[256,4096]{1,0:T(8,128)(2,1)}, u32[]{:S(2)}) copy-start(bf16[256,4096]{1,0:T(8,128)(2,1)} %param.15) | copy-start | bytes 6291460
  7.2 50.7 %reduce-scatter.2.cloned.1.call-start = ((), (), s32[]{:S(2)}) async-start(), calls=%async_computation.7 | async-start | bytes 1966080 | tf_op jit(solution)/shard_map/reduce_scatter | solution.py:101
  16.9 5.5 %copy-start.4 = (bf16[4096,1024]{1,0:T(8,128)(2,1)S(1)}, bf16[4096,1024]{1,0:T(8,128)(2,1)}, u32[]{:S(2)}) copy-start(bf16[4096,1024]{1,0:T(8,128)(2,1)} %param.17) | copy-start | bytes 25165828
  22.4 4.9 %copy-start.5 = (s32[8]{0:T(128)S(1)}, s32[8]{0:T(128)}, u32[]{:S(2)}) copy-start(s32[8]{0:T(128)} %param.29) | copy-start | bytes 100
  22.5 4.9 %copy-start.6 = (s32[128]{0:T(128)S(1)}, s32[128]{0:T(128)}, u32[]{:S(2)}) copy-start(s32[128]{0:T(128)} %param.28) | copy-start | bytes 1540
  26.1 1.9 copy-start.9
  26.1 12.6 %copy-start.7 = (bf16[128]{0:T(256)(128)(2,1)S(1)}, bf16[128]{0:T(256)(128)(2,1)}, u32[]{:S(2)}) copy-start(bf16[128]{0:T(256)(128)(2,1)} %param.21) | copy-start | bytes 772
  26.1 12.6 %copy-start.8 = (bf16[128]{0:T(256)(128)(2,1)S(1)}, bf16[128]{0:T(256)(128)(2,1)}, u32[]{:S(2)}) copy-start(bf16[128]{0:T(256)(128)(2,1)} %param.22) | copy-start | bytes 772
  26.2 12.6 %copy-start.3 = (bf16[1024]{0:T(1024)(128)(2,1)S(1)}, bf16[1024]{0:T(1024)(128)(2,1)}, u32[]{:S(2)}) copy-start(bf16[1024]{0:T(1024)(128)(2,1)} %param.20) | copy-start | bytes 6148
  29.7 30.7 %all-to-all-start.2 = ((s32[16,1,24]{2,1,0:T(1,128)}), s32[16,1,24]{2,1,0:T(1,128)S(1)}, u32[]{:S(2)}, u32[]{:S(2)}) async-start(s32[16,1,24]{2,1,0:T(1,128)} %bitcast.19), calls=%async_computation.3 | async-start | bytes 16384 | tf_op jit(solution)/shard_map/all_to_all | solution.py:164
  61.0 11.9 %all-to-all-start = ((s32[16,1,24]{2,1,0:T(1,128)}), s32[16,1,24]{2,1,0:T(1,128)S(1)}, u32[]{:S(2)}, u32[]{:S(2)}) async-start(s32[16,1,24]{2,1,0:T(1,128)} %bitcast.2), calls=%async_computation | async-start | bytes 16384 | tf_op jit(solution)/shard_map/all_to_all | solution.py:171
  73.5 12.8 %all-to-all-start.3 = ((bf16[16,24,256]{2,1,0:T(8,128)(2,1)}), bf16[16,24,256]{2,1,0:T(8,128)(2,1)S(1)}, u32[]{:S(2)}, u32[]{:S(2)}) async-start(bf16[16,24,256]{2,1,0:T(8,128)(2,1)} %bitcast.32), calls=%async_computation.4 | async-start | bytes 393216 | tf_op jit(solution)/shard_map/all_to_all | solution.py:157
  87.3 20.0 %all-to-all-start.1 = ((bf16[16,24,1024]{2,1,0:T(8,128)(2,1)}), bf16[16,24,1024]{2,1,0:T(8,128)(2,1)S(1)}, u32[]{:S(2)}, u32[]{:S(2)}) async-start(bf16[16,24,1024]{2,1,0:T(8,128)(2,1)} %bitcast.6), calls=%async_computation.2 | async-start | bytes 1572864 | tf_op jit(solution)/shard_map/all_to_all | solution.py:150
  160.8 27.2 %all-to-all-start.5 = ((f32[16,1,192]{2,1,0:T(1,128)}), f32[16,1,192]{2,1,0:T(1,128)S(1)}, u32[]{:S(2)}, u32[]{:S(2)}) async-start(f32[16,1,192]{2,1,0:T(1,128)} %reshape.453), calls=%async_computation.6 | async-start | bytes 32768 | tf_op jit(solution)/shard_map/all_to_all | solution.py:243
  187.9 33.9 %all-to-all-start.4 = ((f32[16,24,1024]{2,1,0:T(8,128)}), f32[16,24,1024]{2,1,0:T(8,128)S(1)}, u32[]{:S(2)}, u32[]{:S(2)}) async-start(f32[16,24,1024]{2,1,0:T(8,128)} %reshape_reshape.6), calls=%async_computation.5 | async-start | bytes 3145728 | tf_op jit(solution)/shard_map/all_to_all | solution.py:236
  221.9 2.9 %copy-start.1 = (bf16[1,4096,128]{2,1,0:T(8,128)(2,1)S(1)}, bf16[1,4096,128]{2,1,0:T(8,128)(2,1)}, u32[]{:S(2)}) copy-start(bf16[1,4096,128]{2,1,0:T(8,128)(2,1)} %param.23) | copy-start | bytes 3145732
Sparse Core Ops, SparseCore 0:
  27.5 30.4 reduce-scatter.1
where the time goes:
time: 233 us; the launch traced here: 232 us
  waiting for transfers between devices  69.9 us (30%)
  matrix products  57.2 us (25%)
  other arithmetic  35.9 us (15%)
  starting transfers between devices  32.5 us (14%)
  local copies, waits for them, and re-layouts  14.7 us (6%)
  between operations  14.6 us (6%)
  blocking collectives  6.73 us (3%)
    all_to_all x1, waiting for transfers between devices, body(): lax.all_to_all(partial_out.reshape(holders * pair_count, capacity, query_...  24.6 us
    reduce_sum x2, other arithmetic, absorb(): weight_sum = weight_sum * shrink + jnp.sum(weights, axis=-1)  22.6 us
    dot_general x1, matrix products, shared_product(): jnp.einsum('skgt,tkd->skgd', weights, prompt_values, preferred_element_ty...  19.3 us
    dot_general x1, matrix products, body(): jnp.einsum('skgd,tkd->skgt', arrived_query, prompt_keys, preferred_elemen...  18.8 us
    reduce_scatter x1, waiting for transfers between devices, body(): lax.psum_scatter(jnp.concatenate([jnp.dot(normed, w_query, preferred_elem...  17.9 us
    all_to_all x1, waiting for transfers between devices, body(): lax.all_to_all(duplicate(send_query, holders, pair_count, capacity), ('me...  14.5 us
    all_to_all x1, starting transfers between devices, body(): lax.all_to_all(duplicate(send_length, holders, pair_count, capacity), ('m...  9.02 us
    all_to_all x1, waiting for transfers between devices, body(): lax.all_to_all(duplicate(send_fresh, holders, pair_count, capacity), ('me...  7.24 us
  transfers between devices with their start and end apart: 7, of which 5 were waited for; matrix products, arithmetic and copies ran while one was open for 16% of the time, Pallas kernels for 0%

commit v1 on v0

v1 whole, which is shorter than its diff:
```python
from functools import partial

import jax
import jax.numpy as jnp
from jax import lax
from jax.experimental import pallas as pl
from jax.experimental.pallas import tpu as pltpu
from jax.sharding import PartitionSpec as P

D = 8192
HD = 128
PREFIX = 8192
EPSILON = 1e-06
ROPE_BASE = 1000000.0
MASKED = -1e30
ROWS = 128
HOLDERS = 8
CAP = 24
HEADS = 8
QW = HEADS * HD
SLOTS = HOLDERS * CAP
LENGTH_AT = QW
KEY_AT = QW + HD
VALUE_AT = QW + 2 * HD
ROW_WIDTH = QW + 3 * HD
SCALE = 1.4426950408889634 / HD**0.5
F32 = jnp.float32
BF16 = jnp.bfloat16
VMEM_LIMIT = 56 * 1024 * 1024


def params(**more):
    return pltpu.CompilerParams(vmem_limit_bytes=VMEM_LIMIT, **more)


def lane_ids(shape):
    return lax.broadcasted_iota(jnp.int32, shape, len(shape) - 1)


def to_column(row):
    size = row.shape[1]
    spread = jnp.broadcast_to(row, (size, size))
    diagonal = lax.broadcasted_iota(jnp.int32, (size, size), 0) == lane_ids((size, size))
    return jnp.sum(jnp.where(diagonal, spread, jnp.zeros_like(spread)), axis=1, keepdims=True)


def project_kernel(
    span_ref, inverse_ref, hidden_ref, gain_ref, wq_ref, wk_ref, wv_ref, keep_ref, send_ref, scale_ref
):
    span = span_ref[0]
    step = pl.program_id(0)

    @pl.when(step == 0)
    def _():
        first = to_column(inverse_ref[0:1, :])
        second = to_column(inverse_ref[1:2, :])
        scale_ref[0:ROWS, :] = jnp.broadcast_to(jnp.where(span == 0, first, second), (ROWS, HD))
        scale_ref[ROWS:, :] = jnp.broadcast_to(jnp.where(span == 0, second, first), (ROWS, HD))
        keep_ref[...] = jnp.zeros_like(keep_ref)
        send_ref[...] = jnp.zeros_like(send_ref)

    own_start = pl.multiple_of(span * ROWS, ROWS)
    other_start = pl.multiple_of((1 - span) * ROWS, ROWS)
    gain = gain_ref[...].astype(F32)
    for start, where, out_ref in ((other_start, ROWS, send_ref), (own_start, 0, keep_ref)):
        rows = hidden_ref[pl.ds(start, ROWS), :].astype(F32)
        normed = (rows * scale_ref[where : where + ROWS, 0:1] * gain).astype(BF16)
        for at, w_ref in ((0, wq_ref), (QW, wk_ref), (QW + HD, wv_ref)):
            width = w_ref.shape[1]
            out_ref[:, at : at + width] += jnp.dot(normed, w_ref[...], preferred_element_type=F32)


def project(span, inverse, hidden, gain, w_query, w_key, w_value):
    depth = hidden.shape[1]
    part = 1024
    width = QW + 2 * HD
    out = jax.ShapeDtypeStruct((ROWS, width), F32)
    whole = pl.BlockSpec((ROWS, width), lambda k: (0, 0))
    return pl.pallas_call(
        project_kernel,
        grid=(depth // part,),
        in_specs=[
            pl.BlockSpec(memory_space=pltpu.SMEM),
            pl.BlockSpec((2, ROWS), lambda k: (0, 0)),
            pl.BlockSpec((2 * ROWS, part), lambda k: (0, k)),
            pl.BlockSpec((1, part), lambda k: (0, k)),
            pl.BlockSpec((part, QW), lambda k: (k, 0)),
            pl.BlockSpec((part, HD), lambda k: (k, 0)),
            pl.BlockSpec((part, HD), lambda k: (k, 0)),
        ],
        out_specs=[whole, whole],
        out_shape=[out, out],
        scratch_shapes=[pltpu.VMEM((2 * ROWS, HD), F32)],
        compiler_params=params(),
        cost_estimate=pl.CostEstimate(
            flops=2 * 2 * ROWS * depth * width, bytes_accessed=14 * 2**20, transcendentals=0
        ),
    )(span, inverse, hidden, gain, w_query, w_key, w_value)


def spread_kernel(
    home_ref,
    me_ref,
    keep_ref,
    came_ref,
    bias_ref,
    cos_ref,
    sin_ref,
    length_ref,
    ids_ref,
    out0_ref,
    out1_ref,
    out2_ref,
    out3_ref,
    target_ref,
):
    ids = ids_ref[...]
    owner = jnp.zeros_like(ids)
    for prompt in range(HOLDERS):
        owner = jnp.where(ids == prompt, home_ref[prompt], owner)
    owner_column = to_column(owner.astype(F32))
    square = (ROWS, ROWS)
    earlier = lax.broadcasted_iota(jnp.int32, square, 0) < lane_ids(square)
    same = jnp.broadcast_to(owner_column, square) == jnp.broadcast_to(owner.astype(F32), square)
    rank = jnp.sum(jnp.where(earlier & same, 1.0, 0.0), axis=0, keepdims=True).astype(jnp.int32)
    target = (owner ^ me_ref[0]) * CAP + rank
    target_ref[...] = target
    placing = jnp.where(
        lax.broadcasted_iota(jnp.int32, (SLOTS, ROWS), 0) == jnp.broadcast_to(target, (SLOTS, ROWS)),
        1.0,
        0.0,
    ).astype(BF16)
    cosine = cos_ref[...]
    sine = sin_ref[...]
    outs = (out0_ref, out1_ref, out2_ref, out3_ref)
    for head in range(HEADS + 3):
        at = head * HD
        if head == HEADS:
            rows = length_ref[...]
        else:
            source = at if head < HEADS else at - HD
            part = slice(source, source + HD)
            total = keep_ref[:, part] + came_ref[:, part] + bias_ref[:, part]
            if head < HEADS + 2:
                half = HD // 2
                swapped = jnp.concatenate([total[:, half:], total[:, :half]], axis=1)
                total = total * cosine + swapped * sine
            rows = total.astype(BF16)
        placed = jnp.dot(placing, rows, preferred_element_type=F32).astype(BF16)
        placed = placed.astype(F32).reshape(HOLDERS, CAP, HD)
        for index, out_ref in enumerate(outs):
            out_ref[:, :, at : at + HD] = placed[2 * index : 2 * index + 2].astype(BF16)


def spread(home, me, keep, came, bias, cosine, sine, lengths, ids):
    block = jax.ShapeDtypeStruct((2, CAP, ROW_WIDTH), BF16)
    smem = pl.BlockSpec(memory_space=pltpu.SMEM)
    vmem = pl.BlockSpec(memory_space=pltpu.VMEM)
    return pl.pallas_call(
        spread_kernel,
        in_specs=[smem, smem] + [vmem] * 7,
        out_specs=[vmem] * 5,
        out_shape=[block] * 4 + [jax.ShapeDtypeStruct((1, ROWS), jnp.int32)],
        compiler_params=params(),
        cost_estimate=pl.CostEstimate(
            flops=2 * SLOTS * ROWS * ROW_WIDTH, bytes_accessed=2 * 2**20, transcendentals=0
        ),
    )(home, me, keep, came, bias, cosine, sine, lengths, ids)


NT = (((1,), (1,)), ((), ()))


def reply_kernel(where_ref, parity_ref, rows_ref, keys_ref, values_ref, out_ref, log_ref, wide_ref):
    wide_ref[...] = rows_ref[0, :, 0:KEY_AT].astype(F32)
    group = 8
    lanes = lane_ids((group, HD))
    lines = lax.broadcasted_iota(jnp.int32, (group, HD), 0)
    for part in range(CAP // group):
        slots = slice(part * group, (part + 1) * group)
        visible = lanes.astype(F32) < wide_ref[slots, LENGTH_AT : LENGTH_AT + HD]
        stacked = jnp.concatenate(
            [wide_ref[slots, head * HD : (head + 1) * HD] for head in range(HEADS)], axis=0
        ).astype(BF16)
        keys = keys_ref[0, slots].reshape(group * HD, HD)
        values = values_ref[0, slots].reshape(group * HD, HD)
        scores = lax.dot_general(stacked, keys, NT, preferred_element_type=F32)
        weights = []
        sums = []
        logs = jnp.zeros((group, HD), F32)
        for head in range(HEADS):
            mine = slice(head * group, (head + 1) * group)
            own = scores[mine, 0:HD]
            for slot in range(1, group):
                own = jnp.where(lines == slot, scores[mine, slot * HD : (slot + 1) * HD], own)
            own = jnp.where(visible, own, MASKED)
            highest = jnp.max(own, axis=1, keepdims=True)
            weight = jnp.exp2((own - highest) * SCALE)
            total = jnp.sum(weight, axis=1, keepdims=True)
            sums.append(total)
            logs = jnp.where(lanes == head, highest * SCALE + jnp.log2(total), logs)
            weights.append(
                jnp.concatenate(
                    [jnp.where(lines == slot, weight, 0.0) for slot in range(group)], axis=1
                )
            )
        mixed = jnp.dot(
            jnp.concatenate(weights, axis=0).astype(BF16), values, preferred_element_type=F32
        )
        for head in range(HEADS):
            out_ref[0, slots, head * HD : (head + 1) * HD] = (
                mixed[head * group : (head + 1) * group] / sums[head]
            )
        log_ref[0, slots, :] = logs


def reply(where, parity, rows, keys, values):
    quarter = 4
    cached = pl.BlockSpec((1, CAP, HD, HD), lambda b, w, q: (2 * b + q[0], 0, 0, 0))
    return pl.pallas_call(
        reply_kernel,
        grid_spec=pltpu.PrefetchScalarGridSpec(
            num_scalar_prefetch=2,
            grid=(quarter,),
            in_specs=[
                pl.BlockSpec((1, CAP, rows.shape[2]), lambda b, w, q: (w[b], 0, 0)),
                cached,
                cached,
            ],
            out_specs=[
                pl.BlockSpec((1, CAP, QW), lambda b, w, q: (b, 0, 0)),
                pl.BlockSpec((1, CAP, HD), lambda b, w, q: (b, 0, 0)),
            ],
            scratch_shapes=[pltpu.VMEM((CAP, KEY_AT), F32)],
        ),
        out_shape=[
            jax.ShapeDtypeStruct((quarter, CAP, QW), F32),
            jax.ShapeDtypeStruct((quarter, CAP, HD), F32),
        ],
        compiler_params=params(),
        cost_estimate=pl.CostEstimate(
            flops=2 * 10**9, bytes_accessed=8 * 2**20, transcendentals=10**6
        ),
    )(where, parity, rows, keys, values)


def merge_in(out_ref, log_ref, at, other_out, other_log):
    held = log_ref[at]
    highest = jnp.maximum(held, other_log)
    mine = jnp.exp2(held - highest)
    theirs = jnp.exp2(other_log - highest)
    total = mine + theirs
    log_ref[at] = highest + jnp.log2(total)
    mine = mine / total
    theirs = theirs / total
    for head in range(HEADS):
        part = slice(head * HD, (head + 1) * HD)
        out_ref[at, :, part] = (
            out_ref[at, :, part] * mine[:, head : head + 1]
            + other_out(part) * theirs[:, head : head + 1]
        )


def prefix_kernel(
    own,
    where_ref,
    rows_ref,
    keys_ref,
    values_ref,
    reply_ref,
    reply_log_ref,
    *refs,
):
    if own:
        out_ref, log_ref, query_ref, score_ref = refs
    else:
        sent_ref, query_ref, score_ref, out_ref, log_ref = refs
    span = 512
    tokens = keys_ref.shape[0]
    units = 2
    unit_heads = HEADS // units
    unit_rows = unit_heads * SLOTS
    for head in range(HEADS):
        rows = rows_ref[:, :, head * HD : (head + 1) * HD].astype(F32)
        query_ref[head * SLOTS : (head + 1) * SLOTS, :] = rows.reshape(SLOTS, HD).astype(BF16)
    block_lanes = lane_ids((HOLDERS, CAP, HD))
    logs = jnp.zeros((HOLDERS, CAP, HD), F32)
    for unit in range(units):
        queries = query_ref.at[unit * unit_rows : (unit + 1) * unit_rows]

        def score(step, highest):
            start = pl.multiple_of(step * span, span)
            scores = lax.dot_general(
                queries[...], keys_ref[pl.ds(start, span), :], NT, preferred_element_type=F32
            )
            score_ref[step] = scores
            for piece in range(span // HD):
                highest = jnp.maximum(highest, scores[:, piece * HD : (piece + 1) * HD])
            return highest

        highest = lax.fori_loop(
            0, tokens // span, score, jnp.full((unit_rows, HD), MASKED, F32)
        )
        highest = jnp.max(highest, axis=1, keepdims=True)

        def mix(step, carried):
            total, mixed = carried
            start = pl.multiple_of(step * span, span)
            weights = jnp.exp2((score_ref[step] - highest) * SCALE)
            for piece in range(span // HD):
                total = total + weights[:, piece * HD : (piece + 1) * HD]
            mixed = mixed + jnp.dot(
                weights.astype(BF16), values_ref[pl.ds(start, span), :], preferred_element_type=F32
            )
            return total, mixed

        empty = jnp.zeros((unit_rows, HD), F32)
        total, mixed = lax.fori_loop(0, tokens // span, mix, (empty, empty))
        total = jnp.sum(total, axis=1, keepdims=True)
        mixed = mixed / total
        log = jnp.broadcast_to(highest * SCALE + jnp.log2(total), (unit_rows, HD))
        for index in range(unit_heads):
            head = unit * unit_heads + index
            mine = slice(index * SLOTS, (index + 1) * SLOTS)
            out_ref[:, :, head * HD : (head + 1) * HD] = mixed[mine].reshape(HOLDERS, CAP, HD)
            logs = jnp.where(block_lanes == head, log[mine].reshape(HOLDERS, CAP, HD), logs)
    log_ref[...] = logs
    for index in range(reply_ref.shape[0]):
        merge_in(
            out_ref,
            log_ref,
            where_ref[index],
            lambda part: reply_ref[index, :, part],
            reply_log_ref[index],
        )
    if own:
        lanes = lane_ids((CAP, HD))
        for block in range(HOLDERS):
            key = rows_ref[block, :, KEY_AT : KEY_AT + HD].astype(F32)
            value = rows_ref[block, :, VALUE_AT : VALUE_AT + HD].astype(F32)
            logs = jnp.zeros((CAP, HD), F32)
            for head in range(HEADS):
                query = rows_ref[block, :, head * HD : (head + 1) * HD].astype(F32)
                score = jnp.sum(query * key, axis=1, keepdims=True) * SCALE
                logs = jnp.where(lanes == head, score, logs)
            merge_in(out_ref, log_ref, block, lambda part: value, logs)
    else:
        log = log_ref[...]
        high = log.astype(BF16).astype(F32)
        middle = (log - high).astype(BF16).astype(F32)
        low = log - high - middle
        packed = jnp.where(block_lanes < HEADS, high, 0.0)
        for index, piece in ((1, middle), (2, low)):
            moved = jnp.concatenate([piece[:, :, HD - 8 * index :], piece[:, :, : HD - 8 * index]], axis=2)
            here = (block_lanes >= 8 * index) & (block_lanes < 8 * index + 8)
            packed = jnp.where(here, moved, packed)
        sent_ref[:, :, 0:QW] = out_ref[...].astype(BF16)
        sent_ref[:, :, QW:] = packed.astype(BF16)


def prefix(own, where, rows, keys, values, reply_out, reply_log):
    smem = pl.BlockSpec(memory_space=pltpu.SMEM)
    vmem = pl.BlockSpec(memory_space=pltpu.VMEM)
    out = (HOLDERS, CAP, QW)
    log = (HOLDERS, CAP, HD)
    scratch = [
        pltpu.VMEM((HEADS * SLOTS, HD), BF16),
        pltpu.VMEM((keys.shape[0] // 512, HEADS * SLOTS // 2, 512), F32),
    ]
    if own:
        out_shape = [jax.ShapeDtypeStruct(out, F32), jax.ShapeDtypeStruct(log, F32)]
    else:
        out_shape = [jax.ShapeDtypeStruct((HOLDERS, CAP, QW + HD), BF16)]
        scratch += [pltpu.VMEM(out, F32), pltpu.VMEM(log, F32)]
    work = HEADS * SLOTS * keys.shape[0]
    return pl.pallas_call(
        partial(prefix_kernel, own),
        in_specs=[smem] + [vmem] * 5,
        out_specs=[vmem] * len(out_shape),
        out_shape=out_shape,
        scratch_shapes=scratch,
        compiler_params=params(),
        cost_estimate=pl.CostEstimate(
            flops=4 * work * HD, bytes_accessed=4 * 2**20, transcendentals=work
        ),
    )(where, rows, keys, values, reply_out, reply_log)


def combine_kernel(out_ref, log_ref, came_ref, out0_ref, out1_ref, out2_ref, out3_ref):
    for block in range(HOLDERS):
        packed = came_ref[block, :, QW:].astype(F32)
        came_log = packed
        for index in (1, 2):
            came_log = came_log + jnp.concatenate(
                [packed[:, 8 * index :], packed[:, : 8 * index]], axis=1
            )
        held = log_ref[block]
        highest = jnp.maximum(held, came_log)
        mine = jnp.exp2(held - highest)
        theirs = jnp.exp2(came_log - highest)
        total = mine + theirs
        mine = mine / total
        theirs = theirs / total
        target = (out0_ref, out1_ref, out2_ref, out3_ref)[block // 2]
        for head in range(HEADS):
            part = slice(head * HD, (head + 1) * HD)
            target[block % 2, :, part] = (
                out_ref[block, :, part] * mine[:, head : head + 1]
                + came_ref[block, :, part].astype(F32) * theirs[:, head : head + 1]
            ).astype(BF16)


def combine(out, log, came):
    vmem = pl.BlockSpec(memory_space=pltpu.VMEM)
    return pl.pallas_call(
        combine_kernel,
        in_specs=[vmem] * 3,
        out_specs=[vmem] * 4,
        out_shape=[jax.ShapeDtypeStruct((2, CAP, QW), BF16)] * 4,
        compiler_params=params(),
        cost_estimate=pl.CostEstimate(flops=10**6, bytes_accessed=2 * 2**20, transcendentals=10**5),
    )(out, log, came)


def unplace_kernel(target_ref, near0_ref, near1_ref, near2_ref, near3_ref, far_ref, out_ref, rows_ref):
    for index, near in enumerate((near0_ref, near1_ref, near2_ref, near3_ref)):
        rows_ref[2 * index] = near[0].astype(F32)
        rows_ref[2 * index + 1] = far_ref[index].astype(F32)
    rows = rows_ref[...].reshape(SLOTS, QW).astype(BF16)
    target = target_ref[...]
    placing = jnp.where(
        lax.broadcasted_iota(jnp.int32, (SLOTS, ROWS), 0) == jnp.broadcast_to(target, (SLOTS, ROWS)),
        1.0,
        0.0,
    ).astype(BF16)
    out_ref[...] = lax.dot_general(
        placing, rows, (((0,), (0,)), ((), ())), preferred_element_type=F32
    ).astype(BF16)


def unplace(target, nears, far):
    vmem = pl.BlockSpec(memory_space=pltpu.VMEM)
    return pl.pallas_call(
        unplace_kernel,
        in_specs=[vmem] * 6,
        out_specs=vmem,
        out_shape=jax.ShapeDtypeStruct((ROWS, QW), BF16),
        scratch_shapes=[pltpu.VMEM((HOLDERS, CAP, QW), F32)],
        compiler_params=params(),
        cost_estimate=pl.CostEstimate(
            flops=2 * SLOTS * ROWS * QW, bytes_accessed=2**20, transcendentals=0
        ),
    )(target, *nears, far)


def store_kernel(me_ref, span_ref, own_ref, other_ref, out_ref):
    for block in range(HOLDERS):
        origin = me_ref[0] ^ block
        for rows_ref, parity in ((own_ref, span_ref[0]), (other_ref, 1 - span_ref[0])):
            for kind in range(2):
                out_ref[kind, 2 * origin + parity] = rows_ref[block, :, kind * HD : (kind + 1) * HD]


def store(me, span, own, other):
    smem = pl.BlockSpec(memory_space=pltpu.SMEM)
    vmem = pl.BlockSpec(memory_space=pltpu.VMEM)
    return pl.pallas_call(
        store_kernel,
        in_specs=[smem, smem, vmem, vmem],
        out_specs=vmem,
        out_shape=jax.ShapeDtypeStruct((2, 2 * HOLDERS, CAP, HD), BF16),
        compiler_params=params(),
        cost_estimate=pl.CostEstimate(flops=0, bytes_accessed=2**19, transcendentals=0),
    )(me, span, own, other)


def other_pair(values):
    return lax.ppermute(values, "pair", [(0, 1), (1, 0)])


def flip(values, bits):
    return lax.ppermute(values, "memory", [(m, m ^ bits) for m in range(HOLDERS)])


def body(
    hidden,
    norm_gain,
    w_query,
    w_key,
    w_value,
    query_bias,
    key_bias,
    value_bias,
    prefix_keys,
    prefix_values,
    reply_keys,
    reply_values,
    reply_length,
    prefix_ids,
    prompt_home,
):
    me = lax.axis_index("memory").astype(jnp.int32).reshape(1)
    span = lax.axis_index("pair").astype(jnp.int32).reshape(1)

    widened = hidden.astype(F32)
    squares = jnp.sum(widened * widened, axis=1)
    squares = squares + other_pair(squares)
    inverse = lax.rsqrt(squares / D + EPSILON).reshape(2, ROWS)
    keep, send = project(
        span, inverse, hidden, norm_gain.reshape(1, -1), w_query, w_key, w_value
    )
    came = other_pair(send)

    half = HD // 2
    ladder = jnp.arange(half, dtype=F32) * (2.0 / HD)
    frequency = jnp.power(ROPE_BASE, -ladder)
    angles = (PREFIX + reply_length).astype(F32)[:, None] * frequency
    cosine = jnp.cos(angles)
    sine = jnp.sin(angles)
    cosine = jnp.concatenate([cosine, cosine], axis=1)
    sine = jnp.concatenate([-sine, sine], axis=1)
    lengths = jnp.broadcast_to(reply_length.astype(BF16)[:, None], (ROWS, HD))
    bias = jnp.concatenate([query_bias, key_bias, value_bias]).astype(F32).reshape(1, -1)
    *blocks, target = spread(
        prompt_home, me, keep, came, bias, cosine, sine, lengths, prefix_ids.reshape(1, ROWS)
    )

    near = [blocks[0]] + [flip(blocks[step], 2 * step) for step in range(1, 4)]
    far = flip(jnp.stack([block[1] for block in near]), 1)
    rows = jnp.stack([piece for step in range(4) for piece in (near[step][0], far[step])])
    partner_rows = other_pair(rows[:, :, :KEY_AT])
    fresh = rows[:, :, KEY_AT:]
    partner_fresh = other_pair(fresh)

    origin = 4 * span[0] + jnp.arange(4, dtype=jnp.int32)
    where = me[0] ^ origin
    caches = (8, CAP, HD, HD)
    keys = reply_keys.reshape(caches)
    values = reply_values.reshape(caches)
    prompt_keys = prefix_keys[0]
    prompt_values = prefix_values[0]
    own_reply = reply(where, span, rows, keys, values)
    out, log = prefix(True, where, rows, prompt_keys, prompt_values, *own_reply)
    partner_reply = reply(where, 1 - span, partner_rows, keys, values)
    (sent,) = prefix(False, where, partner_rows, prompt_keys, prompt_values, *partner_reply)
    came = other_pair(sent)
    merged = combine(out, log, came)

    nears = [merged[0]] + [flip(merged[step], 2 * step) for step in range(1, 4)]
    fars = flip(jnp.stack([block[1] for block in nears]), 1)
    attention = unplace(target, nears, fars)
    stored = store(me, span, fresh, partner_fresh).reshape(2, 1, 2 * SLOTS, HD)
    return attention, stored


def solution(mesh):
    in_specs = (
        P("memory", "pair"),
        P("pair"),
        P("pair", "compute"),
        P("pair", "compute"),
        P("pair", "compute"),
        P("compute"),
        P("compute"),
        P("compute"),
        P("memory", "pair", "compute"),
        P("memory", "pair", "compute"),
        P("memory", "pair", None, "compute"),
        P("memory", "pair", None, "compute"),
        P(("memory", "pair")),
        P(("memory", "pair")),
        P(),
    )
    out_specs = (P(("memory", "pair"), "compute"), P(None, "memory", None, "compute"))
    return jax.shard_map(body, mesh=mesh, in_specs=in_specs, out_specs=out_specs, check_vma=False)
```

time: 233 us -> 148 us (0.64)
  Pallas kernels: 0 us -> 70.5 us
  matrix products: 57.2 us -> 0 us
  other arithmetic: 35.9 us -> 5.74 us
  waiting for transfers between devices: 69.9 us -> 39.9 us
  between operations: 14.6 us -> 0.77 us
  starting transfers between devices: 32.5 us -> 21.8 us
  blocking collectives: 6.73 us -> 0 us
  local copies, waits for them, and re-layouts: 14.7 us -> 8.53 us
    pallas_call x0 -> x9, Pallas kernels: none -> 70.5 us  [the longest x2 37.6 us: prefix(): pl.pallas_call(partial(prefix_kernel, own), in_specs=[smem] + [vmem] * 5,...]
    dot_general x8 -> x0, matrix products: 57.2 us -> none  [the longest x1 19.3 us: shared_product(): jnp.einsum('skgt,tkd->skgd', weights, prompt_values, preferred_element_ty...]
    all_to_all x6 -> x0, waiting for transfers between devices: 52.1 us -> none  [the longest x1 24.6 us: body(): lax.all_to_all(partial_out.reshape(holders * pair_count, capacity, query_...]
    ppermute x0 -> x13, waiting for transfers between devices: none -> 39.9 us  [the longest x5 29.2 us: other_pair(): return lax.ppermute(values, 'pair', [(0, 1), (1, 0)])]
    all_to_all x6 -> x0, starting transfers between devices: 32.5 us -> none  [the longest x1 9.02 us: body(): lax.all_to_all(duplicate(send_length, holders, pair_count, capacity), ('m...]
    reduce_sum x7 -> x1, other arithmetic: 25.7 us -> 2.09 us  [body(): squares = jnp.sum(widened * widened, axis=1)]
    ppermute x0 -> x13, starting transfers between devices: none -> 21.8 us  [the longest x8 12 us: flip(): lax.ppermute(values, 'memory', [(m, m ^ bits) for m in range(HOLDERS)])]
    reduce_scatter x1 -> x0, waiting for transfers between devices: 17.9 us -> none  [body(): lax.psum_scatter(jnp.concatenate([jnp.dot(normed, w_query, preferred_elem...]
  transfers between devices with their start and end apart: 7 -> 13, of which waited for: 5 -> 8; matrix products, arithmetic and copies ran while one was open for 16% -> 5% of each run, Pallas kernels for 0% -> 20%
where the time goes in v1:
time: 148 us; the launch traced here: 147 us
  Pallas kernels  70.5 us (48%)
  waiting for transfers between devices  39.9 us (27%)
  starting transfers between devices  21.8 us (15%)
  local copies, waits for them, and re-layouts  8.53 us (6%)
  other arithmetic  5.74 us (4%)
    pallas_call x2, Pallas kernels, prefix(): pl.pallas_call(partial(prefix_kernel, own), in_specs=[smem] + [vmem] * 5,...  37.6 us
    ppermute x5, waiting for transfers between devices, other_pair(): return lax.ppermute(values, 'pair', [(0, 1), (1, 0)])  29.2 us
    pallas_call x2, Pallas kernels, reply(): pl.pallas_call(reply_kernel, grid_spec=pltpu.PrefetchScalarGridSpec(num_s...  15 us
    ppermute x8, starting transfers between devices, flip(): lax.ppermute(values, 'memory', [(m, m ^ bits) for m in range(HOLDERS)])  12 us
    ppermute x8, waiting for transfers between devices, flip(): lax.ppermute(values, 'memory', [(m, m ^ bits) for m in range(HOLDERS)])  10.7 us
    ppermute x5, starting transfers between devices, other_pair(): return lax.ppermute(values, 'pair', [(0, 1), (1, 0)])  9.76 us
    pallas_call x1, Pallas kernels, project(): pl.pallas_call(project_kernel, grid=(depth // part,), in_specs=[pl.BlockS...  8.17 us
    pallas_call x1, Pallas kernels, combine(): pl.pallas_call(combine_kernel, in_specs=[vmem] * 3, out_specs=[vmem] * 4,...  3.42 us
  transfers between devices with their start and end apart: 13, of which 8 were waited for; matrix products, arithmetic and copies ran while one was open for 5% of the time, Pallas kernels for 20%

profile of v1, /device:TPU:1, one launch (start us, length us, event | category | flops | bytes accessed | tf_op | source)
XLA Modules:
  0.0 147.2 jit_solution(11352564503119788911)
XLA Ops:
  0.6 2.1 %multiply_reduce_fusion = f32[256]{0:T(256)S(1)} fusion(bf16[256,4096]{1,0:T(8,128)(2,1)} %hidden_ref.1), kind=kLoop, calls=%fused_computation | loop fusion | flops 3145472 | bytes 2098176 | tf_op jit(solution)/shard_map/reduce_sum | solution.py:506
  2.7 4.5 %collective-permute-start = (f32[256]{0:T(256)S(1)}, f32[256]{0:T(256)S(1)}, u32[]{:S(2)}, u32[]{:S(2)}) collective-permute-start(f32[256]{0:T(256)S(1)} %multiply_reduce_fusion), channel_id=1, source_target_pairs={{0,1},{1,0},{2,3},{3,2},{4,5},{5,4},{6,7},{7,6},{8,9},{9,8},{10,11... | collective-permute-start | bytes 3080 | tf_op jit(solution)/shard_map/ppermute | solution.py:478
  7.9 1.3 reshape.82.gain_ref
  10.5 8.2 %shard_map.158 = (f32[128,1280]{1,0:T(8,128)}, f32[128,1280]{1,0:T(8,128)}) custom-call(s32[1]{0:T(128)} %bitcast.1.span_ref.parity_ref, f32[2,128]{1,0:T(2,128)} %rsqrt_bitcast_fusion.inverse_ref, bf16[256,4096]{1,0:T(8,128)(2,1)} %hidden_ref.1, bf16[1,4096]{1,0:T(2,128)(2,1)} %reshape.82.gain_ref, bf16[4096,1024]{1,0:T(8,128)(2,1)} %wq_ref.1, ...), custom_call_target="tpu_custom_call" | custom-call | flops 2684354560 | bytes 14680064 | tf_op jit(solution)/shard_map/pallas_call | solution.py:79
  21.6 14.1 %collective-permute-done.1.came_ref = f32[128,1280]{1,0:T(8,128)S(1)} collective-permute-done((f32[128,1280]{1,0:T(8,128)}, f32[128,1280]{1,0:T(8,128)S(1)}, u32[]{:S(2)}, u32[]{:S(2)}) %collective-permute-start.1) | collective-permute-done | bytes 655392 | tf_op jit(solution)/shard_map/ppermute | solution.py:478
  36.6 2.6 %shard_map.159 = (bf16[2,24,1408]{2,1,0:T(8,128)(2,1)}, bf16[2,24,1408]{2,1,0:T(8,128)(2,1)}, bf16[2,24,1408]{2,1,0:T(8,128)(2,1)}, bf16[2,24,1408]{2,1,0:T(8,128)(2,1)}, s32[1,128]{1,0:T(1,128)}) custom-call(s32[8]{0:T(128)} %home_ref.1, s32[1]{0:T(128)} %bitcast.me_ref, f32[128,1280]{1,0:T(8,128)} %get-tuple-element.19.keep_ref, f32[128,1280]{1,0:T(8,128)} %copy-done.1, ...), custom_call_target="tpu_custom_call" | custom-call | flops 69206016 | bytes 2097152 | tf_op jit(solution)/shard_map/pallas_call | solution.py:159
  40.5 2.6 %collective-permute-start.3 = (bf16[2,24,1408]{2,1,0:T(8,128)(2,1)}, bf16[2,24,1408]{2,1,0:T(8,128)(2,1)S(1)}, u32[]{:S(2)}, u32[]{:S(2)}) collective-permute-start(bf16[2,24,1408]{2,1,0:T(8,128)(2,1)} %get-tuple-element.24), channel_id=1, source_target_pairs={{0,8},{2,10},{4,12},{6,14},{8,0},{10,2},{12,4},{14,6},{1,9},{3,11}... | collective-permute-start | bytes 405512 | tf_op jit(solution)/shard_map/ppermute | solution.py:482
  44.1 3.6 %collective-permute-done.3 = bf16[2,24,1408]{2,1,0:T(8,128)(2,1)S(1)} collective-permute-done((bf16[2,24,1408]{2,1,0:T(8,128)(2,1)}, bf16[2,24,1408]{2,1,0:T(8,128)(2,1)S(1)}, u32[]{:S(2)}, u32[]{:S(2)}) %collective-permute-start.3) | collective-permute-done | bytes 135200 | tf_op jit(solution)/shard_map/ppermute | solution.py:482
  47.7 2.7 %collective-permute-done.4 = bf16[2,24,1408]{2,1,0:T(8,128)(2,1)S(1)} collective-permute-done((bf16[2,24,1408]{2,1,0:T(8,128)(2,1)}, bf16[2,24,1408]{2,1,0:T(8,128)(2,1)S(1)}, u32[]{:S(2)}, u32[]{:S(2)}) %collective-permute-start.4) | collective-permute-done | bytes 135200 | tf_op jit(solution)/shard_map/ppermute | solution.py:482
  50.4 2.0 %collective-permute-start.5 = (bf16[4,24,1408]{2,1,0:T(8,128)(2,1)S(1)}, bf16[4,24,1408]{2,1,0:T(8,128)(2,1)S(1)}, u32[]{:S(2)}, u32[]{:S(2)}) collective-permute-start(bf16[4,24,1408]{2,1,0:T(8,128)(2,1)S(1)} %pad_maximum_fusion), channel_id=1, source_target_pairs={{0,2},{2,0},{4,6},{6,4},{8,10},{10,8},{12,14},{14,12},{1,3},{3,1},... | collective-permute-start | bytes 811016 | tf_op jit(solution)/shard_map/ppermute | solution.py:482
  55.3 11.5 %collective-permute-done.6.rows_ref = bf16[8,24,1152]{2,1,0:T(8,128)(2,1)S(1)} collective-permute-done((bf16[8,24,1152]{2,1,0:T(8,128)(2,1)S(1)}, bf16[8,24,1152]{2,1,0:T(8,128)(2,1)S(1)}, u32[]{:S(2)}, u32[]{:S(2)}) %collective-permute-start.6) | collective-permute-done | bytes 442400 | tf_op jit(solution)/shard_map/ppermute | solution.py:478
  67.5 7.5 %shard_map.162 = (f32[4,24,1024]{2,1,0:T(8,128)}, f32[4,24,128]{2,1,0:T(8,128)}) custom-call(s32[4]{0:T(128)} %add_xor_fusion.where_ref, s32[1]{0:T(128)S(6)} %sub.3.parity_ref, bf16[8,24,1152]{2,1,0:T(8,128)(2,1)} %copy-done.3, bf16[8,24,128,128]{3,2,1,0:T(8,128)(2,1)} %bitcast.14, bf16[8,24,128,128]{3,2,1,0:T(8,128)(2,1)} %bitcast.16), custom_call_target="tpu_custom_call" | custom-call | flops 2000000000 | bytes 8388608 | tf_op jit(solution)/shard_map/pallas_call | solution.py:220
  75.0 17.9 %shard_map.163 = bf16[8,24,1152]{2,1,0:T(8,128)(2,1)} custom-call(s32[4]{0:T(128)} %add_xor_fusion.where_ref, bf16[8,24,1152]{2,1,0:T(8,128)(2,1)} %copy-done.3, bf16[4096,128]{1,0:T(8,128)(2,1)} %bitcast.22, bf16[4096,128]{1,0:T(8,128)(2,1)} %bitcast.24, f32[4,24,1024]{2,1,0:T(8,128)} %get-tuple-element.30.reply_ref, ...), custom_call_target="tpu_custom_call" | custom-call | flops 3221225472 | bytes 4194304 | tf_op jit(solution)/shard_map/pallas_call | solution.py:376
  93.8 7.5 %shard_map.160 = (f32[4,24,1024]{2,1,0:T(8,128)}, f32[4,24,128]{2,1,0:T(8,128)}) custom-call(s32[4]{0:T(128)} %add_xor_fusion.where_ref, s32[1]{0:T(128)} %bitcast.1.span_ref.parity_ref, bf16[8,24,1408]{2,1,0:T(8,128)(2,1)} %copy-done, bf16[8,24,128,128]{3,2,1,0:T(8,128)(2,1)} %bitcast.15, bf16[8,24,128,128]{3,2,1,0:T(8,128)(2,1)} %bitcast.17), custom_call_target="tpu_custom_call" | custom-call | flops 2000000000 | bytes 8388608 | tf_op jit(solution)/shard_map/pallas_call | solution.py:220
  101.3 19.6 %shard_map.161 = (f32[8,24,1024]{2,1,0:T(8,128)}, f32[8,24,128]{2,1,0:T(8,128)}) custom-call(s32[4]{0:T(128)} %add_xor_fusion.where_ref, bf16[8,24,1408]{2,1,0:T(8,128)(2,1)} %copy-done, bf16[4096,128]{1,0:T(8,128)(2,1)} %bitcast.23, bf16[4096,128]{1,0:T(8,128)(2,1)} %bitcast.25, f32[4,24,1024]{2,1,0:T(8,128)} %get-tuple-element.26.reply_ref, ...), custom_call_target="tpu_custom_call" | custom-call | flops 3221225472 | bytes 4194304 | tf_op jit(solution)/shard_map/pallas_call | solution.py:376
  121.7 3.4 %shard_map.164 = (bf16[2,24,1024]{2,1,0:T(8,128)(2,1)}, bf16[2,24,1024]{2,1,0:T(8,128)(2,1)}, bf16[2,24,1024]{2,1,0:T(8,128)(2,1)}, bf16[2,24,1024]{2,1,0:T(8,128)(2,1)}) custom-call(f32[8,24,1024]{2,1,0:T(8,128)} %get-tuple-element.28.out_ref, f32[8,24,128]{2,1,0:T(8,128)} %get-tuple-element.29.log_ref, bf16[8,24,1152]{2,1,0:T(8,128)(2,1)} %copy-done.2), custom_call_target="tpu_custom_call" | custom-call | flops 1000000 | bytes 2097152 | tf_op jit(solution)/shard_map/pallas_call | solution.py:415
  125.2 1.9 %collective-permute-start.9 = (bf16[2,24,1024]{2,1,0:T(8,128)(2,1)}, bf16[2,24,1024]{2,1,0:T(8,128)(2,1)S(1)}, u32[]{:S(2)}, u32[]{:S(2)}) collective-permute-start(bf16[2,24,1024]{2,1,0:T(8,128)(2,1)} %get-tuple-element.34), channel_id=1, source_target_pairs={{0,8},{2,10},{4,12},{6,14},{8,0},{10,2},{12,4},{14,6},{1,9},{3,11}... | collective-permute-start | bytes 294920 | tf_op jit(solution)/shard_map/ppermute | solution.py:482
  127.1 1.9 %collective-permute-start.10 = (bf16[2,24,1024]{2,1,0:T(8,128)(2,1)}, bf16[2,24,1024]{2,1,0:T(8,128)(2,1)S(1)}, u32[]{:S(2)}, u32[]{:S(2)}) collective-permute-start(bf16[2,24,1024]{2,1,0:T(8,128)(2,1)} %get-tuple-element.35), channel_id=1, source_target_pairs={{0,12},{2,14},{4,8},{6,10},{8,4},{10,6},{12,0},{14,2},{1,13},{3,15... | collective-permute-start | bytes 294920 | tf_op jit(solution)/shard_map/ppermute | solution.py:482
  130.4 2.6 %collective-permute-done.10.near3_ref = bf16[2,24,1024]{2,1,0:T(8,128)(2,1)S(1)} collective-permute-done((bf16[2,24,1024]{2,1,0:T(8,128)(2,1)}, bf16[2,24,1024]{2,1,0:T(8,128)(2,1)S(1)}, u32[]{:S(2)}, u32[]{:S(2)}) %collective-permute-start.10) | collective-permute-done | bytes 98336 | tf_op jit(solution)/shard_map/ppermute | solution.py:482
  133.1 2.2 %collective-permute-start.11 = (bf16[4,24,1024]{2,1,0:T(8,128)(2,1)S(1)}, bf16[4,24,1024]{2,1,0:T(8,128)(2,1)S(1)}, u32[]{:S(2)}, u32[]{:S(2)}) collective-permute-start(bf16[4,24,1024]{2,1,0:T(8,128)(2,1)S(1)} %pad_maximum_fusion.1), channel_id=1, source_target_pairs={{0,2},{2,0},{4,6},{6,4},{8,10},{10,8},{12,14},{14,12},{1,3},{3,1},... | collective-permute-start | bytes 589832 | tf_op jit(solution)/shard_map/ppermute | solution.py:482
  136.2 2.3 %collective-permute-start.12 = (bf16[8,24,256]{2,1,0:T(8,128)(2,1)S(1)}, bf16[8,24,256]{2,1,0:T(8,128)(2,1)S(1)}, u32[]{:S(2)}, u32[]{:S(2)}) collective-permute-start(bf16[8,24,256]{2,1,0:T(8,128)(2,1)S(1)} %slice.86.own_ref), channel_id=1, source_target_pairs={{0,1},{1,0},{2,3},{3,2},{4,5},{5,4},{6,7},{7,6},{8,9},{9,8},{10,11... | collective-permute-start | bytes 294920 | tf_op jit(solution)/shard_map/ppermute | solution.py:478
  138.5 3.7 %collective-permute-done.12.other_ref = bf16[8,24,256]{2,1,0:T(8,128)(2,1)S(1)} collective-permute-done((bf16[8,24,256]{2,1,0:T(8,128)(2,1)S(1)}, bf16[8,24,256]{2,1,0:T(8,128)(2,1)S(1)}, u32[]{:S(2)}, u32[]{:S(2)}) %collective-permute-start.12) | collective-permute-done | bytes 98336 | tf_op jit(solution)/shard_map/ppermute | solution.py:478
  142.8 1.7 %shard_map.166 = bf16[2,16,24,128]{3,2,1,0:T(8,128)(2,1)} custom-call(s32[1]{0:T(128)} %bitcast.me_ref, s32[1]{0:T(128)} %bitcast.1.span_ref.parity_ref, bf16[8,24,256]{2,1,0:T(8,128)(2,1)} %copy-done.4, bf16[8,24,256]{2,1,0:T(8,128)(2,1)} %copy-done.9), custom_call_target="tpu_custom_call" | custom-call | bytes 524288 | tf_op jit(solution)/shard_map/pallas_call | solution.py:467
  145.2 2.1 %shard_map.165 = bf16[128,1024]{1,0:T(8,128)(2,1)} custom-call(s32[1,128]{1,0:T(1,128)} %get-tuple-element.21.target_ref, bf16[2,24,1024]{2,1,0:T(8,128)(2,1)} %get-tuple-element.32.near0_ref, bf16[2,24,1024]{2,1,0:T(8,128)(2,1)} %copy-done.5, bf16[2,24,1024]{2,1,0:T(8,128)(2,1)} %copy-done.6, bf16[2,24,1024]{2,1,0:T(8,128)(2,1)} %copy-done.7, ...), custom_call_target="tpu_custom_call" | custom-call | flops 50331648 | bytes 1048576 | tf_op jit(solution)/shard_map/pallas_call | solution.py:443
  (65 shorter events, 16.9 us)
Async XLA Ops:
  2.7 7.2 %collective-permute-start = (f32[256]{0:T(256)S(1)}, f32[256]{0:T(256)S(1)}, u32[]{:S(2)}, u32[]{:S(2)}) collective-permute-start(f32[256]{0:T(256)S(1)} %multiply_reduce_fusion), channel_id=1, source_target_pairs={{0,1},{1,0},{2,3},{3,2},{4,5},{5,4},{6,7},{7,6},{8,9},{9,8},{10,11... | collective-permute-start | bytes 3080 | tf_op jit(solution)/shard_map/ppermute | solution.py:478
  10.5 10.5 %copy-start.10 = (bf16[128]{0:T(256)(128)(2,1)S(1)}, bf16[128]{0:T(256)(128)(2,1)}, u32[]{:S(2)}) copy-start(bf16[128]{0:T(256)(128)(2,1)} %param.22) | copy-start | bytes 772
  10.5 10.5 %copy-start.11 = (bf16[128]{0:T(256)(128)(2,1)S(1)}, bf16[128]{0:T(256)(128)(2,1)}, u32[]{:S(2)}) copy-start(bf16[128]{0:T(256)(128)(2,1)} %param.21) | copy-start | bytes 772
  18.7 17.0 %collective-permute-start.1 = (f32[128,1280]{1,0:T(8,128)}, f32[128,1280]{1,0:T(8,128)S(1)}, u32[]{:S(2)}, u32[]{:S(2)}) collective-permute-start(f32[128,1280]{1,0:T(8,128)} %get-tuple-element.20), channel_id=1, source_target_pairs={{0,1},{1,0},{2,3},{3,2},{4,5},{5,4},{6,7},{7,6},{8,9},{9,8},{10,11... | collective-permute-start | bytes 1966088 | tf_op jit(solution)/shard_map/ppermute | solution.py:478
  35.7 0.9 copy-start.1
  39.2 4.8 %collective-permute-start.2 = (bf16[2,24,1408]{2,1,0:T(8,128)(2,1)}, bf16[2,24,1408]{2,1,0:T(8,128)(2,1)S(1)}, u32[]{:S(2)}, u32[]{:S(2)}) collective-permute-start(bf16[2,24,1408]{2,1,0:T(8,128)(2,1)} %get-tuple-element.23), channel_id=1, source_target_pairs={{0,4},{2,6},{4,0},{6,2},{8,12},{10,14},{12,8},{14,10},{1,5},{3,7},... | collective-permute-start | bytes 405512 | tf_op jit(solution)/shard_map/ppermute | solution.py:482
  40.5 7.2 %collective-permute-start.3 = (bf16[2,24,1408]{2,1,0:T(8,128)(2,1)}, bf16[2,24,1408]{2,1,0:T(8,128)(2,1)S(1)}, u32[]{:S(2)}, u32[]{:S(2)}) collective-permute-start(bf16[2,24,1408]{2,1,0:T(8,128)(2,1)} %get-tuple-element.24), channel_id=1, source_target_pairs={{0,8},{2,10},{4,12},{6,14},{8,0},{10,2},{12,4},{14,6},{1,9},{3,11}... | collective-permute-start | bytes 405512 | tf_op jit(solution)/shard_map/ppermute | solution.py:482
  43.1 7.3 %collective-permute-start.4 = (bf16[2,24,1408]{2,1,0:T(8,128)(2,1)}, bf16[2,24,1408]{2,1,0:T(8,128)(2,1)S(1)}, u32[]{:S(2)}, u32[]{:S(2)}) collective-permute-start(bf16[2,24,1408]{2,1,0:T(8,128)(2,1)} %get-tuple-element.25), channel_id=1, source_target_pairs={{0,12},{2,14},{4,8},{6,10},{8,4},{10,6},{12,0},{14,2},{1,13},{3,15... | collective-permute-start | bytes 405512 | tf_op jit(solution)/shard_map/ppermute | solution.py:482
  50.4 3.2 %collective-permute-start.5 = (bf16[4,24,1408]{2,1,0:T(8,128)(2,1)S(1)}, bf16[4,24,1408]{2,1,0:T(8,128)(2,1)S(1)}, u32[]{:S(2)}, u32[]{:S(2)}) collective-permute-start(bf16[4,24,1408]{2,1,0:T(8,128)(2,1)S(1)} %pad_maximum_fusion), channel_id=1, source_target_pairs={{0,2},{2,0},{4,6},{6,4},{8,10},{10,8},{12,14},{14,12},{1,3},{3,1},... | collective-permute-start | bytes 811016 | tf_op jit(solution)/shard_map/ppermute | solution.py:482
  53.7 21.3 %copy-start = (bf16[8,24,1408]{2,1,0:T(8,128)(2,1)}, bf16[8,24,1408]{2,1,0:T(8,128)(2,1)S(1)}, u32[]{:S(2)}) copy-start(bf16[8,24,1408]{2,1,0:T(8,128)(2,1)S(1)} %slice_dynamic-update-slice_fusion.rows_ref) | copy-start | bytes 1622020
  53.8 13.0 %collective-permute-start.6 = (bf16[8,24,1152]{2,1,0:T(8,128)(2,1)S(1)}, bf16[8,24,1152]{2,1,0:T(8,128)(2,1)S(1)}, u32[]{:S(2)}, u32[]{:S(2)}) collective-permute-start(bf16[8,24,1152]{2,1,0:T(8,128)(2,1)S(1)} %slice.82), channel_id=1, source_target_pairs={{0,1},{1,0},{2,3},{3,2},{4,5},{5,4},{6,7},{7,6},{8,9},{9,8},{10,11... | collective-permute-start | bytes 1327112 | tf_op jit(solution)/shard_map/ppermute | solution.py:478
  66.8 0.8 copy-start.3
  93.0 28.0 %collective-permute-start.7 = (bf16[8,24,1152]{2,1,0:T(8,128)(2,1)}, bf16[8,24,1152]{2,1,0:T(8,128)(2,1)S(1)}, u32[]{:S(2)}, u32[]{:S(2)}) collective-permute-start(bf16[8,24,1152]{2,1,0:T(8,128)(2,1)} %shard_map.163), channel_id=1, source_target_pairs={{0,1},{1,0},{2,3},{3,2},{4,5},{5,4},{6,7},{7,6},{8,9},{9,8},{10,11... | collective-permute-start | bytes 1327112 | tf_op jit(solution)/shard_map/ppermute | solution.py:478
  120.9 0.8 copy-start.2
  125.2 4.7 %collective-permute-start.8 = (bf16[2,24,1024]{2,1,0:T(8,128)(2,1)}, bf16[2,24,1024]{2,1,0:T(8,128)(2,1)S(1)}, u32[]{:S(2)}, u32[]{:S(2)}) collective-permute-start(bf16[2,24,1024]{2,1,0:T(8,128)(2,1)} %get-tuple-element.33), channel_id=1, source_target_pairs={{0,4},{2,6},{4,0},{6,2},{8,12},{10,14},{12,8},{14,10},{1,5},{3,7},... | collective-permute-start | bytes 294920 | tf_op jit(solution)/shard_map/ppermute | solution.py:482
  125.2 5.3 %collective-permute-start.9 = (bf16[2,24,1024]{2,1,0:T(8,128)(2,1)}, bf16[2,24,1024]{2,1,0:T(8,128)(2,1)S(1)}, u32[]{:S(2)}, u32[]{:S(2)}) collective-permute-start(bf16[2,24,1024]{2,1,0:T(8,128)(2,1)} %get-tuple-element.34), channel_id=1, source_target_pairs={{0,8},{2,10},{4,12},{6,14},{8,0},{10,2},{12,4},{14,6},{1,9},{3,11}... | collective-permute-start | bytes 294920 | tf_op jit(solution)/shard_map/ppermute | solution.py:482
  127.1 5.9 %collective-permute-start.10 = (bf16[2,24,1024]{2,1,0:T(8,128)(2,1)}, bf16[2,24,1024]{2,1,0:T(8,128)(2,1)S(1)}, u32[]{:S(2)}, u32[]{:S(2)}) collective-permute-start(bf16[2,24,1024]{2,1,0:T(8,128)(2,1)} %get-tuple-element.35), channel_id=1, source_target_pairs={{0,12},{2,14},{4,8},{6,10},{8,4},{10,6},{12,0},{14,2},{1,13},{3,15... | collective-permute-start | bytes 294920 | tf_op jit(solution)/shard_map/ppermute | solution.py:482
  129.8 14.7 %copy-start.5 = (bf16[2,24,1024]{2,1,0:T(8,128)(2,1)}, bf16[2,24,1024]{2,1,0:T(8,128)(2,1)S(1)}, u32[]{:S(2)}) copy-start(bf16[2,24,1024]{2,1,0:T(8,128)(2,1)S(1)} %collective-permute-done.8.near1_ref) | copy-start | bytes 294916
  130.4 14.1 %copy-start.6 = (bf16[2,24,1024]{2,1,0:T(8,128)(2,1)}, bf16[2,24,1024]{2,1,0:T(8,128)(2,1)S(1)}, u32[]{:S(2)}) copy-start(bf16[2,24,1024]{2,1,0:T(8,128)(2,1)S(1)} %collective-permute-done.9.near2_ref) | copy-start | bytes 294916
  133.0 11.5 %copy-start.7 = (bf16[2,24,1024]{2,1,0:T(8,128)(2,1)}, bf16[2,24,1024]{2,1,0:T(8,128)(2,1)S(1)}, u32[]{:S(2)}) copy-start(bf16[2,24,1024]{2,1,0:T(8,128)(2,1)S(1)} %collective-permute-done.10.near3_ref) | copy-start | bytes 294916
  133.1 11.4 %collective-permute-start.11 = (bf16[4,24,1024]{2,1,0:T(8,128)(2,1)S(1)}, bf16[4,24,1024]{2,1,0:T(8,128)(2,1)S(1)}, u32[]{:S(2)}, u32[]{:S(2)}) collective-permute-start(bf16[4,24,1024]{2,1,0:T(8,128)(2,1)S(1)} %pad_maximum_fusion.1), channel_id=1, source_target_pairs={{0,2},{2,0},{4,6},{6,4},{8,10},{10,8},{12,14},{14,12},{1,3},{3,1},... | collective-permute-start | bytes 589832 | tf_op jit(solution)/shard_map/ppermute | solution.py:482
  136.2 6.0 %copy-start.4 = (bf16[8,24,256]{2,1,0:T(8,128)(2,1)}, bf16[8,24,256]{2,1,0:T(8,128)(2,1)S(1)}, u32[]{:S(2)}) copy-start(bf16[8,24,256]{2,1,0:T(8,128)(2,1)S(1)} %slice.86.own_ref) | copy-start | bytes 294916
  136.2 6.0 %collective-permute-start.12 = (bf16[8,24,256]{2,1,0:T(8,128)(2,1)S(1)}, bf16[8,24,256]{2,1,0:T(8,128)(2,1)S(1)}, u32[]{:S(2)}, u32[]{:S(2)}) collective-permute-start(bf16[8,24,256]{2,1,0:T(8,128)(2,1)S(1)} %slice.86.own_ref), channel_id=1, source_target_pairs={{0,1},{1,0},{2,3},{3,2},{4,5},{5,4},{6,7},{7,6},{8,9},{9,8},{10,11... | collective-permute-start | bytes 294920 | tf_op jit(solution)/shard_map/ppermute | solution.py:478
  144.5 0.7 copy-start.8
  (1 other events, 0.6 us)

commit v2 on v1

--- a/solution.py
+++ b/solution.py
@@ -19,6 +19,7 @@
 HEADS = 8
 QW = HEADS * HD
 SLOTS = HOLDERS * CAP
+BLOCK = 256
 LENGTH_AT = QW
 KEY_AT = QW + HD
 VALUE_AT = QW + 2 * HD
@@ -26,11 +27,10 @@
 SCALE = 1.4426950408889634 / HD**0.5
 F32 = jnp.float32
 BF16 = jnp.bfloat16
-VMEM_LIMIT = 56 * 1024 * 1024
-
-
-def params(**more):
-    return pltpu.CompilerParams(vmem_limit_bytes=VMEM_LIMIT, **more)
+
+
+def params(mebibytes):
+    return pltpu.CompilerParams(vmem_limit_bytes=mebibytes * 2**20)
 
 
 def lane_ids(shape):
@@ -45,57 +45,53 @@
 
 
 def project_kernel(
-    span_ref, inverse_ref, hidden_ref, gain_ref, wq_ref, wk_ref, wv_ref, keep_ref, send_ref, scale_ref
+    span_ref,
+    mine_ref,
+    theirs_ref,
+    hidden_ref,
+    gain_ref,
+    wq_ref,
+    wk_ref,
+    wv_ref,
+    keep_ref,
+    send_ref,
+    normed_ref,
 ):
     span = span_ref[0]
-    step = pl.program_id(0)
-
-    @pl.when(step == 0)
-    def _():
-        first = to_column(inverse_ref[0:1, :])
-        second = to_column(inverse_ref[1:2, :])
-        scale_ref[0:ROWS, :] = jnp.broadcast_to(jnp.where(span == 0, first, second), (ROWS, HD))
-        scale_ref[ROWS:, :] = jnp.broadcast_to(jnp.where(span == 0, second, first), (ROWS, HD))
-        keep_ref[...] = jnp.zeros_like(keep_ref)
-        send_ref[...] = jnp.zeros_like(send_ref)
-
-    own_start = pl.multiple_of(span * ROWS, ROWS)
-    other_start = pl.multiple_of((1 - span) * ROWS, ROWS)
-    gain = gain_ref[...].astype(F32)
-    for start, where, out_ref in ((other_start, ROWS, send_ref), (own_start, 0, keep_ref)):
-        rows = hidden_ref[pl.ds(start, ROWS), :].astype(F32)
-        normed = (rows * scale_ref[where : where + ROWS, 0:1] * gain).astype(BF16)
-        for at, w_ref in ((0, wq_ref), (QW, wk_ref), (QW + HD, wv_ref)):
-            width = w_ref.shape[1]
-            out_ref[:, at : at + width] += jnp.dot(normed, w_ref[...], preferred_element_type=F32)
-
-
-def project(span, inverse, hidden, gain, w_query, w_key, w_value):
+    inverse = lax.rsqrt((mine_ref[...] + theirs_ref[...]) / D + EPSILON)
+    first = to_column(inverse[0:1, :])
+    second = to_column(inverse[1:2, :])
+    scales = (jnp.where(span == 0, first, second), jnp.where(span == 0, second, first))
+    gain = gain_ref[...].astype(F32).reshape(1, -1)
+    for where, start in enumerate((span * ROWS, (1 - span) * ROWS)):
+        rows = hidden_ref[pl.ds(pl.multiple_of(start, ROWS), ROWS), :].astype(F32)
+        normed = rows * scales[where] * gain
+        normed_ref[where * ROWS : (where + 1) * ROWS, :] = normed.astype(BF16)
+    pieces = [(at, wq_ref.at[:, at : at + 256]) for at in range(0, QW, 256)]
+    pieces += [(QW, wk_ref), (QW + HD, wv_ref)]
+    for at, w_ref in pieces:
+        part = slice(at, at + w_ref.shape[1])
+        total = jnp.dot(normed_ref[...], w_ref[...], preferred_element_type=F32)
+        keep_ref[:, part] = total[:ROWS]
+        send_ref[:, part] = total[ROWS:]
+
+
+def project(span, mine, theirs, hidden, gain, w_query, w_key, w_value):
     depth = hidden.shape[1]
-    part = 1024
     width = QW + 2 * HD
     out = jax.ShapeDtypeStruct((ROWS, width), F32)
-    whole = pl.BlockSpec((ROWS, width), lambda k: (0, 0))
+    vmem = pl.BlockSpec(memory_space=pltpu.VMEM)
     return pl.pallas_call(
         project_kernel,
-        grid=(depth // part,),
-        in_specs=[
-            pl.BlockSpec(memory_space=pltpu.SMEM),
-            pl.BlockSpec((2, ROWS), lambda k: (0, 0)),
-            pl.BlockSpec((2 * ROWS, part), lambda k: (0, k)),
-            pl.BlockSpec((1, part), lambda k: (0, k)),
-            pl.BlockSpec((part, QW), lambda k: (k, 0)),
-            pl.BlockSpec((part, HD), lambda k: (k, 0)),
-            pl.BlockSpec((part, HD), lambda k: (k, 0)),
-        ],
-        out_specs=[whole, whole],
+        in_specs=[pl.BlockSpec(memory_space=pltpu.SMEM)] + [vmem] * 7,
+        out_specs=[vmem] * 2,
         out_shape=[out, out],
-        scratch_shapes=[pltpu.VMEM((2 * ROWS, HD), F32)],
-        compiler_params=params(),
+        scratch_shapes=[pltpu.VMEM((2 * ROWS, depth), BF16)],
+        compiler_params=params(20),
         cost_estimate=pl.CostEstimate(
             flops=2 * 2 * ROWS * depth * width, bytes_accessed=14 * 2**20, transcendentals=0
         ),
-    )(span, inverse, hidden, gain, w_query, w_key, w_value)
+    )(span, mine, theirs, hidden, gain, w_query, w_key, w_value)
 
 
 def spread_kernel(
@@ -136,7 +132,7 @@
     for head in range(HEADS + 3):
         at = head * HD
         if head == HEADS:
-            rows = length_ref[...]
+            rows = jnp.broadcast_to(to_column(length_ref[...].astype(F32)), square).astype(BF16)
         else:
             source = at if head < HEADS else at - HD
             part = slice(source, source + HD)
@@ -161,7 +157,7 @@
         in_specs=[smem, smem] + [vmem] * 7,
         out_specs=[vmem] * 5,
         out_shape=[block] * 4 + [jax.ShapeDtypeStruct((1, ROWS), jnp.int32)],
-        compiler_params=params(),
+        compiler_params=params(8),
         cost_estimate=pl.CostEstimate(
             flops=2 * SLOTS * ROWS * ROW_WIDTH, bytes_accessed=2 * 2**20, transcendentals=0
         ),
@@ -174,44 +170,48 @@
 def reply_kernel(where_ref, parity_ref, rows_ref, keys_ref, values_ref, out_ref, log_ref, wide_ref):
     wide_ref[...] = rows_ref[0, :, 0:KEY_AT].astype(F32)
     group = 8
+    parts = CAP // group
     lanes = lane_ids((group, HD))
     lines = lax.broadcasted_iota(jnp.int32, (group, HD), 0)
-    for part in range(CAP // group):
+    scores = []
+    for part in range(parts):
         slots = slice(part * group, (part + 1) * group)
-        visible = lanes.astype(F32) < wide_ref[slots, LENGTH_AT : LENGTH_AT + HD]
         stacked = jnp.concatenate(
             [wide_ref[slots, head * HD : (head + 1) * HD] for head in range(HEADS)], axis=0
         ).astype(BF16)
         keys = keys_ref[0, slots].reshape(group * HD, HD)
-        values = values_ref[0, slots].reshape(group * HD, HD)
-        scores = lax.dot_general(stacked, keys, NT, preferred_element_type=F32)
-        weights = []
-        sums = []
+        scores.append(lax.dot_general(stacked, keys, NT, preferred_element_type=F32))
+    weights = []
+    totals = []
+    for part in range(parts):
+        slots = slice(part * group, (part + 1) * group)
+        visible = lanes.astype(F32) < wide_ref[slots, LENGTH_AT : LENGTH_AT + HD]
+        visible = jnp.concatenate([visible] * HEADS, axis=0)
+        own = jnp.zeros((HEADS * group, HD), F32)
+        line = lax.broadcasted_iota(jnp.int32, own.shape, 0) % group
+        for slot in range(group):
+            own = jnp.where(line == slot, scores[part][:, slot * HD : (slot + 1) * HD], own)
+        own = jnp.where(visible, own, MASKED)
+        highest = jnp.max(own, axis=1, keepdims=True)
+        weight = jnp.exp2((own - highest) * SCALE)
+        total = jnp.sum(weight, axis=1, keepdims=True)
+        totals.append(total)
+        log = jnp.broadcast_to(highest * SCALE + jnp.log2(total), own.shape)
         logs = jnp.zeros((group, HD), F32)
         for head in range(HEADS):
-            mine = slice(head * group, (head + 1) * group)
-            own = scores[mine, 0:HD]
-            for slot in range(1, group):
-                own = jnp.where(lines == slot, scores[mine, slot * HD : (slot + 1) * HD], own)
-            own = jnp.where(visible, own, MASKED)
-            highest = jnp.max(own, axis=1, keepdims=True)
-            weight = jnp.exp2((own - highest) * SCALE)
-            total = jnp.sum(weight, axis=1, keepdims=True)
-            sums.append(total)
-            logs = jnp.where(lanes == head, highest * SCALE + jnp.log2(total), logs)
-            weights.append(
-                jnp.concatenate(
-                    [jnp.where(lines == slot, weight, 0.0) for slot in range(group)], axis=1
-                )
+            logs = jnp.where(lanes == head, log[head * group : (head + 1) * group], logs)
+        log_ref[0, slots, :] = logs
+        weights.append(
+            jnp.concatenate(
+                [jnp.where(line == slot, weight, 0.0).astype(BF16) for slot in range(group)], axis=1
             )
-        mixed = jnp.dot(
-            jnp.concatenate(weights, axis=0).astype(BF16), values, preferred_element_type=F32
         )
+    for part in range(parts):
+        slots = slice(part * group, (part + 1) * group)
+        values = values_ref[0, slots].reshape(group * HD, HD)
+        mixed = jnp.dot(weights[part], values, preferred_element_type=F32) / totals[part]
         for head in range(HEADS):
-            out_ref[0, slots, head * HD : (head + 1) * HD] = (
-                mixed[head * group : (head + 1) * group] / sums[head]
-            )
-        log_ref[0, slots, :] = logs
+            out_ref[0, slots, head * HD : (head + 1) * HD] = mixed[head * group : (head + 1) * group]
 
 
 def reply(where, parity, rows, keys, values):
@@ -237,7 +237,7 @@
             jax.ShapeDtypeStruct((quarter, CAP, QW), F32),
             jax.ShapeDtypeStruct((quarter, CAP, HD), F32),
         ],
-        compiler_params=params(),
+        compiler_params=params(12),
         cost_estimate=pl.CostEstimate(
             flops=2 * 10**9, bytes_accessed=8 * 2**20, transcendentals=10**6
         ),
@@ -272,58 +272,40 @@
     *refs,
 ):
     if own:
-        out_ref, log_ref, query_ref, score_ref = refs
+        out_ref, log_ref, *scratch = refs
     else:
-        sent_ref, query_ref, score_ref, out_ref, log_ref = refs
-    span = 512
-    tokens = keys_ref.shape[0]
-    units = 2
-    unit_heads = HEADS // units
-    unit_rows = unit_heads * SLOTS
+        sent_ref, *scratch, out_ref, log_ref = refs
+    query_ref, score0_ref, score1_ref, mixed_ref, logs_ref = scratch
     for head in range(HEADS):
         rows = rows_ref[:, :, head * HD : (head + 1) * HD].astype(F32)
         query_ref[head * SLOTS : (head + 1) * SLOTS, :] = rows.reshape(SLOTS, HD).astype(BF16)
+    held = (score0_ref, score1_ref)
+    total_rows = HEADS * SLOTS
+
+    def score(block):
+        queries = query_ref[block * BLOCK : (block + 1) * BLOCK]
+        held[block % 2][...] = lax.dot_general(
+            queries, keys_ref[...], NT, preferred_element_type=F32
+        )
+
+    score(0)
+    for block in range(total_rows // BLOCK):
+        here = slice(block * BLOCK, (block + 1) * BLOCK)
+        scores = held[block % 2][...]
+        highest = jnp.max(scores, axis=1, keepdims=True)
+        if block + 1 < total_rows // BLOCK:
+            score(block + 1)
+        weights = jnp.exp2((scores - highest) * SCALE)
+        total = jnp.sum(weights, axis=1, keepdims=True)
+        mixed = jnp.dot(weights.astype(BF16), values_ref[...], preferred_element_type=F32)
+        mixed_ref[here] = mixed / total
+        logs_ref[here] = jnp.broadcast_to(highest * SCALE + jnp.log2(total), (BLOCK, HD))
     block_lanes = lane_ids((HOLDERS, CAP, HD))
     logs = jnp.zeros((HOLDERS, CAP, HD), F32)
-    for unit in range(units):
-        queries = query_ref.at[unit * unit_rows : (unit + 1) * unit_rows]
-
-        def score(step, highest):
-            start = pl.multiple_of(step * span, span)
-            scores = lax.dot_general(
-                queries[...], keys_ref[pl.ds(start, span), :], NT, preferred_element_type=F32
-            )
-            score_ref[step] = scores
-            for piece in range(span // HD):
-                highest = jnp.maximum(highest, scores[:, piece * HD : (piece + 1) * HD])
-            return highest
-
-        highest = lax.fori_loop(
-            0, tokens // span, score, jnp.full((unit_rows, HD), MASKED, F32)
-        )
-        highest = jnp.max(highest, axis=1, keepdims=True)
-
-        def mix(step, carried):
-            total, mixed = carried
-            start = pl.multiple_of(step * span, span)
-            weights = jnp.exp2((score_ref[step] - highest) * SCALE)
-            for piece in range(span // HD):
-                total = total + weights[:, piece * HD : (piece + 1) * HD]
-            mixed = mixed + jnp.dot(
-                weights.astype(BF16), values_ref[pl.ds(start, span), :], preferred_element_type=F32
-            )
-            return total, mixed
-
-        empty = jnp.zeros((unit_rows, HD), F32)
-        total, mixed = lax.fori_loop(0, tokens // span, mix, (empty, empty))
-        total = jnp.sum(total, axis=1, keepdims=True)
-        mixed = mixed / total
-        log = jnp.broadcast_to(highest * SCALE + jnp.log2(total), (unit_rows, HD))
-        for index in range(unit_heads):
-            head = unit * unit_heads + index
-            mine = slice(index * SLOTS, (index + 1) * SLOTS)
-            out_ref[:, :, head * HD : (head + 1) * HD] = mixed[mine].reshape(HOLDERS, CAP, HD)
-            logs = jnp.where(block_lanes == head, log[mine].reshape(HOLDERS, CAP, HD), logs)
+    for head in range(HEADS):
+        mine = slice(head * SLOTS, (head + 1) * SLOTS)
+        out_ref[:, :, head * HD : (head + 1) * HD] = mixed_ref[mine].reshape(HOLDERS, CAP, HD)
+        logs = jnp.where(block_lanes == head, logs_ref[mine].reshape(HOLDERS, CAP, HD), logs)
     log_ref[...] = logs
     for index in range(reply_ref.shape[0]):
         merge_in(
@@ -365,7 +347,10 @@
     log = (HOLDERS, CAP, HD)
     scratch = [
         pltpu.VMEM((HEADS * SLOTS, HD), BF16),
-        pltpu.VMEM((keys.shape[0] // 512, HEADS * SLOTS // 2, 512), F32),
+        pltpu.VMEM((BLOCK, keys.shape[0]), F32),
+        pltpu.VMEM((BLOCK, keys.shape[0]), F32),
+        pltpu.VMEM((HEADS * SLOTS, HD), F32),
+        pltpu.VMEM((HEADS * SLOTS, HD), F32),
     ]
     if own:
         out_shape = [jax.ShapeDtypeStruct(out, F32), jax.ShapeDtypeStruct(log, F32)]
@@ -379,7 +364,7 @@
         out_specs=[vmem] * len(out_shape),
         out_shape=out_shape,
         scratch_shapes=scratch,
-        compiler_params=params(),
+        compiler_params=params(24),
         cost_estimate=pl.CostEstimate(
             flops=4 * work * HD, bytes_accessed=4 * 2**20, transcendentals=work
         ),
@@ -417,7 +402,7 @@
         in_specs=[vmem] * 3,
         out_specs=[vmem] * 4,
         out_shape=[jax.ShapeDtypeStruct((2, CAP, QW), BF16)] * 4,
-        compiler_params=params(),
+        compiler_params=params(6),
         cost_estimate=pl.CostEstimate(flops=10**6, bytes_accessed=2 * 2**20, transcendentals=10**5),
     )(out, log, came)
 
@@ -446,7 +431,7 @@
         out_specs=vmem,
         out_shape=jax.ShapeDtypeStruct((ROWS, QW), BF16),
         scratch_shapes=[pltpu.VMEM((HOLDERS, CAP, QW), F32)],
-        compiler_params=params(),
+        compiler_params=params(6),
         cost_estimate=pl.CostEstimate(
             flops=2 * SLOTS * ROWS * QW, bytes_accessed=2**20, transcendentals=0
         ),
@@ -469,7 +454,7 @@
         in_specs=[smem, smem, vmem, vmem],
         out_specs=vmem,
         out_shape=jax.ShapeDtypeStruct((2, 2 * HOLDERS, CAP, HD), BF16),
-        compiler_params=params(),
+        compiler_params=params(4),
         cost_estimate=pl.CostEstimate(flops=0, bytes_accessed=2**19, transcendentals=0),
     )(me, span, own, other)
 
@@ -504,10 +489,16 @@
 
     widened = hidden.astype(F32)
     squares = jnp.sum(widened * widened, axis=1)
-    squares = squares + other_pair(squares)
-    inverse = lax.rsqrt(squares / D + EPSILON).reshape(2, ROWS)
+    theirs = other_pair(squares)
     keep, send = project(
-        span, inverse, hidden, norm_gain.reshape(1, -1), w_query, w_key, w_value
+        span,
+        squares.reshape(2, ROWS),
+        theirs.reshape(2, ROWS),
+        hidden,
+        norm_gain,
+        w_query,
+        w_key,
+        w_value,
     )
     came = other_pair(send)
 
@@ -519,10 +510,9 @@
     sine = jnp.sin(angles)
     cosine = jnp.concatenate([cosine, cosine], axis=1)
     sine = jnp.concatenate([-sine, sine], axis=1)
-    lengths = jnp.broadcast_to(reply_length.astype(BF16)[:, None], (ROWS, HD))
     bias = jnp.concatenate([query_bias, key_bias, value_bias]).astype(F32).reshape(1, -1)
     *blocks, target = spread(
-        prompt_home, me, keep, came, bias, cosine, sine, lengths, prefix_ids.reshape(1, ROWS)
+        prompt_home, me, keep, came, bias, cosine, sine, reply_length.reshape(1, ROWS), prefix_ids.reshape(1, ROWS)
     )
 
     near = [blocks[0]] + [flip(blocks[step], 2 * step) for step in range(1, 4)]
@@ -540,16 +530,20 @@
     prompt_keys = prefix_keys[0]
     prompt_values = prefix_values[0]
     own_reply = reply(where, span, rows, keys, values)
-    out, log = prefix(True, where, rows, prompt_keys, prompt_values, *own_reply)
+    own_reply, partner_rows, partner_fresh = lax.optimization_barrier(
+        (own_reply, partner_rows, partner_fresh)
+    )
+    stored = store(me, span, fresh, partner_fresh).reshape(2, 1, 2 * SLOTS, HD)
     partner_reply = reply(where, 1 - span, partner_rows, keys, values)
     (sent,) = prefix(False, where, partner_rows, prompt_keys, prompt_values, *partner_reply)
     came = other_pair(sent)
+    rows, sent, stored = lax.optimization_barrier((rows, sent, stored))
+    out, log = prefix(True, where, rows, prompt_keys, prompt_values, *own_reply)
     merged = combine(out, log, came)
 
     nears = [merged[0]] + [flip(merged[step], 2 * step) for step in range(1, 4)]
     fars = flip(jnp.stack([block[1] for block in nears]), 1)
     attention = unplace(target, nears, fars)
-    stored = store(me, span, fresh, partner_fresh).reshape(2, 1, 2 * SLOTS, HD)
     return attention, stored
 
 

time: 148 us -> 108 us (0.73)
  Pallas kernels: 70.5 us -> 33.8 us
  waiting for transfers between devices: 39.9 us -> 28.1 us
  local copies, waits for them, and re-layouts: 8.53 us -> 14.6 us
  starting transfers between devices: 21.8 us -> 26.8 us
  other arithmetic: 5.74 us -> 3.25 us
    pallas_call x2, Pallas kernels: 37.6 us -> 19.6 us  [prefix(): pl.pallas_call(partial(prefix_kernel, own), in_specs=[smem] + [vmem] * 5,...]
    ppermute x5, waiting for transfers between devices: 29.2 us -> 16.5 us  [other_pair(): return lax.ppermute(values, 'pair', [(0, 1), (1, 0)])]
    unnamed x30 -> x40, local copies, waits for them, and re-layouts: 2.99 us -> 13.8 us
    pallas_call x2, Pallas kernels: 15 us -> 6.34 us  [reply(): pl.pallas_call(reply_kernel, grid_spec=pltpu.PrefetchScalarGridSpec(num_s...]
    pallas_call x1, Pallas kernels: 8.17 us -> 3.55 us  [project(): pl.pallas_call(project_kernel, in_specs=[pl.BlockSpec(memory_space=pltpu....]
    ppermute x5, starting transfers between devices: 9.76 us -> 13.3 us  [other_pair(): return lax.ppermute(values, 'pair', [(0, 1), (1, 0)])]
    pallas_call x1, Pallas kernels: 3.42 us -> 1.4 us  [combine(): pl.pallas_call(combine_kernel, in_specs=[vmem] * 3, out_specs=[vmem] * 4,...]
    ppermute x8, starting transfers between devices: 12 us -> 13.5 us  [flip(): lax.ppermute(values, 'memory', [(m, m ^ bits) for m in range(HOLDERS)])]
  transfers between devices with their start and end apart: 13 -> 13, of which waited for: 8 -> 8; matrix products, arithmetic and copies ran while one was open for 5% -> 2% of each run, Pallas kernels for 20% -> 13%
where the time goes in v2:
time: 108 us; the launch traced here: 107 us
  Pallas kernels  33.8 us (31%)
  waiting for transfers between devices  28.1 us (26%)
  starting transfers between devices  26.8 us (25%)
  local copies, waits for them, and re-layouts  14.6 us (14%)
  other arithmetic  3.25 us (3%)
    pallas_call x2, Pallas kernels, prefix(): pl.pallas_call(partial(prefix_kernel, own), in_specs=[smem] + [vmem] * 5,...  19.6 us
    ppermute x5, waiting for transfers between devices, other_pair(): return lax.ppermute(values, 'pair', [(0, 1), (1, 0)])  16.5 us
    unnamed x40, local copies, waits for them, and re-layouts  13.8 us
    ppermute x8, starting transfers between devices, flip(): lax.ppermute(values, 'memory', [(m, m ^ bits) for m in range(HOLDERS)])  13.5 us
    ppermute x5, starting transfers between devices, other_pair(): return lax.ppermute(values, 'pair', [(0, 1), (1, 0)])  13.3 us
    ppermute x8, waiting for transfers between devices, flip(): lax.ppermute(values, 'memory', [(m, m ^ bits) for m in range(HOLDERS)])  11.6 us
    pallas_call x2, Pallas kernels, reply(): pl.pallas_call(reply_kernel, grid_spec=pltpu.PrefetchScalarGridSpec(num_s...  6.34 us
    pallas_call x1, Pallas kernels, project(): pl.pallas_call(project_kernel, in_specs=[pl.BlockSpec(memory_space=pltpu....  3.55 us
  transfers between devices with their start and end apart: 13, of which 8 were waited for; matrix products, arithmetic and copies ran while one was open for 2% of the time, Pallas kernels for 13%

profile of v2, /device:TPU:1, one launch (start us, length us, event | category | flops | bytes accessed | tf_op | source)
XLA Modules:
  0.0 107.5 jit_solution(17476945010212897968)
XLA Ops:
  0.6 2.1 %multiply_reduce_fusion = f32[256]{0:T(256)S(1)} fusion(bf16[256,4096]{1,0:T(8,128)(2,1)} %hidden_ref.1), kind=kLoop, calls=%fused_computation | loop fusion | flops 3145472 | bytes 2098176 | tf_op jit(solution)/shard_map/reduce_sum | solution.py:491
  2.7 4.5 %collective-permute-start = (f32[256]{0:T(256)S(1)}, f32[256]{0:T(256)S(1)}, u32[]{:S(2)}, u32[]{:S(2)}) collective-permute-start(f32[256]{0:T(256)S(1)} %multiply_reduce_fusion), channel_id=1, source_target_pairs={{0,1},{1,0},{2,3},{3,2},{4,5},{5,4},{6,7},{7,6},{8,9},{9,8},{10,11... | collective-permute-start | bytes 3080 | tf_op jit(solution)/shard_map/ppermute | solution.py:463
  8.6 3.4 %copy-done.3 = bf16[4096,1024]{1,0:T(8,128)(2,1)S(1)} copy-done((bf16[4096,1024]{1,0:T(8,128)(2,1)S(1)}, bf16[4096,1024]{1,0:T(8,128)(2,1)}, u32[]{:S(2)}) %copy-start.3) | copy-done | bytes 8388632
  11.9 1.6 %copy-done.4 = bf16[256,4096]{1,0:T(8,128)(2,1)S(1)} copy-done((bf16[256,4096]{1,0:T(8,128)(2,1)S(1)}, bf16[256,4096]{1,0:T(8,128)(2,1)}, u32[]{:S(2)}) %copy-start.4) | copy-done | bytes 2097176
  16.7 3.5 %shard_map.158 = (f32[128,1280]{1,0:T(8,128)S(1)}, f32[128,1280]{1,0:T(8,128)S(1)}) custom-call(s32[1]{0:T(128)} %bitcast.1.span_ref.parity_ref, f32[2,128]{1,0:T(2,128)S(1)} %bitcast.20, f32[2,128]{1,0:T(2,128)S(1)} %bitcast.21, bf16[256,4096]{1,0:T(8,128)(2,1)S(1)} %copy-done.4, bf16[4096]{0:T(1024)(128)(2,1)S(1)} %copy-done.7, ...), custom_call_target="tpu_custom_call" | custom-call | flops 2684354560 | bytes 14680064 | tf_op jit(solution)/shard_map/pallas_call | solution.py:84
  20.3 2.7 %collective-permute-start.1 = (f32[128,1280]{1,0:T(8,128)S(1)}, f32[128,1280]{1,0:T(8,128)S(1)}, u32[]{:S(2)}, u32[]{:S(2)}) collective-permute-start(f32[128,1280]{1,0:T(8,128)S(1)} %get-tuple-element.26), channel_id=1, source_target_pairs={{0,1},{1,0},{2,3},{3,2},{4,5},{5,4},{6,7},{7,6},{8,9},{9,8},{10,11... | collective-permute-start | bytes 1966088 | tf_op jit(solution)/shard_map/ppermute | solution.py:463
  23.4 13.5 %collective-permute-done.1.came_ref = f32[128,1280]{1,0:T(8,128)S(1)} collective-permute-done((f32[128,1280]{1,0:T(8,128)S(1)}, f32[128,1280]{1,0:T(8,128)S(1)}, u32[]{:S(2)}, u32[]{:S(2)}) %collective-permute-start.1) | collective-permute-done | bytes 655392 | tf_op jit(solution)/shard_map/ppermute | solution.py:463
  39.5 2.6 %collective-permute-start.3 = (bf16[2,24,1408]{2,1,0:T(8,128)(2,1)S(1)}, bf16[2,24,1408]{2,1,0:T(8,128)(2,1)S(1)}, u32[]{:S(2)}, u32[]{:S(2)}) collective-permute-start(bf16[2,24,1408]{2,1,0:T(8,128)(2,1)S(1)} %get-tuple-element.30), channel_id=1, source_target_pairs={{0,8},{2,10},{4,12},{6,14},{8,0},{10,2},{12,4},{14,6},{1,9},{3,11}... | collective-permute-start | bytes 405512 | tf_op jit(solution)/shard_map/ppermute | solution.py:467
  42.2 4.1 %collective-permute-done.3 = bf16[2,24,1408]{2,1,0:T(8,128)(2,1)S(1)} collective-permute-done((bf16[2,24,1408]{2,1,0:T(8,128)(2,1)S(1)}, bf16[2,24,1408]{2,1,0:T(8,128)(2,1)S(1)}, u32[]{:S(2)}, u32[]{:S(2)}) %collective-permute-start.3) | collective-permute-done | bytes 135200 | tf_op jit(solution)/shard_map/ppermute | solution.py:467
  46.3 1.5 %collective-permute-done.4 = bf16[2,24,1408]{2,1,0:T(8,128)(2,1)S(1)} collective-permute-done((bf16[2,24,1408]{2,1,0:T(8,128)(2,1)S(1)}, bf16[2,24,1408]{2,1,0:T(8,128)(2,1)S(1)}, u32[]{:S(2)}, u32[]{:S(2)}) %collective-permute-start.4) | collective-permute-done | bytes 135200 | tf_op jit(solution)/shard_map/ppermute | solution.py:467
  47.9 3.4 %collective-permute-start.5 = (bf16[4,24,1408]{2,1,0:T(8,128)(2,1)S(1)}, bf16[4,24,1408]{2,1,0:T(8,128)(2,1)S(1)}, u32[]{:S(2)}, u32[]{:S(2)}) collective-permute-start(bf16[4,24,1408]{2,1,0:T(8,128)(2,1)S(1)} %pad_maximum_fusion), channel_id=1, source_target_pairs={{0,2},{2,0},{4,6},{6,4},{8,10},{10,8},{12,14},{14,12},{1,3},{3,1},... | collective-permute-start | bytes 811016 | tf_op jit(solution)/shard_map/ppermute | solution.py:467
  52.5 2.6 %collective-permute-start.6 = (bf16[8,24,1152]{2,1,0:T(8,128)(2,1)S(1)}, bf16[8,24,1152]{2,1,0:T(8,128)(2,1)S(1)}, u32[]{:S(2)}, u32[]{:S(2)}) collective-permute-start(bf16[8,24,1152]{2,1,0:T(8,128)(2,1)S(1)} %slice.82), channel_id=1, source_target_pairs={{0,1},{1,0},{2,3},{3,2},{4,5},{5,4},{6,7},{7,6},{8,9},{9,8},{10,11... | collective-permute-start | bytes 1327112 | tf_op jit(solution)/shard_map/ppermute | solution.py:463
  55.9 2.8 %copy-done = bf16[1,192,128,128]{3,2,1,0:T(8,128)(2,1)S(1)} copy-done((bf16[1,192,128,128]{3,2,1,0:T(8,128)(2,1)S(1)}, bf16[1,192,128,128]{3,2,1,0:T(8,128)(2,1)}, u32[]{:S(2)}) %copy-start) | copy-done | bytes 6291480
  58.7 2.8 %copy-done.1 = bf16[1,192,128,128]{3,2,1,0:T(8,128)(2,1)S(1)} copy-done((bf16[1,192,128,128]{3,2,1,0:T(8,128)(2,1)S(1)}, bf16[1,192,128,128]{3,2,1,0:T(8,128)(2,1)}, u32[]{:S(2)}) %copy-start.1) | copy-done | bytes 6291480
  61.4 3.2 %shard_map.160 = (f32[4,24,1024]{2,1,0:T(8,128)S(1)}, f32[4,24,128]{2,1,0:T(8,128)S(1)}) custom-call(s32[4]{0:T(128)S(1)} %add_xor_fusion.where_ref, s32[1]{0:T(128)} %bitcast.1.span_ref.parity_ref, bf16[8,24,1408]{2,1,0:T(8,128)(2,1)S(1)} %slice_dynamic-update-slice_fusion.rows_ref, bf16[8,24,128,128]{3,2,1,0:T(8,128)(2,1)S(1)} %bitcast.14, ...), custom_call_target="tpu_custom_call" | custom-call | flops 2000000000 | bytes 8388608 | tf_op jit(solution)/shard_map/pallas_call | solution.py:220
  64.6 3.0 %collective-permute-done.7.other_ref = bf16[8,24,256]{2,1,0:T(8,128)(2,1)S(1)} collective-permute-done((bf16[8,24,256]{2,1,0:T(8,128)(2,1)S(1)}, bf16[8,24,256]{2,1,0:T(8,128)(2,1)S(1)}, u32[]{:S(2)}, u32[]{:S(2)}) %collective-permute-start.7) | collective-permute-done | bytes 98336 | tf_op jit(solution)/shard_map/ppermute | solution.py:463
  67.7 3.2 %shard_map.161 = (f32[4,24,1024]{2,1,0:T(8,128)S(1)}, f32[4,24,128]{2,1,0:T(8,128)S(1)}) custom-call(s32[4]{0:T(128)S(1)} %add_xor_fusion.where_ref, s32[1]{0:T(128)S(6)} %sub.3.parity_ref, bf16[8,24,1152]{2,1,0:T(8,128)(2,1)S(1)} %collective-permute-done.6.rows_ref, bf16[8,24,128,128]{3,2,1,0:T(8,128)(2,1)S(1)} %bitcast.17, ...), custom_call_target="tpu_custom_call" | custom-call | flops 2000000000 | bytes 8388608 | tf_op jit(solution)/shard_map/pallas_call | solution.py:220
  70.9 9.4 %shard_map.162 = bf16[8,24,1152]{2,1,0:T(8,128)(2,1)S(1)} custom-call(s32[4]{0:T(128)S(1)} %add_xor_fusion.where_ref, bf16[8,24,1152]{2,1,0:T(8,128)(2,1)S(1)} %collective-permute-done.6.rows_ref, bf16[4096,128]{1,0:T(8,128)(2,1)S(1)} %bitcast.24, bf16[4096,128]{1,0:T(8,128)(2,1)S(1)} %bitcast.26, f32[4,24,1024]{2,1,0:T(8,128)S(1)} %get-tuple-element.35.reply_ref, ...), custom_call_target="tpu_custom_call" | custom-call | flops 3221225472 | bytes 4194304 | tf_op jit(solution)/shard_map/pallas_call | solution.py:361
  80.3 2.8 %collective-permute-start.8 = (bf16[8,24,1152]{2,1,0:T(8,128)(2,1)S(1)}, bf16[8,24,1152]{2,1,0:T(8,128)(2,1)S(1)}, u32[]{:S(2)}, u32[]{:S(2)}) collective-permute-start(bf16[8,24,1152]{2,1,0:T(8,128)(2,1)S(1)} %shard_map.162), channel_id=1, source_target_pairs={{0,1},{1,0},{2,3},{3,2},{4,5},{5,4},{6,7},{7,6},{8,9},{9,8},{10,11... | collective-permute-start | bytes 1327112 | tf_op jit(solution)/shard_map/ppermute | solution.py:463
  83.8 10.2 %shard_map.164 = (f32[8,24,1024]{2,1,0:T(8,128)S(1)}, f32[8,24,128]{2,1,0:T(8,128)S(1)}) custom-call(s32[4]{0:T(128)S(1)} %add_xor_fusion.where_ref, bf16[8,24,1408]{2,1,0:T(8,128)(2,1)S(1)} %slice_dynamic-update-slice_fusion.rows_ref, bf16[4096,128]{1,0:T(8,128)(2,1)S(1)} %bitcast.25, bf16[4096,128]{1,0:T(8,128)(2,1)S(1)} %bitcast.27, ...), custom_call_target="tpu_custom_call" | custom-call | flops 3221225472 | bytes 4194304 | tf_op jit(solution)/shard_map/pallas_call | solution.py:361
  95.6 1.9 %collective-permute-start.10 = (bf16[2,24,1024]{2,1,0:T(8,128)(2,1)S(1)}, bf16[2,24,1024]{2,1,0:T(8,128)(2,1)S(1)}, u32[]{:S(2)}, u32[]{:S(2)}) collective-permute-start(bf16[2,24,1024]{2,1,0:T(8,128)(2,1)S(1)} %get-tuple-element.45), channel_id=1, source_target_pairs={{0,8},{2,10},{4,12},{6,14},{8,0},{10,2},{12,4},{14,6},{1,9},{3,11}... | collective-permute-start | bytes 294920 | tf_op jit(solution)/shard_map/ppermute | solution.py:467
  97.5 1.9 %collective-permute-start.11 = (bf16[2,24,1024]{2,1,0:T(8,128)(2,1)S(1)}, bf16[2,24,1024]{2,1,0:T(8,128)(2,1)S(1)}, u32[]{:S(2)}, u32[]{:S(2)}) collective-permute-start(bf16[2,24,1024]{2,1,0:T(8,128)(2,1)S(1)} %get-tuple-element.46), channel_id=1, source_target_pairs={{0,12},{2,14},{4,8},{6,10},{8,4},{10,6},{12,0},{14,2},{1,13},{3,15... | collective-permute-start | bytes 294920 | tf_op jit(solution)/shard_map/ppermute | solution.py:467
  100.9 2.3 %collective-permute-done.11.near3_ref = bf16[2,24,1024]{2,1,0:T(8,128)(2,1)S(1)} collective-permute-done((bf16[2,24,1024]{2,1,0:T(8,128)(2,1)S(1)}, bf16[2,24,1024]{2,1,0:T(8,128)(2,1)S(1)}, u32[]{:S(2)}, u32[]{:S(2)}) %collective-permute-start.11) | collective-permute-done | bytes 98336 | tf_op jit(solution)/shard_map/ppermute | solution.py:467
  103.2 2.2 %collective-permute-start.12 = (bf16[4,24,1024]{2,1,0:T(8,128)(2,1)S(1)}, bf16[4,24,1024]{2,1,0:T(8,128)(2,1)S(1)}, u32[]{:S(2)}, u32[]{:S(2)}) collective-permute-start(bf16[4,24,1024]{2,1,0:T(8,128)(2,1)S(1)} %pad_maximum_fusion.1), channel_id=1, source_target_pairs={{0,2},{2,0},{4,6},{6,4},{8,10},{10,8},{12,14},{14,12},{1,3},{3,1},... | collective-permute-start | bytes 589832 | tf_op jit(solution)/shard_map/ppermute | solution.py:467
  (73 shorter events, 15.4 us)
Async XLA Ops:
  2.7 5.8 %collective-permute-start = (f32[256]{0:T(256)S(1)}, f32[256]{0:T(256)S(1)}, u32[]{:S(2)}, u32[]{:S(2)}) collective-permute-start(f32[256]{0:T(256)S(1)} %multiply_reduce_fusion), channel_id=1, source_target_pairs={{0,1},{1,0},{2,3},{3,2},{4,5},{5,4},{6,7},{7,6},{8,9},{9,8},{10,11... | collective-permute-start | bytes 3080 | tf_op jit(solution)/shard_map/ppermute | solution.py:463
  8.6 3.4 %copy-start.3 = (bf16[4096,1024]{1,0:T(8,128)(2,1)S(1)}, bf16[4096,1024]{1,0:T(8,128)(2,1)}, u32[]{:S(2)}) copy-start(bf16[4096,1024]{1,0:T(8,128)(2,1)} %wq_ref.1) | copy-start | bytes 25165828
  16.7 6.7 %copy-start.13 = (bf16[128]{0:T(256)(128)(2,1)S(1)}, bf16[128]{0:T(256)(128)(2,1)}, u32[]{:S(2)}) copy-start(bf16[128]{0:T(256)(128)(2,1)} %param.22) | copy-start | bytes 772
  16.7 6.7 %copy-start.14 = (bf16[128]{0:T(256)(128)(2,1)S(1)}, bf16[128]{0:T(256)(128)(2,1)}, u32[]{:S(2)}) copy-start(bf16[128]{0:T(256)(128)(2,1)} %param.21) | copy-start | bytes 772
  16.7 20.2 %copy-start.8 = (s32[8]{0:T(128)S(1)}, s32[8]{0:T(128)}, u32[]{:S(2)}) copy-start(s32[8]{0:T(128)} %home_ref.1) | copy-start | bytes 100
  16.7 20.2 %copy-start.9 = (s32[128]{0:T(128)S(1)}, s32[128]{0:T(128)}, u32[]{:S(2)}) copy-start(s32[128]{0:T(128)} %param.27) | copy-start | bytes 1540
  16.7 20.2 %copy-start.10 = (s32[128]{0:T(128)S(1)}, s32[128]{0:T(128)}, u32[]{:S(2)}) copy-start(s32[128]{0:T(128)} %param.28) | copy-start | bytes 1540
  20.3 16.7 %collective-permute-start.1 = (f32[128,1280]{1,0:T(8,128)S(1)}, f32[128,1280]{1,0:T(8,128)S(1)}, u32[]{:S(2)}, u32[]{:S(2)}) collective-permute-start(f32[128,1280]{1,0:T(8,128)S(1)} %get-tuple-element.26), channel_id=1, source_target_pairs={{0,1},{1,0},{2,3},{3,2},{4,5},{5,4},{6,7},{7,6},{8,9},{9,8},{10,11... | collective-permute-start | bytes 1966088 | tf_op jit(solution)/shard_map/ppermute | solution.py:463
  36.9 30.7 %slice-start = ((s8[6291456]{0:T(1024)(128)(4,1)}), s8[2097152]{0:T(1024)(128)(4,1)S(1)}, s32[]{:S(2)}) async-start(s8[6291456]{0:T(1024)(128)(4,1)} %bitcast.15), calls=%async_computation | async-start | bytes 4194304
  38.2 4.0 %collective-permute-start.2 = (bf16[2,24,1408]{2,1,0:T(8,128)(2,1)S(1)}, bf16[2,24,1408]{2,1,0:T(8,128)(2,1)S(1)}, u32[]{:S(2)}, u32[]{:S(2)}) collective-permute-start(bf16[2,24,1408]{2,1,0:T(8,128)(2,1)S(1)} %get-tuple-element.29), channel_id=1, source_target_pairs={{0,4},{2,6},{4,0},{6,2},{8,12},{10,14},{12,8},{14,10},{1,5},{3,7},... | collective-permute-start | bytes 405512 | tf_op jit(solution)/shard_map/ppermute | solution.py:467
  39.5 6.8 %collective-permute-start.3 = (bf16[2,24,1408]{2,1,0:T(8,128)(2,1)S(1)}, bf16[2,24,1408]{2,1,0:T(8,128)(2,1)S(1)}, u32[]{:S(2)}, u32[]{:S(2)}) collective-permute-start(bf16[2,24,1408]{2,1,0:T(8,128)(2,1)S(1)} %get-tuple-element.30), channel_id=1, source_target_pairs={{0,8},{2,10},{4,12},{6,14},{8,0},{10,2},{12,4},{14,6},{1,9},{3,11}... | collective-permute-start | bytes 405512 | tf_op jit(solution)/shard_map/ppermute | solution.py:467
  42.2 5.6 %collective-permute-start.4 = (bf16[2,24,1408]{2,1,0:T(8,128)(2,1)S(1)}, bf16[2,24,1408]{2,1,0:T(8,128)(2,1)S(1)}, u32[]{:S(2)}, u32[]{:S(2)}) collective-permute-start(bf16[2,24,1408]{2,1,0:T(8,128)(2,1)S(1)} %get-tuple-element.31), channel_id=1, source_target_pairs={{0,12},{2,14},{4,8},{6,10},{8,4},{10,6},{12,0},{14,2},{1,13},{3,15... | collective-permute-start | bytes 405512 | tf_op jit(solution)/shard_map/ppermute | solution.py:467
  47.9 4.5 %collective-permute-start.5 = (bf16[4,24,1408]{2,1,0:T(8,128)(2,1)S(1)}, bf16[4,24,1408]{2,1,0:T(8,128)(2,1)S(1)}, u32[]{:S(2)}, u32[]{:S(2)}) collective-permute-start(bf16[4,24,1408]{2,1,0:T(8,128)(2,1)S(1)} %pad_maximum_fusion), channel_id=1, source_target_pairs={{0,2},{2,0},{4,6},{6,4},{8,10},{10,8},{12,14},{14,12},{1,3},{3,1},... | collective-permute-start | bytes 811016 | tf_op jit(solution)/shard_map/ppermute | solution.py:467
  52.5 15.1 %collective-permute-start.6 = (bf16[8,24,1152]{2,1,0:T(8,128)(2,1)S(1)}, bf16[8,24,1152]{2,1,0:T(8,128)(2,1)S(1)}, u32[]{:S(2)}, u32[]{:S(2)}) collective-permute-start(bf16[8,24,1152]{2,1,0:T(8,128)(2,1)S(1)} %slice.82), channel_id=1, source_target_pairs={{0,1},{1,0},{2,3},{3,2},{4,5},{5,4},{6,7},{7,6},{8,9},{9,8},{10,11... | collective-permute-start | bytes 1327112 | tf_op jit(solution)/shard_map/ppermute | solution.py:463
  55.2 12.5 %collective-permute-start.7 = (bf16[8,24,256]{2,1,0:T(8,128)(2,1)S(1)}, bf16[8,24,256]{2,1,0:T(8,128)(2,1)S(1)}, u32[]{:S(2)}, u32[]{:S(2)}) collective-permute-start(bf16[8,24,256]{2,1,0:T(8,128)(2,1)S(1)} %slice.83.own_ref), channel_id=1, source_target_pairs={{0,1},{1,0},{2,3},{3,2},{4,5},{5,4},{6,7},{7,6},{8,9},{9,8},{10,11... | collective-permute-start | bytes 294920 | tf_op jit(solution)/shard_map/ppermute | solution.py:463
  61.4 6.2 %slice-start.1 = ((s8[6291456]{0:T(1024)(128)(4,1)}), s8[4194304]{0:T(1024)(128)(4,1)S(1)}, s32[]{:S(2)}) async-start(s8[6291456]{0:T(1024)(128)(4,1)} %bitcast.15), calls=%async_computation.1 | async-start | bytes 8388608
  61.4 6.2 %copy-start.2 = (bf16[1,192,128,128]{3,2,1,0:T(8,128)(2,1)S(1)}, bf16[1,192,128,128]{3,2,1,0:T(8,128)(2,1)}, u32[]{:S(2)}) copy-start(bf16[1,192,128,128]{3,2,1,0:T(8,128)(2,1)} %param.26) | copy-start | bytes 18874372
  67.6 3.2 %copy-start.11 = (bf16[1,4096,128]{2,1,0:T(8,128)(2,1)S(1)}, bf16[1,4096,128]{2,1,0:T(8,128)(2,1)}, u32[]{:S(2)}) copy-start(bf16[1,4096,128]{2,1,0:T(8,128)(2,1)} %param.23) | copy-start | bytes 3145732
  67.7 3.2 %copy-start.12 = (bf16[1,4096,128]{2,1,0:T(8,128)(2,1)S(1)}, bf16[1,4096,128]{2,1,0:T(8,128)(2,1)}, u32[]{:S(2)}) copy-start(bf16[1,4096,128]{2,1,0:T(8,128)(2,1)} %param.24) | copy-start | bytes 3145732
  80.3 13.8 %collective-permute-start.8 = (bf16[8,24,1152]{2,1,0:T(8,128)(2,1)S(1)}, bf16[8,24,1152]{2,1,0:T(8,128)(2,1)S(1)}, u32[]{:S(2)}, u32[]{:S(2)}) collective-permute-start(bf16[8,24,1152]{2,1,0:T(8,128)(2,1)S(1)} %shard_map.162), channel_id=1, source_target_pairs={{0,1},{1,0},{2,3},{3,2},{4,5},{5,4},{6,7},{7,6},{8,9},{9,8},{10,11... | collective-permute-start | bytes 1327112 | tf_op jit(solution)/shard_map/ppermute | solution.py:463
  95.5 3.9 %collective-permute-start.9 = (bf16[2,24,1024]{2,1,0:T(8,128)(2,1)S(1)}, bf16[2,24,1024]{2,1,0:T(8,128)(2,1)S(1)}, u32[]{:S(2)}, u32[]{:S(2)}) collective-permute-start(bf16[2,24,1024]{2,1,0:T(8,128)(2,1)S(1)} %get-tuple-element.44), channel_id=1, source_target_pairs={{0,4},{2,6},{4,0},{6,2},{8,12},{10,14},{12,8},{14,10},{1,5},{3,7},... | collective-permute-start | bytes 294920 | tf_op jit(solution)/shard_map/ppermute | solution.py:467
  95.6 5.3 %collective-permute-start.10 = (bf16[2,24,1024]{2,1,0:T(8,128)(2,1)S(1)}, bf16[2,24,1024]{2,1,0:T(8,128)(2,1)S(1)}, u32[]{:S(2)}, u32[]{:S(2)}) collective-permute-start(bf16[2,24,1024]{2,1,0:T(8,128)(2,1)S(1)} %get-tuple-element.45), channel_id=1, source_target_pairs={{0,8},{2,10},{4,12},{6,14},{8,0},{10,2},{12,4},{14,6},{1,9},{3,11}... | collective-permute-start | bytes 294920 | tf_op jit(solution)/shard_map/ppermute | solution.py:467
  97.5 5.7 %collective-permute-start.11 = (bf16[2,24,1024]{2,1,0:T(8,128)(2,1)S(1)}, bf16[2,24,1024]{2,1,0:T(8,128)(2,1)S(1)}, u32[]{:S(2)}, u32[]{:S(2)}) collective-permute-start(bf16[2,24,1024]{2,1,0:T(8,128)(2,1)S(1)} %get-tuple-element.46), channel_id=1, source_target_pairs={{0,12},{2,14},{4,8},{6,10},{8,4},{10,6},{12,0},{14,2},{1,13},{3,15... | collective-permute-start | bytes 294920 | tf_op jit(solution)/shard_map/ppermute | solution.py:467
  103.2 3.3 %collective-permute-start.12 = (bf16[4,24,1024]{2,1,0:T(8,128)(2,1)S(1)}, bf16[4,24,1024]{2,1,0:T(8,128)(2,1)S(1)}, u32[]{:S(2)}, u32[]{:S(2)}) collective-permute-start(bf16[4,24,1024]{2,1,0:T(8,128)(2,1)S(1)} %pad_maximum_fusion.1), channel_id=1, source_target_pairs={{0,2},{2,0},{4,6},{6,4},{8,10},{10,8},{12,14},{14,12},{1,3},{3,1},... | collective-permute-start | bytes 589832 | tf_op jit(solution)/shard_map/ppermute | solution.py:467
  (6 other events, 10.3 us)

commit v3 on v2

--- a/solution.py
+++ b/solution.py
@@ -20,6 +20,8 @@
 QW = HEADS * HD
 SLOTS = HOLDERS * CAP
 BLOCK = 256
+PIECES = 8
+CUT = 768
 LENGTH_AT = QW
 KEY_AT = QW + HD
 VALUE_AT = QW + 2 * HD
@@ -54,40 +56,81 @@
     wk_ref,
     wv_ref,
     keep_ref,
-    send_ref,
+    send0_ref,
+    send1_ref,
+    rows_ref,
+    query_ref,
+    key_ref,
+    value_ref,
     normed_ref,
+    sems,
 ):
+    depth = rows_ref.shape[1]
+    step = depth // PIECES
+    copies = [pltpu.make_async_copy(hidden_ref, rows_ref, sems.at[0])]
+    for piece in range(PIECES):
+        part = pl.ds(piece * step, step)
+        copies.append(
+            pltpu.make_async_copy(wq_ref.at[part], query_ref.at[part], sems.at[1 + piece])
+        )
+    copies.append(pltpu.make_async_copy(wk_ref, key_ref, sems.at[1 + PIECES]))
+    copies.append(pltpu.make_async_copy(wv_ref, value_ref, sems.at[2 + PIECES]))
+    for copy in copies:
+        copy.start()
     span = span_ref[0]
     inverse = lax.rsqrt((mine_ref[...] + theirs_ref[...]) / D + EPSILON)
     first = to_column(inverse[0:1, :])
     second = to_column(inverse[1:2, :])
     scales = (jnp.where(span == 0, first, second), jnp.where(span == 0, second, first))
     gain = gain_ref[...].astype(F32).reshape(1, -1)
+    copies[0].wait()
     for where, start in enumerate((span * ROWS, (1 - span) * ROWS)):
-        rows = hidden_ref[pl.ds(pl.multiple_of(start, ROWS), ROWS), :].astype(F32)
+        rows = rows_ref[pl.ds(pl.multiple_of(start, ROWS), ROWS), :].astype(F32)
         normed = rows * scales[where] * gain
         normed_ref[where * ROWS : (where + 1) * ROWS, :] = normed.astype(BF16)
-    pieces = [(at, wq_ref.at[:, at : at + 256]) for at in range(0, QW, 256)]
-    pieces += [(QW, wk_ref), (QW + HD, wv_ref)]
-    for at, w_ref in pieces:
-        part = slice(at, at + w_ref.shape[1])
+
+    def add(at, total, fresh):
+        width = total.shape[1]
+        send_ref, here = (send0_ref, at) if at < CUT else (send1_ref, at - CUT)
+        for out_ref, rows, column in ((keep_ref, total[:ROWS], at), (send_ref, total[ROWS:], here)):
+            part = slice(column, column + width)
+            out_ref[:, part] = rows if fresh else out_ref[:, part] + rows
+
+    for piece in range(PIECES):
+        copies[1 + piece].wait()
+        part = slice(piece * step, (piece + 1) * step)
+        for at in range(0, QW, 256):
+            weights = query_ref[part, at : at + 256]
+            add(at, jnp.dot(normed_ref[:, part], weights, preferred_element_type=F32), piece == 0)
+    for index, w_ref in enumerate((key_ref, value_ref)):
+        copies[1 + PIECES + index].wait()
         total = jnp.dot(normed_ref[...], w_ref[...], preferred_element_type=F32)
-        keep_ref[:, part] = total[:ROWS]
-        send_ref[:, part] = total[ROWS:]
+        add(QW + index * HD, total, True)
 
 
 def project(span, mine, theirs, hidden, gain, w_query, w_key, w_value):
     depth = hidden.shape[1]
     width = QW + 2 * HD
-    out = jax.ShapeDtypeStruct((ROWS, width), F32)
     vmem = pl.BlockSpec(memory_space=pltpu.VMEM)
+    hbm = pl.BlockSpec(memory_space=pltpu.HBM)
     return pl.pallas_call(
         project_kernel,
-        in_specs=[pl.BlockSpec(memory_space=pltpu.SMEM)] + [vmem] * 7,
-        out_specs=[vmem] * 2,
-        out_shape=[out, out],
-        scratch_shapes=[pltpu.VMEM((2 * ROWS, depth), BF16)],
-        compiler_params=params(20),
+        in_specs=[pl.BlockSpec(memory_space=pltpu.SMEM), vmem, vmem, hbm, vmem, hbm, hbm, hbm],
+        out_specs=[vmem] * 3,
+        out_shape=[
+            jax.ShapeDtypeStruct((ROWS, width), F32),
+            jax.ShapeDtypeStruct((ROWS, CUT), F32),
+            jax.ShapeDtypeStruct((ROWS, width - CUT), F32),
+        ],
+        scratch_shapes=[
+            pltpu.VMEM((2 * ROWS, depth), BF16),
+            pltpu.VMEM((depth, QW), BF16),
+            pltpu.VMEM((depth, HD), BF16),
+            pltpu.VMEM((depth, HD), BF16),
+            pltpu.VMEM((2 * ROWS, depth), BF16),
+            pltpu.SemaphoreType.DMA((3 + PIECES,)),
+        ],
+        compiler_params=params(56),
         cost_estimate=pl.CostEstimate(
             flops=2 * 2 * ROWS * depth * width, bytes_accessed=14 * 2**20, transcendentals=0
         ),
@@ -98,7 +141,8 @@
     home_ref,
     me_ref,
     keep_ref,
-    came_ref,
+    came0_ref,
+    came1_ref,
     bias_ref,
     cos_ref,
     sin_ref,
@@ -136,7 +180,8 @@
         else:
             source = at if head < HEADS else at - HD
             part = slice(source, source + HD)
-            total = keep_ref[:, part] + came_ref[:, part] + bias_ref[:, part]
+            came_ref, here = (came0_ref, source) if source < CUT else (came1_ref, source - CUT)
+            total = keep_ref[:, part] + came_ref[:, here : here + HD] + bias_ref[:, part]
             if head < HEADS + 2:
                 half = HD // 2
                 swapped = jnp.concatenate([total[:, half:], total[:, :half]], axis=1)
@@ -148,27 +193,27 @@
             out_ref[:, :, at : at + HD] = placed[2 * index : 2 * index + 2].astype(BF16)
 
 
-def spread(home, me, keep, came, bias, cosine, sine, lengths, ids):
+def spread(home, me, keep, came0, came1, bias, cosine, sine, lengths, ids):
     block = jax.ShapeDtypeStruct((2, CAP, ROW_WIDTH), BF16)
     smem = pl.BlockSpec(memory_space=pltpu.SMEM)
     vmem = pl.BlockSpec(memory_space=pltpu.VMEM)
     return pl.pallas_call(
         spread_kernel,
-        in_specs=[smem, smem] + [vmem] * 7,
+        in_specs=[smem, smem] + [vmem] * 8,
         out_specs=[vmem] * 5,
         out_shape=[block] * 4 + [jax.ShapeDtypeStruct((1, ROWS), jnp.int32)],
         compiler_params=params(8),
         cost_estimate=pl.CostEstimate(
             flops=2 * SLOTS * ROWS * ROW_WIDTH, bytes_accessed=2 * 2**20, transcendentals=0
         ),
-    )(home, me, keep, came, bias, cosine, sine, lengths, ids)
+    )(home, me, keep, came0, came1, bias, cosine, sine, lengths, ids)
 
 
 NT = (((1,), (1,)), ((), ()))
 
 
-def reply_kernel(where_ref, parity_ref, rows_ref, keys_ref, values_ref, out_ref, log_ref, wide_ref):
-    wide_ref[...] = rows_ref[0, :, 0:KEY_AT].astype(F32)
+def attend_replies(rows_ref, keys_ref, values_ref, out_ref, log_ref, wide_ref):
+    wide_ref[...] = rows_ref[:, 0:KEY_AT].astype(F32)
     group = 8
     parts = CAP // group
     lanes = lane_ids((group, HD))
@@ -179,7 +224,7 @@
         stacked = jnp.concatenate(
             [wide_ref[slots, head * HD : (head + 1) * HD] for head in range(HEADS)], axis=0
         ).astype(BF16)
-        keys = keys_ref[0, slots].reshape(group * HD, HD)
+        keys = keys_ref[slots].reshape(group * HD, HD)
         scores.append(lax.dot_general(stacked, keys, NT, preferred_element_type=F32))
     weights = []
     totals = []
@@ -200,7 +245,7 @@
         logs = jnp.zeros((group, HD), F32)
         for head in range(HEADS):
             logs = jnp.where(lanes == head, log[head * group : (head + 1) * group], logs)
-        log_ref[0, slots, :] = logs
+        log_ref[slots, :] = logs
         weights.append(
             jnp.concatenate(
                 [jnp.where(line == slot, weight, 0.0).astype(BF16) for slot in range(group)], axis=1
@@ -208,10 +253,16 @@
         )
     for part in range(parts):
         slots = slice(part * group, (part + 1) * group)
-        values = values_ref[0, slots].reshape(group * HD, HD)
+        values = values_ref[slots].reshape(group * HD, HD)
         mixed = jnp.dot(weights[part], values, preferred_element_type=F32) / totals[part]
         for head in range(HEADS):
-            out_ref[0, slots, head * HD : (head + 1) * HD] = mixed[head * group : (head + 1) * group]
+            out_ref[slots, head * HD : (head + 1) * HD] = mixed[head * group : (head + 1) * group]
+
+
+def reply_kernel(where_ref, parity_ref, rows_ref, keys_ref, values_ref, out_ref, log_ref, wide_ref):
+    attend_replies(
+        rows_ref.at[0], keys_ref.at[0], values_ref.at[0], out_ref.at[0], log_ref.at[0], wide_ref
+    )
 
 
 def reply(where, parity, rows, keys, values):
@@ -261,20 +312,12 @@
         )
 
 
-def prefix_kernel(
-    own,
-    where_ref,
-    rows_ref,
-    keys_ref,
-    values_ref,
-    reply_ref,
-    reply_log_ref,
-    *refs,
-):
+def prefix_kernel(own, where_ref, rows_ref, keys_ref, values_ref, *refs):
     if own:
-        out_ref, log_ref, *scratch = refs
+        reply_ref, reply_log_ref, out_ref, log_ref, *scratch = refs
     else:
-        sent_ref, *scratch, out_ref, log_ref = refs
+        parity_ref, cached_keys_ref, cached_values_ref, fresh_ref, sent_ref, *refs = refs
+        *scratch, out_ref, log_ref, reply_ref, reply_log_ref, wide_ref = refs
     query_ref, score0_ref, score1_ref, mixed_ref, logs_ref = scratch
     for head in range(HEADS):
         rows = rows_ref[:, :, head * HD : (head + 1) * HD].astype(F32)
@@ -295,6 +338,16 @@
         highest = jnp.max(scores, axis=1, keepdims=True)
         if block + 1 < total_rows // BLOCK:
             score(block + 1)
+        if not own and block < reply_ref.shape[0]:
+            cached = 2 * block + parity_ref[0]
+            attend_replies(
+                rows_ref.at[where_ref[block]],
+                cached_keys_ref.at[cached],
+                cached_values_ref.at[cached],
+                reply_ref.at[block],
+                reply_log_ref.at[block],
+                wide_ref.at[block],
+            )
         weights = jnp.exp2((scores - highest) * SCALE)
         total = jnp.sum(weights, axis=1, keepdims=True)
         mixed = jnp.dot(weights.astype(BF16), values_ref[...], preferred_element_type=F32)
@@ -337,10 +390,11 @@
             here = (block_lanes >= 8 * index) & (block_lanes < 8 * index + 8)
             packed = jnp.where(here, moved, packed)
         sent_ref[:, :, 0:QW] = out_ref[...].astype(BF16)
-        sent_ref[:, :, QW:] = packed.astype(BF16)
-
-
-def prefix(own, where, rows, keys, values, reply_out, reply_log):
+        sent_ref[:, :, QW : QW + HD] = packed.astype(BF16)
+        sent_ref[:, :, QW + HD :] = fresh_ref[...]
+
+
+def prefix(own, where, rows, keys, values, *others):
     smem = pl.BlockSpec(memory_space=pltpu.SMEM)
     vmem = pl.BlockSpec(memory_space=pltpu.VMEM)
     out = (HOLDERS, CAP, QW)
@@ -355,12 +409,14 @@
     if own:
         out_shape = [jax.ShapeDtypeStruct(out, F32), jax.ShapeDtypeStruct(log, F32)]
     else:
-        out_shape = [jax.ShapeDtypeStruct((HOLDERS, CAP, QW + HD), BF16)]
+        out_shape = [jax.ShapeDtypeStruct((HOLDERS, CAP, ROW_WIDTH), BF16)]
         scratch += [pltpu.VMEM(out, F32), pltpu.VMEM(log, F32)]
+        scratch += [pltpu.VMEM((4, CAP, QW), F32), pltpu.VMEM((4, CAP, HD), F32)]
+        scratch += [pltpu.VMEM((4, CAP, KEY_AT), F32)]
     work = HEADS * SLOTS * keys.shape[0]
     return pl.pallas_call(
         partial(prefix_kernel, own),
-        in_specs=[smem] + [vmem] * 5,
+        in_specs=[smem] + [vmem] * 3 + [vmem if own else smem] + [vmem] * (len(others) - 1),
         out_specs=[vmem] * len(out_shape),
         out_shape=out_shape,
         scratch_shapes=scratch,
@@ -368,12 +424,12 @@
         cost_estimate=pl.CostEstimate(
             flops=4 * work * HD, bytes_accessed=4 * 2**20, transcendentals=work
         ),
-    )(where, rows, keys, values, reply_out, reply_log)
+    )(where, rows, keys, values, *others)
 
 
 def combine_kernel(out_ref, log_ref, came_ref, out0_ref, out1_ref, out2_ref, out3_ref):
     for block in range(HOLDERS):
-        packed = came_ref[block, :, QW:].astype(F32)
+        packed = came_ref[block, :, QW : QW + HD].astype(F32)
         came_log = packed
         for index in (1, 2):
             came_log = came_log + jnp.concatenate(
@@ -490,7 +546,7 @@
     widened = hidden.astype(F32)
     squares = jnp.sum(widened * widened, axis=1)
     theirs = other_pair(squares)
-    keep, send = project(
+    keep, send0, send1 = project(
         span,
         squares.reshape(2, ROWS),
         theirs.reshape(2, ROWS),
@@ -500,7 +556,8 @@
         w_key,
         w_value,
     )
-    came = other_pair(send)
+    came0 = other_pair(send0)
+    came1 = other_pair(send1)
 
     half = HD // 2
     ladder = jnp.arange(half, dtype=F32) * (2.0 / HD)
@@ -512,15 +569,17 @@
     sine = jnp.concatenate([-sine, sine], axis=1)
     bias = jnp.concatenate([query_bias, key_bias, value_bias]).astype(F32).reshape(1, -1)
     *blocks, target = spread(
-        prompt_home, me, keep, came, bias, cosine, sine, reply_length.reshape(1, ROWS), prefix_ids.reshape(1, ROWS)
+        prompt_home, me, keep, came0, came1, bias, cosine, sine, reply_length.reshape(1, ROWS), prefix_ids.reshape(1, ROWS)
     )
 
-    near = [blocks[0]] + [flip(blocks[step], 2 * step) for step in range(1, 4)]
+    near = {0: blocks[0]}
+    for step in (2, 1, 3):
+        near[step] = flip(blocks[step], 2 * step)
+    near = [near[step] for step in range(4)]
     far = flip(jnp.stack([block[1] for block in near]), 1)
     rows = jnp.stack([piece for step in range(4) for piece in (near[step][0], far[step])])
     partner_rows = other_pair(rows[:, :, :KEY_AT])
     fresh = rows[:, :, KEY_AT:]
-    partner_fresh = other_pair(fresh)
 
     origin = 4 * span[0] + jnp.arange(4, dtype=jnp.int32)
     where = me[0] ^ origin
@@ -530,20 +589,30 @@
     prompt_keys = prefix_keys[0]
     prompt_values = prefix_values[0]
     own_reply = reply(where, span, rows, keys, values)
-    own_reply, partner_rows, partner_fresh = lax.optimization_barrier(
-        (own_reply, partner_rows, partner_fresh)
+    own_reply, partner_rows = lax.optimization_barrier((own_reply, partner_rows))
+    (sent,) = prefix(
+        False,
+        where,
+        partner_rows,
+        prompt_keys,
+        prompt_values,
+        1 - span,
+        keys,
+        values,
+        fresh,
     )
-    stored = store(me, span, fresh, partner_fresh).reshape(2, 1, 2 * SLOTS, HD)
-    partner_reply = reply(where, 1 - span, partner_rows, keys, values)
-    (sent,) = prefix(False, where, partner_rows, prompt_keys, prompt_values, *partner_reply)
     came = other_pair(sent)
-    rows, sent, stored = lax.optimization_barrier((rows, sent, stored))
+    rows, sent = lax.optimization_barrier((rows, sent))
     out, log = prefix(True, where, rows, prompt_keys, prompt_values, *own_reply)
     merged = combine(out, log, came)
 
-    nears = [merged[0]] + [flip(merged[step], 2 * step) for step in range(1, 4)]
+    nears = {0: merged[0]}
+    for step in (2, 1, 3):
+        nears[step] = flip(merged[step], 2 * step)
+    nears = [nears[step] for step in range(4)]
     fars = flip(jnp.stack([block[1] for block in nears]), 1)
     attention = unplace(target, nears, fars)
+    stored = store(me, span, fresh, came[:, :, QW + HD :]).reshape(2, 1, 2 * SLOTS, HD)
     return attention, stored
 
 

time: 108 us -> 104 us (0.963)
  local copies, waits for them, and re-layouts: 14.6 us -> 7.7 us
  Pallas kernels: 33.8 us -> 37.2 us
  waiting for transfers between devices: 28.1 us -> 26.3 us
  starting transfers between devices: 26.8 us -> 28.4 us
    unnamed x40 -> x38, local copies, waits for them, and re-layouts: 13.8 us -> 7.58 us
    pallas_call x1, Pallas kernels: 3.55 us -> 8.26 us  [project(): pl.pallas_call(project_kernel, in_specs=[pl.BlockSpec(memory_space=pltpu....]
    pallas_call x2 -> x1, Pallas kernels: 6.34 us -> 3.16 us  [reply(): pl.pallas_call(reply_kernel, grid_spec=pltpu.PrefetchScalarGridSpec(num_s...]
    pallas_call x3, Pallas kernels: 20.9 us -> 22.7 us  [the longest x2 21.5 us: prefix(): pl.pallas_call(partial(prefix_kernel, own), in_specs=[smem] + [vmem] * 3...]
  transfers between devices with their start and end apart: 13 -> 13, of which waited for: 8 -> 10; matrix products, arithmetic and copies ran while one was open for 2% -> 1% of each run, Pallas kernels for 13% -> 14%
where the time goes in v3:
time: 104 us
  Pallas kernels  37.2 us (36%)
  starting transfers between devices  28.4 us (27%)
  waiting for transfers between devices  26.3 us (25%)
  local copies, waits for them, and re-layouts  7.7 us (7%)
  other arithmetic  3.24 us (3%)
    pallas_call x2, Pallas kernels, prefix(): pl.pallas_call(partial(prefix_kernel, own), in_specs=[smem] + [vmem] * 3...  21.5 us
    ppermute x5, waiting for transfers between devices, other_pair(): return lax.ppermute(values, 'pair', [(0, 1), (1, 0)])  15.6 us
    ppermute x8, starting transfers between devices, flip(): lax.ppermute(values, 'memory', [(m, m ^ bits) for m in range(HOLDERS)])  14.5 us
    ppermute x5, starting transfers between devices, other_pair(): return lax.ppermute(values, 'pair', [(0, 1), (1, 0)])  13.9 us
    ppermute x8, waiting for transfers between devices, flip(): lax.ppermute(values, 'memory', [(m, m ^ bits) for m in range(HOLDERS)])  10.7 us
    pallas_call x1, Pallas kernels, project(): pl.pallas_call(project_kernel, in_specs=[pl.BlockSpec(memory_space=pltpu....  8.26 us
    unnamed x38, local copies, waits for them, and re-layouts  7.58 us
    pallas_call x1, Pallas kernels, reply(): pl.pallas_call(reply_kernel, grid_spec=pltpu.PrefetchScalarGridSpec(num_s...  3.16 us
  transfers between devices with their start and end apart: 13, of which 10 were waited for; matrix products, arithmetic and copies ran while one was open for 1% of the time, Pallas kernels for 14%

profile of v3, /device:TPU:1, one launch (start us, length us, event | category | flops | bytes accessed | tf_op | source)
XLA Modules:
  0.0 103.7 jit_solution(9371509046257745123)
XLA Ops:
  0.6 2.1 %multiply_reduce_fusion = f32[256]{0:T(256)S(1)} fusion(bf16[256,4096]{1,0:T(8,128)(2,1)} %hidden_ref.1), kind=kLoop, calls=%fused_computation | loop fusion | flops 3145472 | bytes 2098176 | tf_op jit(solution)/shard_map/reduce_sum | solution.py:547
  2.7 4.5 %collective-permute-start = (f32[256]{0:T(256)S(1)}, f32[256]{0:T(256)S(1)}, u32[]{:S(2)}, u32[]{:S(2)}) collective-permute-start(f32[256]{0:T(256)S(1)} %multiply_reduce_fusion), channel_id=1, source_target_pairs={{0,1},{1,0},{2,3},{3,2},{4,5},{5,4},{6,7},{7,6},{8,9},{9,8},{10,11... | collective-permute-start | bytes 3080 | tf_op jit(solution)/shard_map/ppermute | solution.py:519
  8.8 8.3 %shard_map.158 = (f32[128,1280]{1,0:T(8,128)}, f32[128,768]{1,0:T(8,128)}, f32[128,512]{1,0:T(8,128)}) custom-call(s32[1]{0:T(128)} %bitcast.1.span_ref.parity_ref, f32[2,128]{1,0:T(2,128)} %bitcast.28, f32[2,128]{1,0:T(2,128)} %bitcast.29, bf16[256,4096]{1,0:T(8,128)(2,1)} %hidden_ref.1, bf16[4096]{0:T(1024)(128)(2,1)} %gain_ref.1, ...), custom_call_target="tpu_custom_call" | custom-call | flops 2684354560 | bytes 14680064 | tf_op jit(solution)/shard_map/pallas_call | solution.py:116
  17.1 3.0 %collective-permute-start.1 = (f32[128,768]{1,0:T(8,128)}, f32[128,768]{1,0:T(8,128)S(1)}, u32[]{:S(2)}, u32[]{:S(2)}) collective-permute-start(f32[128,768]{1,0:T(8,128)} %get-tuple-element.23), channel_id=1, source_target_pairs={{0,1},{1,0},{2,3},{3,2},{4,5},{5,4},{6,7},{7,6},{8,9},{9,8},{10,11... | collective-permute-start | bytes 1179656 | tf_op jit(solution)/shard_map/ppermute | solution.py:519
  20.7 12.8 %collective-permute-done.2.came1_ref = f32[128,512]{1,0:T(8,128)S(1)} collective-permute-done((f32[128,512]{1,0:T(8,128)}, f32[128,512]{1,0:T(8,128)S(1)}, u32[]{:S(2)}, u32[]{:S(2)}) %collective-permute-start.2) | collective-permute-done | bytes 262176 | tf_op jit(solution)/shard_map/ppermute | solution.py:519
  34.7 1.2 %shard_map.159 = (bf16[2,24,1408]{2,1,0:T(8,128)(2,1)S(1)}, bf16[2,24,1408]{2,1,0:T(8,128)(2,1)S(1)}, bf16[2,24,1408]{2,1,0:T(8,128)(2,1)S(1)}, bf16[2,24,1408]{2,1,0:T(8,128)(2,1)S(1)}, s32[1,128]{1,0:T(1,128)S(1)}) custom-call(s32[8]{0:T(128)S(1)} %copy-done.6, s32[1]{0:T(128)} %bitcast.me_ref, f32[128,1280]{1,0:T(8,128)S(1)} %copy-done.5, ...), custom_call_target="tpu_custom_call" | custom-call | flops 69206016 | bytes 2097152 | tf_op jit(solution)/shard_map/pallas_call | solution.py:200
  35.9 1.4 %collective-permute-start.3 = (bf16[2,24,1408]{2,1,0:T(8,128)(2,1)S(1)}, bf16[2,24,1408]{2,1,0:T(8,128)(2,1)S(1)}, u32[]{:S(2)}, u32[]{:S(2)}) collective-permute-start(bf16[2,24,1408]{2,1,0:T(8,128)(2,1)S(1)} %get-tuple-element.27), channel_id=1, source_target_pairs={{0,4},{2,6},{4,0},{6,2},{8,12},{10,14},{12,8},{14,10},{1,5},{3,7},... | collective-permute-start | bytes 405512 | tf_op jit(solution)/shard_map/ppermute | solution.py:523
  37.3 2.6 %collective-permute-start.4 = (bf16[2,24,1408]{2,1,0:T(8,128)(2,1)S(1)}, bf16[2,24,1408]{2,1,0:T(8,128)(2,1)S(1)}, u32[]{:S(2)}, u32[]{:S(2)}) collective-permute-start(bf16[2,24,1408]{2,1,0:T(8,128)(2,1)S(1)} %get-tuple-element.28), channel_id=1, source_target_pairs={{0,8},{2,10},{4,12},{6,14},{8,0},{10,2},{12,4},{14,6},{1,9},{3,11}... | collective-permute-start | bytes 405512 | tf_op jit(solution)/shard_map/ppermute | solution.py:523
  39.9 3.8 %collective-permute-done.4 = bf16[2,24,1408]{2,1,0:T(8,128)(2,1)S(1)} collective-permute-done((bf16[2,24,1408]{2,1,0:T(8,128)(2,1)S(1)}, bf16[2,24,1408]{2,1,0:T(8,128)(2,1)S(1)}, u32[]{:S(2)}, u32[]{:S(2)}) %collective-permute-start.4) | collective-permute-done | bytes 135200 | tf_op jit(solution)/shard_map/ppermute | solution.py:523
  43.8 1.4 %collective-permute-done.5 = bf16[2,24,1408]{2,1,0:T(8,128)(2,1)S(1)} collective-permute-done((bf16[2,24,1408]{2,1,0:T(8,128)(2,1)S(1)}, bf16[2,24,1408]{2,1,0:T(8,128)(2,1)S(1)}, u32[]{:S(2)}, u32[]{:S(2)}) %collective-permute-start.5) | collective-permute-done | bytes 135200 | tf_op jit(solution)/shard_map/ppermute | solution.py:523
  45.2 4.0 %collective-permute-start.6 = (bf16[4,24,1408]{2,1,0:T(8,128)(2,1)S(1)}, bf16[4,24,1408]{2,1,0:T(8,128)(2,1)S(1)}, u32[]{:S(2)}, u32[]{:S(2)}) collective-permute-start(bf16[4,24,1408]{2,1,0:T(8,128)(2,1)S(1)} %pad_maximum_fusion), channel_id=1, source_target_pairs={{0,2},{2,0},{4,6},{6,4},{8,10},{10,8},{12,14},{14,12},{1,3},{3,1},... | collective-permute-start | bytes 811016 | tf_op jit(solution)/shard_map/ppermute | solution.py:523
  50.6 3.2 %collective-permute-start.7 = (bf16[8,24,1152]{2,1,0:T(8,128)(2,1)S(1)}, bf16[8,24,1152]{2,1,0:T(8,128)(2,1)S(1)}, u32[]{:S(2)}, u32[]{:S(2)}) collective-permute-start(bf16[8,24,1152]{2,1,0:T(8,128)(2,1)S(1)} %slice.86), channel_id=1, source_target_pairs={{0,1},{1,0},{2,3},{3,2},{4,5},{5,4},{6,7},{7,6},{8,9},{9,8},{10,11... | collective-permute-start | bytes 1327112 | tf_op jit(solution)/shard_map/ppermute | solution.py:519
  53.9 2.8 %copy-done = bf16[1,192,128,128]{3,2,1,0:T(8,128)(2,1)S(1)} copy-done((bf16[1,192,128,128]{3,2,1,0:T(8,128)(2,1)S(1)}, bf16[1,192,128,128]{3,2,1,0:T(8,128)(2,1)}, u32[]{:S(2)}) %copy-start) | copy-done | bytes 6291480
  56.6 2.8 %copy-done.1 = bf16[1,192,128,128]{3,2,1,0:T(8,128)(2,1)S(1)} copy-done((bf16[1,192,128,128]{3,2,1,0:T(8,128)(2,1)S(1)}, bf16[1,192,128,128]{3,2,1,0:T(8,128)(2,1)}, u32[]{:S(2)}) %copy-start.1) | copy-done | bytes 6291480
  59.4 3.2 %shard_map.160 = (f32[4,24,1024]{2,1,0:T(8,128)S(1)}, f32[4,24,128]{2,1,0:T(8,128)S(1)}) custom-call(s32[4]{0:T(128)S(1)} %add_xor_fusion.where_ref, s32[1]{0:T(128)} %bitcast.1.span_ref.parity_ref, bf16[8,24,1408]{2,1,0:T(8,128)(2,1)S(1)} %slice_dynamic-update-slice_fusion.rows_ref, bf16[8,24,128,128]{3,2,1,0:T(8,128)(2,1)S(1)} %bitcast.15, ...), custom_call_target="tpu_custom_call" | custom-call | flops 2000000000 | bytes 8388608 | tf_op jit(solution)/shard_map/pallas_call | solution.py:271
  64.0 11.3 %shard_map.161 = bf16[8,24,1408]{2,1,0:T(8,128)(2,1)S(1)} custom-call(s32[4]{0:T(128)S(1)} %add_xor_fusion.where_ref, bf16[8,24,1152]{2,1,0:T(8,128)(2,1)S(1)} %collective-permute-done.7.rows_ref, bf16[4096,128]{1,0:T(8,128)(2,1)S(1)} %bitcast.21, bf16[4096,128]{1,0:T(8,128)(2,1)S(1)} %bitcast.23, s32[1]{0:T(128)S(6)} %sub.3.refs_0_, ...), custom_call_target="tpu_custom_call" | custom-call | flops 3221225472 | bytes 4194304 | tf_op jit(solution)/shard_map/pallas_call | solution.py:417
  75.3 3.1 %collective-permute-start.8 = (bf16[8,24,1408]{2,1,0:T(8,128)(2,1)S(1)}, bf16[8,24,1408]{2,1,0:T(8,128)(2,1)S(1)}, u32[]{:S(2)}, u32[]{:S(2)}) collective-permute-start(bf16[8,24,1408]{2,1,0:T(8,128)(2,1)S(1)} %shard_map.161), channel_id=1, source_target_pairs={{0,1},{1,0},{2,3},{3,2},{4,5},{5,4},{6,7},{7,6},{8,9},{9,8},{10,11... | collective-permute-start | bytes 1622024 | tf_op jit(solution)/shard_map/ppermute | solution.py:519
  78.4 10.2 %shard_map.162 = (f32[8,24,1024]{2,1,0:T(8,128)S(1)}, f32[8,24,128]{2,1,0:T(8,128)S(1)}) custom-call(s32[4]{0:T(128)S(1)} %add_xor_fusion.where_ref, bf16[8,24,1408]{2,1,0:T(8,128)(2,1)S(1)} %slice_dynamic-update-slice_fusion.rows_ref, bf16[4096,128]{1,0:T(8,128)(2,1)S(1)} %bitcast.22, bf16[4096,128]{1,0:T(8,128)(2,1)S(1)} %bitcast.24, ...), custom_call_target="tpu_custom_call" | custom-call | flops 3221225472 | bytes 4194304 | tf_op jit(solution)/shard_map/pallas_call | solution.py:417
  88.6 1.3 %collective-permute-done.8.came_ref = bf16[8,24,1408]{2,1,0:T(8,128)(2,1)S(1)} collective-permute-done((bf16[8,24,1408]{2,1,0:T(8,128)(2,1)S(1)}, bf16[8,24,1408]{2,1,0:T(8,128)(2,1)S(1)}, u32[]{:S(2)}, u32[]{:S(2)}) %collective-permute-start.8) | collective-permute-done | bytes 540704 | tf_op jit(solution)/shard_map/ppermute | solution.py:519
  89.9 1.4 %shard_map.163 = (bf16[2,24,1024]{2,1,0:T(8,128)(2,1)S(1)}, bf16[2,24,1024]{2,1,0:T(8,128)(2,1)S(1)}, bf16[2,24,1024]{2,1,0:T(8,128)(2,1)S(1)}, bf16[2,24,1024]{2,1,0:T(8,128)(2,1)S(1)}) custom-call(f32[8,24,1024]{2,1,0:T(8,128)S(1)} %get-tuple-element.36.out_ref, f32[8,24,128]{2,1,0:T(8,128)S(1)} %get-tuple-element.37.log_ref, ...), custom_call_target="tpu_custom_call" | custom-call | flops 1000000 | bytes 2097152 | tf_op jit(solution)/shard_map/pallas_call | solution.py:456
  91.4 1.9 %collective-permute-start.10 = (bf16[2,24,1024]{2,1,0:T(8,128)(2,1)S(1)}, bf16[2,24,1024]{2,1,0:T(8,128)(2,1)S(1)}, u32[]{:S(2)}, u32[]{:S(2)}) collective-permute-start(bf16[2,24,1024]{2,1,0:T(8,128)(2,1)S(1)} %get-tuple-element.40), channel_id=1, source_target_pairs={{0,8},{2,10},{4,12},{6,14},{8,0},{10,2},{12,4},{14,6},{1,9},{3,11}... | collective-permute-start | bytes 294920 | tf_op jit(solution)/shard_map/ppermute | solution.py:523
  93.3 1.9 %collective-permute-start.11 = (bf16[2,24,1024]{2,1,0:T(8,128)(2,1)S(1)}, bf16[2,24,1024]{2,1,0:T(8,128)(2,1)S(1)}, u32[]{:S(2)}, u32[]{:S(2)}) collective-permute-start(bf16[2,24,1024]{2,1,0:T(8,128)(2,1)S(1)} %get-tuple-element.41), channel_id=1, source_target_pairs={{0,12},{2,14},{4,8},{6,10},{8,4},{10,6},{12,0},{14,2},{1,13},{3,15... | collective-permute-start | bytes 294920 | tf_op jit(solution)/shard_map/ppermute | solution.py:523
  96.4 2.7 %collective-permute-done.11.near3_ref = bf16[2,24,1024]{2,1,0:T(8,128)(2,1)S(1)} collective-permute-done((bf16[2,24,1024]{2,1,0:T(8,128)(2,1)S(1)}, bf16[2,24,1024]{2,1,0:T(8,128)(2,1)S(1)}, u32[]{:S(2)}, u32[]{:S(2)}) %collective-permute-start.11) | collective-permute-done | bytes 98336 | tf_op jit(solution)/shard_map/ppermute | solution.py:523
  99.2 2.5 %collective-permute-start.12 = (bf16[4,24,1024]{2,1,0:T(8,128)(2,1)S(1)}, bf16[4,24,1024]{2,1,0:T(8,128)(2,1)S(1)}, u32[]{:S(2)}, u32[]{:S(2)}) collective-permute-start(bf16[4,24,1024]{2,1,0:T(8,128)(2,1)S(1)} %pad_maximum_fusion.1), channel_id=1, source_target_pairs={{0,2},{2,0},{4,6},{6,4},{8,10},{10,8},{12,14},{14,12},{1,3},{3,1},... | collective-permute-start | bytes 589832 | tf_op jit(solution)/shard_map/ppermute | solution.py:523
  (71 shorter events, 9.3 us)
Async XLA Ops:
  2.7 5.5 %copy-start.9 = (f32[256]{0:T(256)}, f32[256]{0:T(256)S(1)}, u32[]{:S(2)}) copy-start(f32[256]{0:T(256)S(1)} %multiply_reduce_fusion) | copy-start | bytes 3076
  2.7 5.5 %collective-permute-start = (f32[256]{0:T(256)S(1)}, f32[256]{0:T(256)S(1)}, u32[]{:S(2)}, u32[]{:S(2)}) collective-permute-start(f32[256]{0:T(256)S(1)} %multiply_reduce_fusion), channel_id=1, source_target_pairs={{0,1},{1,0},{2,3},{3,2},{4,5},{5,4},{6,7},{7,6},{8,9},{9,8},{10,11... | collective-permute-start | bytes 3080 | tf_op jit(solution)/shard_map/ppermute | solution.py:519
  8.8 11.9 %copy-start.10 = (bf16[1024]{0:T(1024)(128)(2,1)S(1)}, bf16[1024]{0:T(1024)(128)(2,1)}, u32[]{:S(2)}) copy-start(bf16[1024]{0:T(1024)(128)(2,1)} %param.20) | copy-start | bytes 6148
  8.8 11.9 %copy-start.12 = (bf16[128]{0:T(256)(128)(2,1)S(1)}, bf16[128]{0:T(256)(128)(2,1)}, u32[]{:S(2)}) copy-start(bf16[128]{0:T(256)(128)(2,1)} %param.22) | copy-start | bytes 772
  8.8 11.9 %copy-start.13 = (bf16[128]{0:T(256)(128)(2,1)S(1)}, bf16[128]{0:T(256)(128)(2,1)}, u32[]{:S(2)}) copy-start(bf16[128]{0:T(256)(128)(2,1)} %param.21) | copy-start | bytes 772
  8.8 24.8 %copy-start.6 = (s32[8]{0:T(128)S(1)}, s32[8]{0:T(128)}, u32[]{:S(2)}) copy-start(s32[8]{0:T(128)} %home_ref.1) | copy-start | bytes 100
  8.8 24.8 %copy-start.7 = (s32[128]{0:T(128)S(1)}, s32[128]{0:T(128)}, u32[]{:S(2)}) copy-start(s32[128]{0:T(128)} %param.27) | copy-start | bytes 1540
  8.8 24.8 %copy-start.8 = (s32[128]{0:T(128)S(1)}, s32[128]{0:T(128)}, u32[]{:S(2)}) copy-start(s32[128]{0:T(128)} %param.28) | copy-start | bytes 1540
  17.1 16.5 %collective-permute-start.1 = (f32[128,768]{1,0:T(8,128)}, f32[128,768]{1,0:T(8,128)S(1)}, u32[]{:S(2)}, u32[]{:S(2)}) collective-permute-start(f32[128,768]{1,0:T(8,128)} %get-tuple-element.23), channel_id=1, source_target_pairs={{0,1},{1,0},{2,3},{3,2},{4,5},{5,4},{6,7},{7,6},{8,9},{9,8},{10,11... | collective-permute-start | bytes 1179656 | tf_op jit(solution)/shard_map/ppermute | solution.py:519
  20.4 13.1 %collective-permute-start.2 = (f32[128,512]{1,0:T(8,128)}, f32[128,512]{1,0:T(8,128)S(1)}, u32[]{:S(2)}, u32[]{:S(2)}) collective-permute-start(f32[128,512]{1,0:T(8,128)} %get-tuple-element.24), channel_id=1, source_target_pairs={{0,1},{1,0},{2,3},{3,2},{4,5},{5,4},{6,7},{7,6},{8,9},{9,8},{10,11... | collective-permute-start | bytes 786440 | tf_op jit(solution)/shard_map/ppermute | solution.py:519
  34.7 29.1 %slice-start = ((s8[6291456]{0:T(1024)(128)(4,1)}), s8[2097152]{0:T(1024)(128)(4,1)S(1)}, s32[]{:S(2)}) async-start(s8[6291456]{0:T(1024)(128)(4,1)} %bitcast.16), calls=%async_computation | async-start | bytes 4194304
  35.9 4.0 %collective-permute-start.3 = (bf16[2,24,1408]{2,1,0:T(8,128)(2,1)S(1)}, bf16[2,24,1408]{2,1,0:T(8,128)(2,1)S(1)}, u32[]{:S(2)}, u32[]{:S(2)}) collective-permute-start(bf16[2,24,1408]{2,1,0:T(8,128)(2,1)S(1)} %get-tuple-element.27), channel_id=1, source_target_pairs={{0,4},{2,6},{4,0},{6,2},{8,12},{10,14},{12,8},{14,10},{1,5},{3,7},... | collective-permute-start | bytes 405512 | tf_op jit(solution)/shard_map/ppermute | solution.py:523
  37.3 6.5 %collective-permute-start.4 = (bf16[2,24,1408]{2,1,0:T(8,128)(2,1)S(1)}, bf16[2,24,1408]{2,1,0:T(8,128)(2,1)S(1)}, u32[]{:S(2)}, u32[]{:S(2)}) collective-permute-start(bf16[2,24,1408]{2,1,0:T(8,128)(2,1)S(1)} %get-tuple-element.28), channel_id=1, source_target_pairs={{0,8},{2,10},{4,12},{6,14},{8,0},{10,2},{12,4},{14,6},{1,9},{3,11}... | collective-permute-start | bytes 405512 | tf_op jit(solution)/shard_map/ppermute | solution.py:523
  39.9 5.3 %collective-permute-start.5 = (bf16[2,24,1408]{2,1,0:T(8,128)(2,1)S(1)}, bf16[2,24,1408]{2,1,0:T(8,128)(2,1)S(1)}, u32[]{:S(2)}, u32[]{:S(2)}) collective-permute-start(bf16[2,24,1408]{2,1,0:T(8,128)(2,1)S(1)} %get-tuple-element.29), channel_id=1, source_target_pairs={{0,12},{2,14},{4,8},{6,10},{8,4},{10,6},{12,0},{14,2},{1,13},{3,15... | collective-permute-start | bytes 405512 | tf_op jit(solution)/shard_map/ppermute | solution.py:523
  45.2 5.2 %collective-permute-start.6 = (bf16[4,24,1408]{2,1,0:T(8,128)(2,1)S(1)}, bf16[4,24,1408]{2,1,0:T(8,128)(2,1)S(1)}, u32[]{:S(2)}, u32[]{:S(2)}) collective-permute-start(bf16[4,24,1408]{2,1,0:T(8,128)(2,1)S(1)} %pad_maximum_fusion), channel_id=1, source_target_pairs={{0,2},{2,0},{4,6},{6,4},{8,10},{10,8},{12,14},{14,12},{1,3},{3,1},... | collective-permute-start | bytes 811016 | tf_op jit(solution)/shard_map/ppermute | solution.py:523
  50.6 13.1 %collective-permute-start.7 = (bf16[8,24,1152]{2,1,0:T(8,128)(2,1)S(1)}, bf16[8,24,1152]{2,1,0:T(8,128)(2,1)S(1)}, u32[]{:S(2)}, u32[]{:S(2)}) collective-permute-start(bf16[8,24,1152]{2,1,0:T(8,128)(2,1)S(1)} %slice.86), channel_id=1, source_target_pairs={{0,1},{1,0},{2,3},{3,2},{4,5},{5,4},{6,7},{7,6},{8,9},{9,8},{10,11... | collective-permute-start | bytes 1327112 | tf_op jit(solution)/shard_map/ppermute | solution.py:519
  59.4 4.3 %copy-start.2 = (bf16[1,192,128,128]{3,2,1,0:T(8,128)(2,1)S(1)}, bf16[1,192,128,128]{3,2,1,0:T(8,128)(2,1)}, u32[]{:S(2)}) copy-start(bf16[1,192,128,128]{3,2,1,0:T(8,128)(2,1)} %param.26) | copy-start | bytes 18874372
  59.4 4.3 %copy-start.3 = (bf16[1,4096,128]{2,1,0:T(8,128)(2,1)S(1)}, bf16[1,4096,128]{2,1,0:T(8,128)(2,1)}, u32[]{:S(2)}) copy-start(bf16[1,4096,128]{2,1,0:T(8,128)(2,1)} %param.23) | copy-start | bytes 3145732
  59.4 4.6 %copy-start.4 = (bf16[1,4096,128]{2,1,0:T(8,128)(2,1)S(1)}, bf16[1,4096,128]{2,1,0:T(8,128)(2,1)}, u32[]{:S(2)}) copy-start(bf16[1,4096,128]{2,1,0:T(8,128)(2,1)} %param.24) | copy-start | bytes 3145732
  75.3 14.6 %collective-permute-start.8 = (bf16[8,24,1408]{2,1,0:T(8,128)(2,1)S(1)}, bf16[8,24,1408]{2,1,0:T(8,128)(2,1)S(1)}, u32[]{:S(2)}, u32[]{:S(2)}) collective-permute-start(bf16[8,24,1408]{2,1,0:T(8,128)(2,1)S(1)} %shard_map.161), channel_id=1, source_target_pairs={{0,1},{1,0},{2,3},{3,2},{4,5},{5,4},{6,7},{7,6},{8,9},{9,8},{10,11... | collective-permute-start | bytes 1622024 | tf_op jit(solution)/shard_map/ppermute | solution.py:519
  91.3 3.9 %collective-permute-start.9 = (bf16[2,24,1024]{2,1,0:T(8,128)(2,1)S(1)}, bf16[2,24,1024]{2,1,0:T(8,128)(2,1)S(1)}, u32[]{:S(2)}, u32[]{:S(2)}) collective-permute-start(bf16[2,24,1024]{2,1,0:T(8,128)(2,1)S(1)} %get-tuple-element.39), channel_id=1, source_target_pairs={{0,4},{2,6},{4,0},{6,2},{8,12},{10,14},{12,8},{14,10},{1,5},{3,7},... | collective-permute-start | bytes 294920 | tf_op jit(solution)/shard_map/ppermute | solution.py:523
  91.4 5.1 %collective-permute-start.10 = (bf16[2,24,1024]{2,1,0:T(8,128)(2,1)S(1)}, bf16[2,24,1024]{2,1,0:T(8,128)(2,1)S(1)}, u32[]{:S(2)}, u32[]{:S(2)}) collective-permute-start(bf16[2,24,1024]{2,1,0:T(8,128)(2,1)S(1)} %get-tuple-element.40), channel_id=1, source_target_pairs={{0,8},{2,10},{4,12},{6,14},{8,0},{10,2},{12,4},{14,6},{1,9},{3,11}... | collective-permute-start | bytes 294920 | tf_op jit(solution)/shard_map/ppermute | solution.py:523
  93.3 5.9 %collective-permute-start.11 = (bf16[2,24,1024]{2,1,0:T(8,128)(2,1)S(1)}, bf16[2,24,1024]{2,1,0:T(8,128)(2,1)S(1)}, u32[]{:S(2)}, u32[]{:S(2)}) collective-permute-start(bf16[2,24,1024]{2,1,0:T(8,128)(2,1)S(1)} %get-tuple-element.41), channel_id=1, source_target_pairs={{0,12},{2,14},{4,8},{6,10},{8,4},{10,6},{12,0},{14,2},{1,13},{3,15... | collective-permute-start | bytes 294920 | tf_op jit(solution)/shard_map/ppermute | solution.py:523
  99.2 3.6 %collective-permute-start.12 = (bf16[4,24,1024]{2,1,0:T(8,128)(2,1)S(1)}, bf16[4,24,1024]{2,1,0:T(8,128)(2,1)S(1)}, u32[]{:S(2)}, u32[]{:S(2)}) collective-permute-start(bf16[4,24,1024]{2,1,0:T(8,128)(2,1)S(1)} %pad_maximum_fusion.1), channel_id=1, source_target_pairs={{0,2},{2,0},{4,6},{6,4},{8,10},{10,8},{12,14},{14,12},{1,3},{3,1},... | collective-permute-start | bytes 589832 | tf_op jit(solution)/shard_map/ppermute | solution.py:523
  (5 other events, 11.6 us)

commit v4 on v3

--- a/solution.py
+++ b/solution.py
@@ -21,7 +21,7 @@
 SLOTS = HOLDERS * CAP
 BLOCK = 256
 PIECES = 8
-CUT = 768
+CUT = QW
 LENGTH_AT = QW
 KEY_AT = QW + HD
 VALUE_AT = QW + 2 * HD
@@ -46,22 +46,29 @@
     return jnp.sum(jnp.where(diagonal, spread, jnp.zeros_like(spread)), axis=1, keepdims=True)
 
 
-def project_kernel(
+def normalise(span, mine_ref, theirs_ref, gain_ref, rows_ref, normed_ref):
+    inverse = lax.rsqrt((mine_ref[...] + theirs_ref[...]) / D + EPSILON)
+    first = to_column(inverse[0:1, :])
+    second = to_column(inverse[1:2, :])
+    scales = (jnp.where(span == 0, first, second), jnp.where(span == 0, second, first))
+    gain = gain_ref[...].astype(F32).reshape(1, -1)
+    for where, start in enumerate((span * ROWS, (1 - span) * ROWS)):
+        rows = rows_ref[pl.ds(pl.multiple_of(start, ROWS), ROWS), :].astype(F32)
+        normed = rows * scales[where] * gain
+        normed_ref[where * ROWS : (where + 1) * ROWS, :] = normed.astype(BF16)
+
+
+def project_queries_kernel(
     span_ref,
     mine_ref,
     theirs_ref,
     hidden_ref,
     gain_ref,
     wq_ref,
-    wk_ref,
-    wv_ref,
     keep_ref,
-    send0_ref,
-    send1_ref,
+    send_ref,
     rows_ref,
     query_ref,
-    key_ref,
-    value_ref,
     normed_ref,
     sems,
 ):
@@ -73,68 +80,80 @@
         copies.append(
             pltpu.make_async_copy(wq_ref.at[part], query_ref.at[part], sems.at[1 + piece])
         )
-    copies.append(pltpu.make_async_copy(wk_ref, key_ref, sems.at[1 + PIECES]))
-    copies.append(pltpu.make_async_copy(wv_ref, value_ref, sems.at[2 + PIECES]))
     for copy in copies:
         copy.start()
-    span = span_ref[0]
-    inverse = lax.rsqrt((mine_ref[...] + theirs_ref[...]) / D + EPSILON)
-    first = to_column(inverse[0:1, :])
-    second = to_column(inverse[1:2, :])
-    scales = (jnp.where(span == 0, first, second), jnp.where(span == 0, second, first))
-    gain = gain_ref[...].astype(F32).reshape(1, -1)
     copies[0].wait()
-    for where, start in enumerate((span * ROWS, (1 - span) * ROWS)):
-        rows = rows_ref[pl.ds(pl.multiple_of(start, ROWS), ROWS), :].astype(F32)
-        normed = rows * scales[where] * gain
-        normed_ref[where * ROWS : (where + 1) * ROWS, :] = normed.astype(BF16)
-
-    def add(at, total, fresh):
-        width = total.shape[1]
-        send_ref, here = (send0_ref, at) if at < CUT else (send1_ref, at - CUT)
-        for out_ref, rows, column in ((keep_ref, total[:ROWS], at), (send_ref, total[ROWS:], here)):
-            part = slice(column, column + width)
-            out_ref[:, part] = rows if fresh else out_ref[:, part] + rows
-
+    normalise(span_ref[0], mine_ref, theirs_ref, gain_ref, rows_ref, normed_ref)
     for piece in range(PIECES):
         copies[1 + piece].wait()
         part = slice(piece * step, (piece + 1) * step)
         for at in range(0, QW, 256):
-            weights = query_ref[part, at : at + 256]
-            add(at, jnp.dot(normed_ref[:, part], weights, preferred_element_type=F32), piece == 0)
-    for index, w_ref in enumerate((key_ref, value_ref)):
-        copies[1 + PIECES + index].wait()
-        total = jnp.dot(normed_ref[...], w_ref[...], preferred_element_type=F32)
-        add(QW + index * HD, total, True)
-
-
-def project(span, mine, theirs, hidden, gain, w_query, w_key, w_value):
+            here = slice(at, at + 256)
+            total = jnp.dot(normed_ref[:, part], query_ref[part, here], preferred_element_type=F32)
+            for out_ref, rows in ((keep_ref, total[:ROWS]), (send_ref, total[ROWS:])):
+                out_ref[:, here] = rows if piece == 0 else out_ref[:, here] + rows
+
+
+def project_queries(span, mine, theirs, hidden, gain, w_query):
     depth = hidden.shape[1]
-    width = QW + 2 * HD
     vmem = pl.BlockSpec(memory_space=pltpu.VMEM)
     hbm = pl.BlockSpec(memory_space=pltpu.HBM)
     return pl.pallas_call(
-        project_kernel,
-        in_specs=[pl.BlockSpec(memory_space=pltpu.SMEM), vmem, vmem, hbm, vmem, hbm, hbm, hbm],
-        out_specs=[vmem] * 3,
-        out_shape=[
-            jax.ShapeDtypeStruct((ROWS, width), F32),
-            jax.ShapeDtypeStruct((ROWS, CUT), F32),
-            jax.ShapeDtypeStruct((ROWS, width - CUT), F32),
-        ],
+        project_queries_kernel,
+        in_specs=[pl.BlockSpec(memory_space=pltpu.SMEM), vmem, vmem, hbm, vmem, hbm],
+        out_specs=[vmem] * 2,
+        out_shape=[jax.ShapeDtypeStruct((ROWS, QW), F32)] * 2,
         scratch_shapes=[
             pltpu.VMEM((2 * ROWS, depth), BF16),
             pltpu.VMEM((depth, QW), BF16),
-            pltpu.VMEM((depth, HD), BF16),
-            pltpu.VMEM((depth, HD), BF16),
             pltpu.VMEM((2 * ROWS, depth), BF16),
-            pltpu.SemaphoreType.DMA((3 + PIECES,)),
+            pltpu.SemaphoreType.DMA((1 + PIECES,)),
         ],
         compiler_params=params(56),
         cost_estimate=pl.CostEstimate(
-            flops=2 * 2 * ROWS * depth * width, bytes_accessed=14 * 2**20, transcendentals=0
+            flops=2 * 2 * ROWS * depth * QW, bytes_accessed=12 * 2**20, transcendentals=0
         ),
-    )(span, mine, theirs, hidden, gain, w_query, w_key, w_value)
+    )(span, mine, theirs, hidden, gain, w_query)
+
+
+def project_rows_kernel(
+    span_ref,
+    mine_ref,
+    theirs_ref,
+    hidden_ref,
+    gain_ref,
+    wk_ref,
+    wv_ref,
+    held_ref,
+    keep_ref,
+    send_ref,
+    normed_ref,
+):
+    normalise(span_ref[0], mine_ref, theirs_ref, gain_ref, hidden_ref, normed_ref)
+    keep_ref[:, 0:QW] = held_ref[...]
+    for at, w_ref in ((0, wk_ref), (HD, wv_ref)):
+        total = jnp.dot(normed_ref[...], w_ref[...], preferred_element_type=F32)
+        keep_ref[:, QW + at : QW + at + HD] = total[:ROWS]
+        send_ref[:, at : at + HD] = total[ROWS:]
+
+
+def project_rows(span, mine, theirs, hidden, gain, w_key, w_value, held):
+    depth = hidden.shape[1]
+    vmem = pl.BlockSpec(memory_space=pltpu.VMEM)
+    return pl.pallas_call(
+        project_rows_kernel,
+        in_specs=[pl.BlockSpec(memory_space=pltpu.SMEM)] + [vmem] * 7,
+        out_specs=[vmem] * 2,
+        out_shape=[
+            jax.ShapeDtypeStruct((ROWS, QW + 2 * HD), F32),
+            jax.ShapeDtypeStruct((ROWS, 2 * HD), F32),
+        ],
+        scratch_shapes=[pltpu.VMEM((2 * ROWS, depth), BF16)],
+        compiler_params=params(56),
+        cost_estimate=pl.CostEstimate(
+            flops=2 * 2 * ROWS * depth * 2 * HD, bytes_accessed=6 * 2**20, transcendentals=0
+        ),
+    )(span, mine, theirs, hidden, gain, w_key, w_value, held)
 
 
 def spread_kernel(
@@ -546,17 +565,10 @@
     widened = hidden.astype(F32)
     squares = jnp.sum(widened * widened, axis=1)
     theirs = other_pair(squares)
-    keep, send0, send1 = project(
-        span,
-        squares.reshape(2, ROWS),
-        theirs.reshape(2, ROWS),
-        hidden,
-        norm_gain,
-        w_query,
-        w_key,
-        w_value,
-    )
+    sums = (squares.reshape(2, ROWS), theirs.reshape(2, ROWS))
+    held, send0 = project_queries(span, *sums, hidden, norm_gain, w_query)
     came0 = other_pair(send0)
+    keep, send1 = project_rows(span, *sums, hidden, norm_gain, w_key, w_value, held)
     came1 = other_pair(send1)
 
     half = HD // 2

time: 104 us -> 106 us (1.019)
  waiting for transfers between devices: 26.3 us -> 22.2 us
  local copies, waits for them, and re-layouts: 7.7 us -> 10.9 us
  Pallas kernels: 37.2 us -> 40.2 us
    ppermute x5, waiting for transfers between devices: 15.6 us -> 11.9 us  [other_pair(): return lax.ppermute(values, 'pair', [(0, 1), (1, 0)])]
    pallas_call x1 -> x2, Pallas kernels: 8.26 us -> 11.3 us  [the longest x1 6.69 us: project_queries(): pl.pallas_call(project_queries_kernel, in_specs=[pl.BlockSpec(memory_spac...]
    unnamed x38 -> x36, local copies, waits for them, and re-layouts: 7.58 us -> 10.1 us
  transfers between devices with their start and end apart: 13 -> 13, of which waited for: 10 -> 9; matrix products, arithmetic and copies ran while one was open for 1% -> 2% of each run, Pallas kernels for 14% -> 18%
where the time goes in v4:
time: 106 us; the launch traced here: 105 us
  Pallas kernels  40.2 us (38%)
  starting transfers between devices  28 us (26%)
  waiting for transfers between devices  22.2 us (21%)
  local copies, waits for them, and re-layouts  10.9 us (10%)
  other arithmetic  3.25 us (3%)
    pallas_call x2, Pallas kernels, prefix(): pl.pallas_call(partial(prefix_kernel, own), in_specs=[smem] + [vmem] * 3...  21.5 us
    ppermute x8, starting transfers between devices, flip(): lax.ppermute(values, 'memory', [(m, m ^ bits) for m in range(HOLDERS)])  14.9 us
    ppermute x5, starting transfers between devices, other_pair(): return lax.ppermute(values, 'pair', [(0, 1), (1, 0)])  13.1 us
    ppermute x5, waiting for transfers between devices, other_pair(): return lax.ppermute(values, 'pair', [(0, 1), (1, 0)])  11.9 us
    ppermute x8, waiting for transfers between devices, flip(): lax.ppermute(values, 'memory', [(m, m ^ bits) for m in range(HOLDERS)])  10.3 us
    unnamed x36, local copies, waits for them, and re-layouts  10.1 us
    pallas_call x1, Pallas kernels, project_queries(): pl.pallas_call(project_queries_kernel, in_specs=[pl.BlockSpec(memory_spac...  6.69 us
    pallas_call x1, Pallas kernels, project_rows(): pl.pallas_call(project_rows_kernel, in_specs=[pl.BlockSpec(memory_space=p...  4.57 us
  transfers between devices with their start and end apart: 13, of which 9 were waited for; matrix products, arithmetic and copies ran while one was open for 2% of the time, Pallas kernels for 18%

profile of v4, /device:TPU:1, one launch (start us, length us, event | category | flops | bytes accessed | tf_op | source)
XLA Modules:
  0.0 105.4 jit_solution(10337850381744585680)
XLA Ops:
  0.6 2.1 %multiply_reduce_fusion = f32[256]{0:T(256)S(1)} fusion(bf16[256,4096]{1,0:T(8,128)(2,1)} %hidden_ref.3), kind=kLoop, calls=%fused_computation | loop fusion | flops 3145472 | bytes 2098176 | tf_op jit(solution)/shard_map/reduce_sum | solution.py:566
  2.7 4.5 %collective-permute-start = (f32[256]{0:T(256)S(1)}, f32[256]{0:T(256)S(1)}, u32[]{:S(2)}, u32[]{:S(2)}) collective-permute-start(f32[256]{0:T(256)S(1)} %multiply_reduce_fusion), channel_id=1, source_target_pairs={{0,1},{1,0},{2,3},{3,2},{4,5},{5,4},{6,7},{7,6},{8,9},{9,8},{10,11... | collective-permute-start | bytes 3080 | tf_op jit(solution)/shard_map/ppermute | solution.py:538
  9.2 6.7 %shard_map.158 = (f32[128,1024]{1,0:T(8,128)}, f32[128,1024]{1,0:T(8,128)}) custom-call(s32[1]{0:T(128)} %bitcast.1.span_ref.parity_ref, f32[2,128]{1,0:T(2,128)} %bitcast.28, f32[2,128]{1,0:T(2,128)} %bitcast.30, bf16[256,4096]{1,0:T(8,128)(2,1)} %hidden_ref.3, bf16[4096]{0:T(1024)(128)(2,1)} %gain_ref.3, bf16[4096,1024]{1,0:T(8,128)(2,1)} %wq_ref.1), custom_call_target="tpu_custom_call" | custom-call | flops 2147483648 | bytes 12582912 | tf_op jit(solution)/shard_map/pallas_call | solution.py:101
  15.9 2.6 %collective-permute-start.1 = (f32[128,1024]{1,0:T(8,128)}, f32[128,1024]{1,0:T(8,128)S(1)}, u32[]{:S(2)}, u32[]{:S(2)}) collective-permute-start(f32[128,1024]{1,0:T(8,128)} %get-tuple-element.25), channel_id=1, source_target_pairs={{0,1},{1,0},{2,3},{3,2},{4,5},{5,4},{6,7},{7,6},{8,9},{9,8},{10,11... | collective-permute-start | bytes 1572872 | tf_op jit(solution)/shard_map/ppermute | solution.py:538
  18.9 4.6 %shard_map.159 = (f32[128,1280]{1,0:T(8,128)}, f32[128,256]{1,0:T(8,128)}) custom-call(s32[1]{0:T(128)} %bitcast.1.span_ref.parity_ref, f32[2,128]{1,0:T(2,128)} %bitcast.29, f32[2,128]{1,0:T(2,128)} %bitcast.31, bf16[256,4096]{1,0:T(8,128)(2,1)} %hidden_ref.3, bf16[4096]{0:T(1024)(128)(2,1)} %gain_ref.3, bf16[4096,128]{1,0:T(8,128)(2,1)} %wk_ref.1, ...), custom_call_target="tpu_custom_call" | custom-call | flops 536870912 | bytes 6291456 | tf_op jit(solution)/shard_map/pallas_call | solution.py:143
  24.0 8.8 %collective-permute-done.2.came1_ref = f32[128,256]{1,0:T(8,128)S(1)} collective-permute-done((f32[128,256]{1,0:T(8,128)}, f32[128,256]{1,0:T(8,128)S(1)}, u32[]{:S(2)}, u32[]{:S(2)}) %collective-permute-start.2) | collective-permute-done | bytes 131104 | tf_op jit(solution)/shard_map/ppermute | solution.py:538
  36.5 2.6 %collective-permute-start.4 = (bf16[2,24,1408]{2,1,0:T(8,128)(2,1)S(1)}, bf16[2,24,1408]{2,1,0:T(8,128)(2,1)S(1)}, u32[]{:S(2)}, u32[]{:S(2)}) collective-permute-start(bf16[2,24,1408]{2,1,0:T(8,128)(2,1)S(1)} %get-tuple-element.30), channel_id=1, source_target_pairs={{0,8},{2,10},{4,12},{6,14},{8,0},{10,2},{12,4},{14,6},{1,9},{3,11}... | collective-permute-start | bytes 405512 | tf_op jit(solution)/shard_map/ppermute | solution.py:542
  39.2 4.1 %collective-permute-done.4 = bf16[2,24,1408]{2,1,0:T(8,128)(2,1)S(1)} collective-permute-done((bf16[2,24,1408]{2,1,0:T(8,128)(2,1)S(1)}, bf16[2,24,1408]{2,1,0:T(8,128)(2,1)S(1)}, u32[]{:S(2)}, u32[]{:S(2)}) %collective-permute-start.4) | collective-permute-done | bytes 135200 | tf_op jit(solution)/shard_map/ppermute | solution.py:542
  43.3 1.5 %collective-permute-done.5 = bf16[2,24,1408]{2,1,0:T(8,128)(2,1)S(1)} collective-permute-done((bf16[2,24,1408]{2,1,0:T(8,128)(2,1)S(1)}, bf16[2,24,1408]{2,1,0:T(8,128)(2,1)S(1)}, u32[]{:S(2)}, u32[]{:S(2)}) %collective-permute-start.5) | collective-permute-done | bytes 135200 | tf_op jit(solution)/shard_map/ppermute | solution.py:542
  44.9 3.4 %collective-permute-start.6 = (bf16[4,24,1408]{2,1,0:T(8,128)(2,1)S(1)}, bf16[4,24,1408]{2,1,0:T(8,128)(2,1)S(1)}, u32[]{:S(2)}, u32[]{:S(2)}) collective-permute-start(bf16[4,24,1408]{2,1,0:T(8,128)(2,1)S(1)} %pad_maximum_fusion), channel_id=1, source_target_pairs={{0,2},{2,0},{4,6},{6,4},{8,10},{10,8},{12,14},{14,12},{1,3},{3,1},... | collective-permute-start | bytes 811016 | tf_op jit(solution)/shard_map/ppermute | solution.py:542
  49.6 2.7 %collective-permute-start.7 = (bf16[8,24,1152]{2,1,0:T(8,128)(2,1)S(1)}, bf16[8,24,1152]{2,1,0:T(8,128)(2,1)S(1)}, u32[]{:S(2)}, u32[]{:S(2)}) collective-permute-start(bf16[8,24,1152]{2,1,0:T(8,128)(2,1)S(1)} %slice.86), channel_id=1, source_target_pairs={{0,1},{1,0},{2,3},{3,2},{4,5},{5,4},{6,7},{7,6},{8,9},{9,8},{10,11... | collective-permute-start | bytes 1327112 | tf_op jit(solution)/shard_map/ppermute | solution.py:538
  52.3 2.8 %copy-done = bf16[1,192,128,128]{3,2,1,0:T(8,128)(2,1)S(1)} copy-done((bf16[1,192,128,128]{3,2,1,0:T(8,128)(2,1)S(1)}, bf16[1,192,128,128]{3,2,1,0:T(8,128)(2,1)}, u32[]{:S(2)}) %copy-start) | copy-done | bytes 6291480
  55.1 2.8 %copy-done.1 = bf16[1,192,128,128]{3,2,1,0:T(8,128)(2,1)S(1)} copy-done((bf16[1,192,128,128]{3,2,1,0:T(8,128)(2,1)S(1)}, bf16[1,192,128,128]{3,2,1,0:T(8,128)(2,1)}, u32[]{:S(2)}) %copy-start.1) | copy-done | bytes 6291480
  57.9 3.2 %shard_map.161 = (f32[4,24,1024]{2,1,0:T(8,128)S(1)}, f32[4,24,128]{2,1,0:T(8,128)S(1)}) custom-call(s32[4]{0:T(128)S(1)} %add_xor_fusion.where_ref, s32[1]{0:T(128)} %bitcast.1.span_ref.parity_ref, bf16[8,24,1408]{2,1,0:T(8,128)(2,1)S(1)} %slice_dynamic-update-slice_fusion.rows_ref, bf16[8,24,128,128]{3,2,1,0:T(8,128)(2,1)S(1)} %bitcast.15, ...), custom_call_target="tpu_custom_call" | custom-call | flops 2000000000 | bytes 8388608 | tf_op jit(solution)/shard_map/pallas_call | solution.py:290
  61.1 1.6 %collective-permute-done.7.rows_ref = bf16[8,24,1152]{2,1,0:T(8,128)(2,1)S(1)} collective-permute-done((bf16[8,24,1152]{2,1,0:T(8,128)(2,1)S(1)}, bf16[8,24,1152]{2,1,0:T(8,128)(2,1)S(1)}, u32[]{:S(2)}, u32[]{:S(2)}) %collective-permute-start.7) | collective-permute-done | bytes 442400 | tf_op jit(solution)/shard_map/ppermute | solution.py:538
  62.7 2.8 %copy-done.2 = bf16[1,192,128,128]{3,2,1,0:T(8,128)(2,1)S(1)} copy-done((bf16[1,192,128,128]{3,2,1,0:T(8,128)(2,1)S(1)}, bf16[1,192,128,128]{3,2,1,0:T(8,128)(2,1)}, u32[]{:S(2)}) %copy-start.2) | copy-done | bytes 6291480
  65.5 11.3 %shard_map.162 = bf16[8,24,1408]{2,1,0:T(8,128)(2,1)S(1)} custom-call(s32[4]{0:T(128)S(1)} %add_xor_fusion.where_ref, bf16[8,24,1152]{2,1,0:T(8,128)(2,1)S(1)} %collective-permute-done.7.rows_ref, bf16[4096,128]{1,0:T(8,128)(2,1)S(1)} %bitcast.21, bf16[4096,128]{1,0:T(8,128)(2,1)S(1)} %bitcast.23, s32[1]{0:T(128)S(6)} %sub.3.refs_0_, ...), custom_call_target="tpu_custom_call" | custom-call | flops 3221225472 | bytes 4194304 | tf_op jit(solution)/shard_map/pallas_call | solution.py:436
  76.8 2.8 %collective-permute-start.8 = (bf16[8,24,1408]{2,1,0:T(8,128)(2,1)S(1)}, bf16[8,24,1408]{2,1,0:T(8,128)(2,1)S(1)}, u32[]{:S(2)}, u32[]{:S(2)}) collective-permute-start(bf16[8,24,1408]{2,1,0:T(8,128)(2,1)S(1)} %shard_map.162), channel_id=1, source_target_pairs={{0,1},{1,0},{2,3},{3,2},{4,5},{5,4},{6,7},{7,6},{8,9},{9,8},{10,11... | collective-permute-start | bytes 1622024 | tf_op jit(solution)/shard_map/ppermute | solution.py:538
  79.6 10.2 %shard_map.163 = (f32[8,24,1024]{2,1,0:T(8,128)S(1)}, f32[8,24,128]{2,1,0:T(8,128)S(1)}) custom-call(s32[4]{0:T(128)S(1)} %add_xor_fusion.where_ref, bf16[8,24,1408]{2,1,0:T(8,128)(2,1)S(1)} %slice_dynamic-update-slice_fusion.rows_ref, bf16[4096,128]{1,0:T(8,128)(2,1)S(1)} %bitcast.22, bf16[4096,128]{1,0:T(8,128)(2,1)S(1)} %bitcast.24, ...), custom_call_target="tpu_custom_call" | custom-call | flops 3221225472 | bytes 4194304 | tf_op jit(solution)/shard_map/pallas_call | solution.py:436
  89.8 1.4 %collective-permute-done.8.came_ref = bf16[8,24,1408]{2,1,0:T(8,128)(2,1)S(1)} collective-permute-done((bf16[8,24,1408]{2,1,0:T(8,128)(2,1)S(1)}, bf16[8,24,1408]{2,1,0:T(8,128)(2,1)S(1)}, u32[]{:S(2)}, u32[]{:S(2)}) %collective-permute-start.8) | collective-permute-done | bytes 540704 | tf_op jit(solution)/shard_map/ppermute | solution.py:538
  92.7 2.0 %collective-permute-start.10 = (bf16[2,24,1024]{2,1,0:T(8,128)(2,1)S(1)}, bf16[2,24,1024]{2,1,0:T(8,128)(2,1)S(1)}, u32[]{:S(2)}, u32[]{:S(2)}) collective-permute-start(bf16[2,24,1024]{2,1,0:T(8,128)(2,1)S(1)} %get-tuple-element.42), channel_id=1, source_target_pairs={{0,8},{2,10},{4,12},{6,14},{8,0},{10,2},{12,4},{14,6},{1,9},{3,11}... | collective-permute-start | bytes 294920 | tf_op jit(solution)/shard_map/ppermute | solution.py:542
  94.7 1.8 %collective-permute-start.11 = (bf16[2,24,1024]{2,1,0:T(8,128)(2,1)S(1)}, bf16[2,24,1024]{2,1,0:T(8,128)(2,1)S(1)}, u32[]{:S(2)}, u32[]{:S(2)}) collective-permute-start(bf16[2,24,1024]{2,1,0:T(8,128)(2,1)S(1)} %get-tuple-element.43), channel_id=1, source_target_pairs={{0,12},{2,14},{4,8},{6,10},{8,4},{10,6},{12,0},{14,2},{1,13},{3,15... | collective-permute-start | bytes 294920 | tf_op jit(solution)/shard_map/ppermute | solution.py:542
  97.8 1.9 %collective-permute-done.11.near3_ref = bf16[2,24,1024]{2,1,0:T(8,128)(2,1)S(1)} collective-permute-done((bf16[2,24,1024]{2,1,0:T(8,128)(2,1)S(1)}, bf16[2,24,1024]{2,1,0:T(8,128)(2,1)S(1)}, u32[]{:S(2)}, u32[]{:S(2)}) %collective-permute-start.11) | collective-permute-done | bytes 98336 | tf_op jit(solution)/shard_map/ppermute | solution.py:542
  99.7 3.6 %collective-permute-start.12 = (bf16[4,24,1024]{2,1,0:T(8,128)(2,1)S(1)}, bf16[4,24,1024]{2,1,0:T(8,128)(2,1)S(1)}, u32[]{:S(2)}, u32[]{:S(2)}) collective-permute-start(bf16[4,24,1024]{2,1,0:T(8,128)(2,1)S(1)} %pad_maximum_fusion.1), channel_id=1, source_target_pairs={{0,2},{2,0},{4,6},{6,4},{8,10},{10,8},{12,14},{14,12},{1,3},{3,1},... | collective-permute-start | bytes 589832 | tf_op jit(solution)/shard_map/ppermute | solution.py:542
  (70 shorter events, 12.7 us)
Async XLA Ops:
  2.7 5.9 %copy-start.9 = (f32[256]{0:T(256)}, f32[256]{0:T(256)S(1)}, u32[]{:S(2)}) copy-start(f32[256]{0:T(256)S(1)} %multiply_reduce_fusion) | copy-start | bytes 3076
  2.7 5.9 %collective-permute-start = (f32[256]{0:T(256)S(1)}, f32[256]{0:T(256)S(1)}, u32[]{:S(2)}, u32[]{:S(2)}) collective-permute-start(f32[256]{0:T(256)S(1)} %multiply_reduce_fusion), channel_id=1, source_target_pairs={{0,1},{1,0},{2,3},{3,2},{4,5},{5,4},{6,7},{7,6},{8,9},{9,8},{10,11... | collective-permute-start | bytes 3080 | tf_op jit(solution)/shard_map/ppermute | solution.py:538
  15.9 8.0 %copy-start.11 = (bf16[128]{0:T(256)(128)(2,1)S(1)}, bf16[128]{0:T(256)(128)(2,1)}, u32[]{:S(2)}) copy-start(bf16[128]{0:T(256)(128)(2,1)} %param.22) | copy-start | bytes 772
  15.9 8.0 %copy-start.12 = (bf16[128]{0:T(256)(128)(2,1)S(1)}, bf16[128]{0:T(256)(128)(2,1)}, u32[]{:S(2)}) copy-start(bf16[128]{0:T(256)(128)(2,1)} %param.21) | copy-start | bytes 772
  15.9 16.9 %copy-start.6 = (s32[8]{0:T(128)S(1)}, s32[8]{0:T(128)}, u32[]{:S(2)}) copy-start(s32[8]{0:T(128)} %home_ref.1) | copy-start | bytes 100
  15.9 16.9 %copy-start.7 = (s32[128]{0:T(128)S(1)}, s32[128]{0:T(128)}, u32[]{:S(2)}) copy-start(s32[128]{0:T(128)} %param.27) | copy-start | bytes 1540
  15.9 16.9 %copy-start.8 = (s32[128]{0:T(128)S(1)}, s32[128]{0:T(128)}, u32[]{:S(2)}) copy-start(s32[128]{0:T(128)} %param.28) | copy-start | bytes 1540
  15.9 16.9 %collective-permute-start.1 = (f32[128,1024]{1,0:T(8,128)}, f32[128,1024]{1,0:T(8,128)S(1)}, u32[]{:S(2)}, u32[]{:S(2)}) collective-permute-start(f32[128,1024]{1,0:T(8,128)} %get-tuple-element.25), channel_id=1, source_target_pairs={{0,1},{1,0},{2,3},{3,2},{4,5},{5,4},{6,7},{7,6},{8,9},{9,8},{10,11... | collective-permute-start | bytes 1572872 | tf_op jit(solution)/shard_map/ppermute | solution.py:538
  23.5 9.4 %collective-permute-start.2 = (f32[128,256]{1,0:T(8,128)}, f32[128,256]{1,0:T(8,128)S(1)}, u32[]{:S(2)}, u32[]{:S(2)}) collective-permute-start(f32[128,256]{1,0:T(8,128)} %get-tuple-element.26), channel_id=1, source_target_pairs={{0,1},{1,0},{2,3},{3,2},{4,5},{5,4},{6,7},{7,6},{8,9},{9,8},{10,11... | collective-permute-start | bytes 393224 | tf_op jit(solution)/shard_map/ppermute | solution.py:538
  33.9 28.8 %slice-start = ((s8[6291456]{0:T(1024)(128)(4,1)}), s8[2097152]{0:T(1024)(128)(4,1)S(1)}, s32[]{:S(2)}) async-start(s8[6291456]{0:T(1024)(128)(4,1)} %bitcast.16), calls=%async_computation | async-start | bytes 4194304
  35.2 4.0 %collective-permute-start.3 = (bf16[2,24,1408]{2,1,0:T(8,128)(2,1)S(1)}, bf16[2,24,1408]{2,1,0:T(8,128)(2,1)S(1)}, u32[]{:S(2)}, u32[]{:S(2)}) collective-permute-start(bf16[2,24,1408]{2,1,0:T(8,128)(2,1)S(1)} %get-tuple-element.29), channel_id=1, source_target_pairs={{0,4},{2,6},{4,0},{6,2},{8,12},{10,14},{12,8},{14,10},{1,5},{3,7},... | collective-permute-start | bytes 405512 | tf_op jit(solution)/shard_map/ppermute | solution.py:542
  36.5 6.8 %collective-permute-start.4 = (bf16[2,24,1408]{2,1,0:T(8,128)(2,1)S(1)}, bf16[2,24,1408]{2,1,0:T(8,128)(2,1)S(1)}, u32[]{:S(2)}, u32[]{:S(2)}) collective-permute-start(bf16[2,24,1408]{2,1,0:T(8,128)(2,1)S(1)} %get-tuple-element.30), channel_id=1, source_target_pairs={{0,8},{2,10},{4,12},{6,14},{8,0},{10,2},{12,4},{14,6},{1,9},{3,11}... | collective-permute-start | bytes 405512 | tf_op jit(solution)/shard_map/ppermute | solution.py:542
  39.2 5.6 %collective-permute-start.5 = (bf16[2,24,1408]{2,1,0:T(8,128)(2,1)S(1)}, bf16[2,24,1408]{2,1,0:T(8,128)(2,1)S(1)}, u32[]{:S(2)}, u32[]{:S(2)}) collective-permute-start(bf16[2,24,1408]{2,1,0:T(8,128)(2,1)S(1)} %get-tuple-element.31), channel_id=1, source_target_pairs={{0,12},{2,14},{4,8},{6,10},{8,4},{10,6},{12,0},{14,2},{1,13},{3,15... | collective-permute-start | bytes 405512 | tf_op jit(solution)/shard_map/ppermute | solution.py:542
  44.9 4.5 %collective-permute-start.6 = (bf16[4,24,1408]{2,1,0:T(8,128)(2,1)S(1)}, bf16[4,24,1408]{2,1,0:T(8,128)(2,1)S(1)}, u32[]{:S(2)}, u32[]{:S(2)}) collective-permute-start(bf16[4,24,1408]{2,1,0:T(8,128)(2,1)S(1)} %pad_maximum_fusion), channel_id=1, source_target_pairs={{0,2},{2,0},{4,6},{6,4},{8,10},{10,8},{12,14},{14,12},{1,3},{3,1},... | collective-permute-start | bytes 811016 | tf_op jit(solution)/shard_map/ppermute | solution.py:542
  49.6 13.1 %collective-permute-start.7 = (bf16[8,24,1152]{2,1,0:T(8,128)(2,1)S(1)}, bf16[8,24,1152]{2,1,0:T(8,128)(2,1)S(1)}, u32[]{:S(2)}, u32[]{:S(2)}) collective-permute-start(bf16[8,24,1152]{2,1,0:T(8,128)(2,1)S(1)} %slice.86), channel_id=1, source_target_pairs={{0,1},{1,0},{2,3},{3,2},{4,5},{5,4},{6,7},{7,6},{8,9},{9,8},{10,11... | collective-permute-start | bytes 1327112 | tf_op jit(solution)/shard_map/ppermute | solution.py:538
  52.3 2.8 %copy-start = (bf16[1,192,128,128]{3,2,1,0:T(8,128)(2,1)S(1)}, bf16[1,192,128,128]{3,2,1,0:T(8,128)(2,1)}, u32[]{:S(2)}) copy-start(bf16[1,192,128,128]{3,2,1,0:T(8,128)(2,1)} %param.25) | copy-start | bytes 18874372
  57.9 4.8 %slice-start.1 = ((s8[6291456]{0:T(1024)(128)(4,1)}), s8[4194304]{0:T(1024)(128)(4,1)S(1)}, s32[]{:S(2)}) async-start(s8[6291456]{0:T(1024)(128)(4,1)} %bitcast.16), calls=%async_computation.1 | async-start | bytes 8388608
  57.9 4.8 %copy-start.3 = (bf16[1,4096,128]{2,1,0:T(8,128)(2,1)S(1)}, bf16[1,4096,128]{2,1,0:T(8,128)(2,1)}, u32[]{:S(2)}) copy-start(bf16[1,4096,128]{2,1,0:T(8,128)(2,1)} %param.23) | copy-start | bytes 3145732
  57.9 4.8 %copy-start.4 = (bf16[1,4096,128]{2,1,0:T(8,128)(2,1)S(1)}, bf16[1,4096,128]{2,1,0:T(8,128)(2,1)}, u32[]{:S(2)}) copy-start(bf16[1,4096,128]{2,1,0:T(8,128)(2,1)} %param.24) | copy-start | bytes 3145732
  76.8 14.4 %collective-permute-start.8 = (bf16[8,24,1408]{2,1,0:T(8,128)(2,1)S(1)}, bf16[8,24,1408]{2,1,0:T(8,128)(2,1)S(1)}, u32[]{:S(2)}, u32[]{:S(2)}) collective-permute-start(bf16[8,24,1408]{2,1,0:T(8,128)(2,1)S(1)} %shard_map.162), channel_id=1, source_target_pairs={{0,1},{1,0},{2,3},{3,2},{4,5},{5,4},{6,7},{7,6},{8,9},{9,8},{10,11... | collective-permute-start | bytes 1622024 | tf_op jit(solution)/shard_map/ppermute | solution.py:538
  92.6 3.9 %collective-permute-start.9 = (bf16[2,24,1024]{2,1,0:T(8,128)(2,1)S(1)}, bf16[2,24,1024]{2,1,0:T(8,128)(2,1)S(1)}, u32[]{:S(2)}, u32[]{:S(2)}) collective-permute-start(bf16[2,24,1024]{2,1,0:T(8,128)(2,1)S(1)} %get-tuple-element.41), channel_id=1, source_target_pairs={{0,4},{2,6},{4,0},{6,2},{8,12},{10,14},{12,8},{14,10},{1,5},{3,7},... | collective-permute-start | bytes 294920 | tf_op jit(solution)/shard_map/ppermute | solution.py:542
  92.7 5.1 %collective-permute-start.10 = (bf16[2,24,1024]{2,1,0:T(8,128)(2,1)S(1)}, bf16[2,24,1024]{2,1,0:T(8,128)(2,1)S(1)}, u32[]{:S(2)}, u32[]{:S(2)}) collective-permute-start(bf16[2,24,1024]{2,1,0:T(8,128)(2,1)S(1)} %get-tuple-element.42), channel_id=1, source_target_pairs={{0,8},{2,10},{4,12},{6,14},{8,0},{10,2},{12,4},{14,6},{1,9},{3,11}... | collective-permute-start | bytes 294920 | tf_op jit(solution)/shard_map/ppermute | solution.py:542
  94.7 5.0 %collective-permute-start.11 = (bf16[2,24,1024]{2,1,0:T(8,128)(2,1)S(1)}, bf16[2,24,1024]{2,1,0:T(8,128)(2,1)S(1)}, u32[]{:S(2)}, u32[]{:S(2)}) collective-permute-start(bf16[2,24,1024]{2,1,0:T(8,128)(2,1)S(1)} %get-tuple-element.43), channel_id=1, source_target_pairs={{0,12},{2,14},{4,8},{6,10},{8,4},{10,6},{12,0},{14,2},{1,13},{3,15... | collective-permute-start | bytes 294920 | tf_op jit(solution)/shard_map/ppermute | solution.py:542
  99.7 4.7 %collective-permute-start.12 = (bf16[4,24,1024]{2,1,0:T(8,128)(2,1)S(1)}, bf16[4,24,1024]{2,1,0:T(8,128)(2,1)S(1)}, u32[]{:S(2)}, u32[]{:S(2)}) collective-permute-start(bf16[4,24,1024]{2,1,0:T(8,128)(2,1)S(1)} %pad_maximum_fusion.1), channel_id=1, source_target_pairs={{0,2},{2,0},{4,6},{6,4},{8,10},{10,8},{12,14},{14,12},{1,3},{3,1},... | collective-permute-start | bytes 589832 | tf_op jit(solution)/shard_map/ppermute | solution.py:542
  (4 other events, 7.3 us)
